TPU v7x, 128 devices: a whole 4x4x4 slice. The times are simulated.
128 devices in a mesh: gx: 4 (over x_hi, core), gy: 8 (over y, x_lo), gz: 4 (over z).
Axes of the slice: x: 4 (x_hi: 2, x_lo: 2; x = x_hi * 2 + x_lo), y: 4, z: 4, core: 2. Of those that a mesh axis runs over, the one named last changes fastest.
Arguments:
- partial_sums: float32 [128, 256, 4096], P(('gx', 'gy', 'gz')), may hold values from -448 to 448
- correction_pieces: float32 [128, 256, 4096], P(('gx', 'gy', 'gz')), may hold values from -60 to 60
- counts: float32 [128, 256, 4096], P(('gx', 'gy', 'gz')), may hold values from 0 to 3, as said below
Outputs:
- pixel_mean_grid: float32 [256, 4096], P('gz')
- preview: float32 [64, 1024], replicated
Inputs may be any that keep to these rules, and one draw needn't show every extreme that they name: `counts`: weights are real-valued and nonnegative.
All inputs are finite; a program needn't handle non-finite values.
Results may differ from a plain program's by a relative error of at most 0.00002.
Values sent between devices are 32-bit elements; how exact they have to be, the bound alone decides.
No kernel may reach another device: no remote copies, remote signals or barrier semaphores. Data moves between devices by JAX's collectives and lax.ppermute only.
A program may use at most 128 MiB of HBM per device.

v0:
```python
import jax.numpy as jnp

WIDTH = 4096
ROWS = 256


def reference(partial_sums, correction_pieces, counts):
    total = jnp.sum(partial_sums, axis=0) + jnp.sum(correction_pieces, axis=0)
    total_count = jnp.sum(counts, axis=0)
    pixel_mean_grid = total / (total_count + 1.0)
    blocks = pixel_mean_grid.reshape(ROWS // 4, 4, WIDTH // 4, 4)
    preview = jnp.mean(blocks, axis=(1, 3))
    return (pixel_mean_grid, preview)


def solution(mesh):
    return reference
```

profile of v0, /device:TPU:1, one launch (start us, length us, event | category | flops | bytes accessed | tf_op | source)
XLA Modules:
  0.0 246.3 jit_solution(1971329917897051001)
XLA Ops:
  7.2 0.0 all-reduce.7.cloned.1.call-start
  7.2 6.1 %add_bitcast_fusion = f32[256,4096]{1,0:T(8,128)} fusion(f32[1,256,4096]{2,1,0:T(8,128)} %param, f32[1,256,4096]{2,1,0:T(8,128)} %param.1), kind=kLoop, calls=%fused_computation | loop fusion | flops 1048576 | bytes 12582912 | tf_op jit(solution)/add | solution.py:8
  13.3 0.0 copy-start.1
  13.3 0.0 all-reduce.7.cloned.1.call-update
  13.3 0.6 copy-done.1
  13.9 0.6 dynamic-slice
  15.2 163.3 %all-reduce.7.cloned.1.call-done = (f32[256,4096]{1,0:T(8,128)}, f32[256,4096]{1,0:T(8,128)}) async-done(((f32[256,4096]{1,0:T(8,128)}, f32[256,4096]{1,0:T(8,128)}), (f32[256,4096]{1,0:T(8,128)}, f32[256,4096]{1,0:T(8,128)})) %all-reduce.7.cloned.1.call-update) | async-done | bytes 8388624 | tf_op jit(solution)/reduce_sum | solution.py:8
  178.5 1.7 dynamic-slice_divide_fusion
  180.2 0.0 copy-start
  180.2 36.7 %div.15 = f32[16,4,1024,4]{3,2,1,0:T(8,128)} reshape(f32[64,4096]{1,0:T(8,128)S(1)} %dynamic-slice_divide_fusion) | data formatting | bytes 2097152 | tf_op jit(solution)/div | solution.py:10
  216.9 0.0 copy-done
  216.9 12.2 %reduce.3 = f32[16,1024]{1,0:T(8,128)S(1)} reduce(f32[16,4,1024,4]{3,2,1,0:T(8,128)} %div.15, f32[]{:T(128)} %constant.7.clone), dimensions={1,3}, to_apply=%region_3.0 | reduce | flops 245760 | bytes 1114116 | tf_op jit(solution)/reduce_sum | solution.py:12
  229.1 9.7 %all-gather = f32[64,1024]{1,0:T(8,128)S(1)} all-gather(f32[16,1024]{1,0:T(8,128)S(1)} %broadcast_multiply_fusion), channel_id=4, replica_groups=mesh['gx'=4,'gy'=8,'gz'=4] {'gz'}, dimensions={0}, use_global_device_ids=true | all-gather | bytes 327680 | tf_op jit(solution)/div | solution.py:12
  238.8 0.7 copy.4
  (1 shorter events, 0.0 us)
Async XLA Ops:
  7.2 171.3 %all-reduce.7.cloned.1.call-start = ((), (), s32[]{:S(2)}) async-start(), calls=%async_computation | async-start | bytes 16777216 | tf_op jit(solution)/reduce_sum | solution.py:8
  13.3 0.7 copy-start.1
  180.2 36.7 %copy-start = (f32[64,4096]{1,0:T(8,128)}, f32[64,4096]{1,0:T(8,128)S(1)}, u32[]{:S(2)}) copy-start(f32[64,4096]{1,0:T(8,128)S(1)} %dynamic-slice_divide_fusion) | copy-start | bytes 3145732
Sparse Core Ops, SparseCore 0:
  13.4 165.0 all-reduce.6
where the time goes:
time: 249 us; the launch traced here: 246 us
  waiting for transfers between devices  163 us (65%)
  local copies, waits for them, and re-layouts  38.6 us (16%)
  other arithmetic  20 us (8%)
  between operations  14.7 us (6%)
  blocking collectives  9.67 us (4%)
    reduce_sum x1, waiting for transfers between devices, reference(): total = jnp.sum(partial_sums, axis=0) + jnp.sum(correction_pieces, axis=0)  163 us
    div x1, local copies, waits for them, and re-layouts, reference(): pixel_mean_grid = total / (total_count + 1.0)  36.7 us
    reduce_sum x1, other arithmetic, reference(): preview = jnp.mean(blocks, axis=(1, 3))  12.2 us
    div x1, blocking collectives, reference(): preview = jnp.mean(blocks, axis=(1, 3))  9.67 us
    add x1, other arithmetic, reference(): total = jnp.sum(partial_sums, axis=0) + jnp.sum(correction_pieces, axis=0)  6.08 us
  transfers between devices with their start and end apart: 1, of which 1 were waited for; matrix products, arithmetic and copies ran while one was open for 0% of the time, Pallas kernels for 0%

commit v1 on v0

v1 whole, which is shorter than its diff:
```python
import functools

import jax
import jax.numpy as jnp
import numpy as np
from jax import lax
from jax.experimental import pallas as pl
from jax.experimental.pallas import tpu as pltpu
from jax.sharding import PartitionSpec as P

AXES = ("gx", "gy", "gz")
F32 = jnp.float32
VMEM_LIMIT = 48 * 1024 * 1024


def _coords(d):
    gx, gy, gz = d // 32, (d // 4) % 8, d % 4
    return (gx // 2) * 2 + gy % 2, gy // 2, gz, gx % 2


def _device(x, y, z, core):
    return ((x // 2) * 2 + core) * 32 + (y * 2 + x % 2) * 4 + z


def _shift(axis0, axis1, k):
    pairs = []
    for d in range(128):
        at = list(_coords(d))
        axis = (axis0, axis1)[at[3]]
        at[axis] = (at[axis] + k) % 4
        pairs.append((d, _device(*at)))
    return pairs


_SIBLING = [(d, d ^ 32) for d in range(128)]
X, Y, Z = 0, 1, 2


def _send(array, pairs):
    return lax.ppermute(array, AXES, pairs)


def _exchange(arrays, axis0, axis1):
    got = {k: _send(arrays[k], _shift(axis0, axis1, k)) for k in (2, 1, 3)}
    return [arrays[0], got[1], got[2], got[3]]


def _position():
    gx, gy, gz = (lax.axis_index(a) for a in AXES)
    core = gx % 2
    x, y = (gx // 2) * 2 + gy % 2, gy // 2
    first, second = jnp.where(core == 0, gz, y), jnp.where(core == 0, y, gz)
    return jnp.stack([core, first, second, x]).astype(jnp.int32)


def _tile(core, a, b):
    return jnp.where(core == 0, a * 8 + b, b * 8 + 4 + a)


def _split_kernel(pos, p, c, n, out):
    out[0, 0] = p[0] + c[0]
    out[1, 0] = n[0]


def _split(pos, p, c, n, k, own):
    def rows(b, pos):
        me = pos[0]
        core = me if own else 1 - me
        y, z = jnp.where(me == 0, pos[2], pos[1]), jnp.where(me == 0, pos[1], pos[2])
        a = (jnp.where(core == 0, z, y) + k) % 4
        return (0, _tile(core, a, b), 0)

    return rows


def _shape(*dims):
    return jax.ShapeDtypeStruct(dims, F32)


def _params():
    return pltpu.CompilerParams(vmem_limit_bytes=VMEM_LIMIT)


def _for_sibling(pos, p, c, n, k):
    rows = pl.BlockSpec((1, 8, 4096), _split(pos, p, c, n, k, False))
    return pl.pallas_call(
        _split_kernel,
        grid_spec=pltpu.PrefetchScalarGridSpec(
            num_scalar_prefetch=1,
            grid=(4,),
            in_specs=[rows, rows, rows],
            out_specs=pl.BlockSpec((2, 1, 8, 4096), lambda b, pos: (0, b, 0, 0)),
        ),
        out_shape=_shape(2, 4, 8, 4096),
        compiler_params=_params(),
        name="for_sibling",
    )(pos, p, c, n)


def _pair_kernel(pos, p, c, n, got, out):
    out[0, 0] = (p[0] + c[0]) + got[0, 0]
    out[1, 0] = n[0] + got[1, 0]


def _pair(pos, p, c, n, got, k):
    rows = pl.BlockSpec((1, 8, 4096), _split(pos, p, c, n, k, True))
    both = pl.BlockSpec((2, 1, 8, 4096), lambda b, pos: (0, b, 0, 0))
    return pl.pallas_call(
        _pair_kernel,
        grid_spec=pltpu.PrefetchScalarGridSpec(
            num_scalar_prefetch=1,
            grid=(4,),
            in_specs=[rows, rows, rows, both],
            out_specs=both,
        ),
        out_shape=_shape(2, 4, 8, 4096),
        compiler_params=_params(),
        name="pair_sum",
    )(pos, p, c, n, got)


def _second_kernel(pos, a, b, c, d, *outs):
    for k in range(4):
        i = (pos[2] + k) % 4
        outs[k][0] = (a[0, i] + b[0, i]) + (c[0, i] + d[0, i])


def _second(pos, parts):
    whole = pl.BlockSpec((1, 4, 8, 4096), lambda i, pos: (i, 0, 0, 0))
    one = pl.BlockSpec((1, 8, 4096), lambda i, pos: (i, 0, 0))
    return pl.pallas_call(
        _second_kernel,
        grid_spec=pltpu.PrefetchScalarGridSpec(
            num_scalar_prefetch=1, grid=(2,), in_specs=[whole] * 4, out_specs=[one] * 4
        ),
        out_shape=[_shape(2, 8, 4096)] * 4,
        compiler_params=_params(),
        name="first_axis_sum",
    )(pos, *parts)


def _third_kernel(pos, a, b, c, d, *outs):
    for k in range(4):
        at = pl.ds(pl.multiple_of(((pos[3] + k) % 4) * 1024, 1024), 1024)
        outs[k][...] = (a[:, :, at] + b[:, :, at]) + (c[:, :, at] + d[:, :, at])


def _third(pos, parts):
    return pl.pallas_call(
        _third_kernel,
        grid_spec=pltpu.PrefetchScalarGridSpec(num_scalar_prefetch=1, grid=(1,),
            in_specs=[pl.BlockSpec((2, 8, 4096), lambda i, pos: (0, 0, 0))] * 4,
            out_specs=[pl.BlockSpec((2, 8, 1024), lambda i, pos: (0, 0, 0))] * 4),
        out_shape=[_shape(2, 8, 1024)] * 4,
        compiler_params=_params(),
        name="second_axis_sum",
    )(pos, *parts)


def _mean_kernel(a, b, c, d, mean, preview):
    both = (a[...] + b[...]) + (c[...] + d[...])
    grid = both[0] / (both[1] + 1.0)
    mean[...] = grid
    four = jnp.concatenate(
        [jnp.sum(grid[0:4], axis=0, keepdims=True), jnp.sum(grid[4:8], axis=0, keepdims=True)], axis=0
    )
    for j in range(2):
        row = lax.broadcasted_iota(jnp.int32, (512, 128), 0)
        column = lax.broadcasted_iota(jnp.int32, (512, 128), 1)
        pool = jnp.where(row // 4 == column, 0.0625, 0.0).astype(F32)
        preview[:, j * 128 : (j + 1) * 128] = jnp.dot(
            four[:, j * 512 : (j + 1) * 512], pool, precision=lax.Precision.HIGHEST, preferred_element_type=F32
        )


def _mean(parts):
    return pl.pallas_call(
        _mean_kernel,
        out_shape=[_shape(8, 1024), _shape(2, 256)],
        compiler_params=_params(),
        name="mean_and_preview",
    )(*parts)


def _pack_kernel(mean, a, b, c, d, out):
    out[:, :1024] = mean[...]
    for k, part in enumerate((a, b, c, d)):
        out[2 * k : 2 * k + 2, 1024:] = part[...]


def _pack(mean, previews):
    return pl.pallas_call(_pack_kernel, out_shape=_shape(8, 1280), compiler_params=_params(), name="pack")(mean, *previews)


def _row_kernel(a, b, c, d, out):
    for k, part in enumerate((a, b, c, d)):
        out[k] = part[...]


def _row(parts):
    return pl.pallas_call(_row_kernel, out_shape=_shape(4, 8, 1280), compiler_params=_params(), name="gathered_row")(*parts)


def _final_kernel(pos, *refs):
    own, other, grid, preview, lines = refs[:4], refs[4:8], refs[8], refs[9], refs[10]
    core, x = pos[0], pos[3]
    y = jnp.where(core == 0, pos[2], pos[1])
    z = jnp.where(core == 0, pos[1], pos[2])
    for mine, parts in ((True, own), (False, other)):
        c = core if mine else 1 - core
        for k2 in range(4):
            for k1 in range(4):
                fy = (y - jnp.where(c == 0, k1, k2)) % 4
                fx = (x - jnp.where(c == 0, k2, k1)) % 4
                rows = pl.multiple_of((c * 4 + fy) * 8, 8)
                columns = pl.multiple_of(fx * 1024, 1024)
                grid[pl.ds(rows, 8), pl.ds(columns, 1024)] = parts[k2][k1, :, :1024]
                for k in range(4):
                    at = pl.ds(pl.multiple_of(fx * 256, 256), 256)
                    lines[(((z - k) % 4) * 2 + c) * 4 + fy, :, at] = parts[k2][k1, 2 * k : 2 * k + 2, 1024:]
    for i in range(8):
        preview[8 * i : 8 * i + 8, :] = jnp.concatenate([lines[4 * i + j] for j in range(4)], axis=0)


def _final(pos, own, other):
    return pl.pallas_call(
        _final_kernel,
        in_specs=[pl.BlockSpec(memory_space=pltpu.SMEM)] + [pl.BlockSpec()] * 8,
        out_shape=[_shape(64, 4096), _shape(64, 1024)],
        scratch_shapes=[pltpu.VMEM((32, 2, 1024), F32)],
        compiler_params=_params(),
        name="assemble",
    )(pos, *own, *other)


def _local(p, c, n):
    pos = _position()
    blocks = [None] * 4
    for k in (2, 1, 3, 0):
        got = _send(_for_sibling(pos, p, c, n, k), _SIBLING)
        blocks[k] = _pair(pos, p, c, n, got, k)
    parts = _exchange(blocks, Z, Y)
    parts = _exchange(_second(pos, parts), Y, Z)
    parts = _exchange(_third(pos, parts), X, X)
    mean, preview = _mean(parts)
    packed = _pack(mean, _exchange([preview] * 4, Z, Z))
    row = _row(_exchange([packed] * 4, Y, X))
    own = _exchange([row] * 4, X, Y)
    other = [_send(part, _SIBLING) for part in own]
    return _final(pos, own, other)


def solution(mesh):
    return jax.shard_map(
        _local,
        mesh=mesh,
        in_specs=(P(AXES, None, None),) * 3,
        out_specs=(P("gz", None), P(None, None)),
        check_vma=False,
    )
```

time: 249 us -> 107 us (0.43)
  waiting for transfers between devices: 163 us -> 34.5 us
  starting transfers between devices: 0.04 us -> 42.2 us
  local copies, waits for them, and re-layouts: 38.6 us -> 2.19 us
  Pallas kernels: 0 us -> 27.1 us
  other arithmetic: 20 us -> 0.08 us
  between operations: 14.7 us -> 0.8 us
  blocking collectives: 9.67 us -> 0 us
    reduce_sum x1 -> x0, waiting for transfers between devices: 163 us -> none  [reference(): total = jnp.sum(partial_sums, axis=0) + jnp.sum(correction_pieces, axis=0)]
    ppermute x0 -> x26, starting transfers between devices: none -> 42.2 us  [_send(): return lax.ppermute(array, AXES, pairs)]
    div x1 -> x0, local copies, waits for them, and re-layouts: 36.7 us -> none  [reference(): pixel_mean_grid = total / (total_count + 1.0)]
    ppermute x0 -> x26, waiting for transfers between devices: none -> 34.5 us  [_send(): return lax.ppermute(array, AXES, pairs)]
    pallas_call x0 -> x14, Pallas kernels: none -> 27.1 us  [the longest x4 12.1 us: _pair(): pl.pallas_call(_pair_kernel, grid_spec=pltpu.PrefetchScalarGridSpec(num_s...]
    reduce_sum x1 -> x0, other arithmetic: 12.2 us -> none  [reference(): preview = jnp.mean(blocks, axis=(1, 3))]
    div x1 -> x0, blocking collectives: 9.67 us -> none  [reference(): preview = jnp.mean(blocks, axis=(1, 3))]
    add x1 -> x0, other arithmetic: 6.08 us -> none  [reference(): total = jnp.sum(partial_sums, axis=0) + jnp.sum(correction_pieces, axis=0)]
  transfers between devices with their start and end apart: 1 -> 26, of which waited for: 1 -> 11; matrix products, arithmetic and copies ran while one was open for 0% -> 0% of each run, Pallas kernels for 0% -> 19%
where the time goes in v1:
time: 107 us
  starting transfers between devices  42.2 us (39%)
  waiting for transfers between devices  34.5 us (32%)
  Pallas kernels  27.1 us (25%)
  local copies, waits for them, and re-layouts  2.19 us (2%)
    ppermute x26, starting transfers between devices, _send(): return lax.ppermute(array, AXES, pairs)  42.2 us
    ppermute x26, waiting for transfers between devices, _send(): return lax.ppermute(array, AXES, pairs)  34.5 us
    pallas_call x4, Pallas kernels, _pair(): pl.pallas_call(_pair_kernel, grid_spec=pltpu.PrefetchScalarGridSpec(num_s...  12.1 us
    pallas_call x4, Pallas kernels, _for_sibling(): pl.pallas_call(_split_kernel, grid_spec=pltpu.PrefetchScalarGridSpec(num_...  11.2 us
    unnamed x2, local copies, waits for them, and re-layouts  2.19 us
  transfers between devices with their start and end apart: 26, of which 11 were waited for; matrix products, arithmetic and copies ran while one was open for 0% of the time, Pallas kernels for 19%

profile of v1, /device:TPU:1, one launch (start us, length us, event | category | flops | bytes accessed | tf_op | source)
XLA Modules:
  0.0 106.8 jit_solution(4750566937819068536)
XLA Ops:
  0.8 2.2 %copy-done = f32[1,256,4096]{2,1,0:T(8,128)S(1)} copy-done((f32[1,256,4096]{2,1,0:T(8,128)S(1)}, f32[1,256,4096]{2,1,0:T(8,128)}, u32[]{:S(2)}) %copy-start) | copy-done | bytes 4194328
  2.9 2.8 %for_sibling.7 = f32[2,4,8,4096]{3,2,1,0:T(8,128)S(1)} custom-call(s32[4]{0:T(128)S(1)} %pad_add_fusion.pos, f32[1,256,4096]{2,1,0:T(8,128)S(1)} %copy-done, f32[1,256,4096]{2,1,0:T(8,128)} %c.15, f32[1,256,4096]{2,1,0:T(8,128)} %n.15), custom_call_target="tpu_custom_call" | custom-call | tf_op jit(solution)/shard_map/for_sibling/pallas_call | solution.py:86
  7.2 2.8 %for_sibling.5 = f32[2,4,8,4096]{3,2,1,0:T(8,128)S(1)} custom-call(s32[4]{0:T(128)S(1)} %pad_add_fusion.pos, f32[1,256,4096]{2,1,0:T(8,128)S(1)} %copy-done, f32[1,256,4096]{2,1,0:T(8,128)} %c.15, f32[1,256,4096]{2,1,0:T(8,128)} %n.15), custom_call_target="tpu_custom_call" | custom-call | tf_op jit(solution)/shard_map/for_sibling/pallas_call | solution.py:86
  10.1 2.8 %for_sibling.6 = f32[2,4,8,4096]{3,2,1,0:T(8,128)S(1)} custom-call(s32[4]{0:T(128)S(1)} %pad_add_fusion.pos, f32[1,256,4096]{2,1,0:T(8,128)S(1)} %copy-done, f32[1,256,4096]{2,1,0:T(8,128)} %c.15, f32[1,256,4096]{2,1,0:T(8,128)} %n.15), custom_call_target="tpu_custom_call" | custom-call | tf_op jit(solution)/shard_map/for_sibling/pallas_call | solution.py:86
  13.5 2.8 %for_sibling.4 = f32[2,4,8,4096]{3,2,1,0:T(8,128)S(1)} custom-call(s32[4]{0:T(128)S(1)} %pad_add_fusion.pos, f32[1,256,4096]{2,1,0:T(8,128)S(1)} %copy-done, f32[1,256,4096]{2,1,0:T(8,128)} %c.15, f32[1,256,4096]{2,1,0:T(8,128)} %n.15), custom_call_target="tpu_custom_call" | custom-call | tf_op jit(solution)/shard_map/for_sibling/pallas_call | solution.py:86
  16.4 3.0 %pair_sum.7 = f32[2,4,8,4096]{3,2,1,0:T(8,128)S(1)} custom-call(s32[4]{0:T(128)S(1)} %pad_add_fusion.pos, f32[1,256,4096]{2,1,0:T(8,128)} %p.15, f32[1,256,4096]{2,1,0:T(8,128)} %c.15, f32[1,256,4096]{2,1,0:T(8,128)} %n.15, f32[2,4,8,4096]{3,2,1,0:T(8,128)S(1)} %collective-permute-done.5.got), custom_call_target="tpu_custom_call" | custom-call | tf_op jit(solution)/shard_map/pair_sum/pallas_call | solution.py:108
  19.4 2.9 %collective-permute-start.6 = (f32[2,4,8,4096]{3,2,1,0:T(8,128)S(1)}, f32[2,4,8,4096]{3,2,1,0:T(8,128)S(1)}, u32[]{:S(2)}, u32[]{:S(2)}) collective-permute-start(f32[2,4,8,4096]{3,2,1,0:T(8,128)S(1)} %pair_sum.7), channel_id=1, source_target_pairs={{0,3},{1,0},{2,1},{3,2},{4,7},{5,4},{6,5},{7,6},{8,11},{9,8},{10,9... | collective-permute-start | bytes 3145736 | tf_op jit(solution)/shard_map/ppermute | solution.py:40
  22.3 3.0 %pair_sum.5 = f32[2,4,8,4096]{3,2,1,0:T(8,128)S(1)} custom-call(s32[4]{0:T(128)S(1)} %pad_add_fusion.pos, f32[1,256,4096]{2,1,0:T(8,128)} %p.15, f32[1,256,4096]{2,1,0:T(8,128)} %c.15, f32[1,256,4096]{2,1,0:T(8,128)} %n.15, f32[2,4,8,4096]{3,2,1,0:T(8,128)S(1)} %collective-permute-done.1.got), custom_call_target="tpu_custom_call" | custom-call | tf_op jit(solution)/shard_map/pair_sum/pallas_call | solution.py:108
  25.4 3.0 %pair_sum.6 = f32[2,4,8,4096]{3,2,1,0:T(8,128)S(1)} custom-call(s32[4]{0:T(128)S(1)} %pad_add_fusion.pos, f32[1,256,4096]{2,1,0:T(8,128)} %p.15, f32[1,256,4096]{2,1,0:T(8,128)} %c.15, f32[1,256,4096]{2,1,0:T(8,128)} %n.15, f32[2,4,8,4096]{3,2,1,0:T(8,128)S(1)} %collective-permute-done.3.got), custom_call_target="tpu_custom_call" | custom-call | tf_op jit(solution)/shard_map/pair_sum/pallas_call | solution.py:108
  30.2 3.0 %pair_sum.4.a = f32[2,4,8,4096]{3,2,1,0:T(8,128)S(1)} custom-call(s32[4]{0:T(128)S(1)} %pad_add_fusion.pos, f32[1,256,4096]{2,1,0:T(8,128)} %p.15, f32[1,256,4096]{2,1,0:T(8,128)} %c.15, f32[1,256,4096]{2,1,0:T(8,128)} %n.15, f32[2,4,8,4096]{3,2,1,0:T(8,128)S(1)} %collective-permute-done.got), custom_call_target="tpu_custom_call" | custom-call | tf_op jit(solution)/shard_map/pair_sum/pallas_call | solution.py:108
  33.2 12.1 %collective-permute-done.6.d = f32[2,4,8,4096]{3,2,1,0:T(8,128)S(1)} collective-permute-done((f32[2,4,8,4096]{3,2,1,0:T(8,128)S(1)}, f32[2,4,8,4096]{3,2,1,0:T(8,128)S(1)}, u32[]{:S(2)}, u32[]{:S(2)}) %collective-permute-start.6) | collective-permute-done | bytes 1048608 | tf_op jit(solution)/shard_map/ppermute | solution.py:40
  45.3 6.5 %collective-permute-done.2.b = f32[2,4,8,4096]{3,2,1,0:T(8,128)S(1)} collective-permute-done((f32[2,4,8,4096]{3,2,1,0:T(8,128)S(1)}, f32[2,4,8,4096]{3,2,1,0:T(8,128)S(1)}, u32[]{:S(2)}, u32[]{:S(2)}) %collective-permute-start.2) | collective-permute-done | bytes 1048608 | tf_op jit(solution)/shard_map/ppermute | solution.py:40
  54.0 3.3 %collective-permute-start.8 = (f32[2,8,4096]{2,1,0:T(8,128)S(1)}, f32[2,8,4096]{2,1,0:T(8,128)S(1)}, u32[]{:S(2)}, u32[]{:S(2)}) collective-permute-start(f32[2,8,4096]{2,1,0:T(8,128)S(1)} %get-tuple-element.14), channel_id=1, source_target_pairs={{0,16},{1,17},{2,18},{3,19},{4,20},{5,21},{6,22},{7,23},{8,24},{9,... | collective-permute-start | bytes 786440 | tf_op jit(solution)/shard_map/ppermute | solution.py:40
  58.1 2.1 %collective-permute-done.7.b = f32[2,8,4096]{2,1,0:T(8,128)S(1)} collective-permute-done((f32[2,8,4096]{2,1,0:T(8,128)S(1)}, f32[2,8,4096]{2,1,0:T(8,128)S(1)}, u32[]{:S(2)}, u32[]{:S(2)}) %collective-permute-start.7) | collective-permute-done | bytes 262176 | tf_op jit(solution)/shard_map/ppermute | solution.py:40
  60.2 4.0 %collective-permute-done.8.c = f32[2,8,4096]{2,1,0:T(8,128)S(1)} collective-permute-done((f32[2,8,4096]{2,1,0:T(8,128)S(1)}, f32[2,8,4096]{2,1,0:T(8,128)S(1)}, u32[]{:S(2)}, u32[]{:S(2)}) %collective-permute-start.8) | collective-permute-done | bytes 262176 | tf_op jit(solution)/shard_map/ppermute | solution.py:40
  66.1 2.5 %collective-permute-start.11 = (f32[2,8,1024]{2,1,0:T(8,128)S(1)}, f32[2,8,1024]{2,1,0:T(8,128)S(1)}, u32[]{:S(2)}, u32[]{:S(2)}) collective-permute-start(f32[2,8,1024]{2,1,0:T(8,128)S(1)} %get-tuple-element.18), channel_id=1, source_target_pairs={{0,64},{1,65},{2,66},{3,67},{4,68},{5,69},{6,70},{7,71},{8,72},{9,... | collective-permute-start | bytes 196616 | tf_op jit(solution)/shard_map/ppermute | solution.py:40
  72.0 2.0 %collective-permute-start.15 = (f32[2,256]{1,0:T(2,128)S(1)}, f32[2,256]{1,0:T(2,128)S(1)}, u32[]{:S(2)}, u32[]{:S(2)}) collective-permute-start(f32[2,256]{1,0:T(2,128)S(1)} %get-tuple-element.21.a), channel_id=1, source_target_pairs={{0,3},{1,0},{2,1},{3,2},{4,7},{5,4},{6,5},{7,6},{8,11},{9,8},{10,9... | collective-permute-start | bytes 6152 | tf_op jit(solution)/shard_map/ppermute | solution.py:40
  75.6 2.4 %collective-permute-done.14.c = f32[2,256]{1,0:T(2,128)S(1)} collective-permute-done((f32[2,256]{1,0:T(2,128)S(1)}, f32[2,256]{1,0:T(2,128)S(1)}, u32[]{:S(2)}, u32[]{:S(2)}) %collective-permute-start.14) | collective-permute-done | bytes 2080 | tf_op jit(solution)/shard_map/ppermute | solution.py:40
  78.5 2.2 %collective-permute-start.18 = (f32[8,1280]{1,0:T(8,128)S(1)}, f32[8,1280]{1,0:T(8,128)S(1)}, u32[]{:S(2)}, u32[]{:S(2)}) collective-permute-start(f32[8,1280]{1,0:T(8,128)S(1)} %pack.1.a), channel_id=1, source_target_pairs={{0,24},{1,25},{2,26},{3,27},{4,28},{5,29},{6,30},{7,31},{8,0},{9,1... | collective-permute-start | bytes 122888 | tf_op jit(solution)/shard_map/ppermute | solution.py:40
  81.8 3.4 %collective-permute-done.17.c = f32[8,1280]{1,0:T(8,128)S(1)} collective-permute-done((f32[8,1280]{1,0:T(8,128)S(1)}, f32[8,1280]{1,0:T(8,128)S(1)}, u32[]{:S(2)}, u32[]{:S(2)}) %collective-permute-start.17) | collective-permute-done | bytes 40992 | tf_op jit(solution)/shard_map/ppermute | solution.py:40
  87.6 8.9 %collective-permute-start.22 = (f32[4,8,1280]{2,1,0:T(8,128)S(1)}, f32[4,8,1280]{2,1,0:T(8,128)S(1)}, u32[]{:S(2)}, u32[]{:S(2)}) collective-permute-start(f32[4,8,1280]{2,1,0:T(8,128)S(1)} %gathered_row.1.refs_0_), channel_id=1, source_target_pairs={{0,32},{1,33},{2,34},{3,35},{4,36},{5,37},{6,38},{7,39},{8,40},{9,... | collective-permute-start | bytes 491528 | tf_op jit(solution)/shard_map/ppermute | solution.py:40
  96.5 2.6 %collective-permute-start.25 = (f32[4,8,1280]{2,1,0:T(8,128)S(1)}, f32[4,8,1280]{2,1,0:T(8,128)S(1)}, u32[]{:S(2)}, u32[]{:S(2)}) collective-permute-start(f32[4,8,1280]{2,1,0:T(8,128)S(1)} %collective-permute-done.21.refs_3_), channel_id=1, source_target_pairs={{0,32},{1,33},{2,34},{3,35},{4,36},{5,37},{6,38},{7,39},{8,40},{9,... | collective-permute-start | bytes 491528 | tf_op jit(solution)/shard_map/ppermute | solution.py:40
  99.1 3.0 %collective-permute-start.24 = (f32[4,8,1280]{2,1,0:T(8,128)S(1)}, f32[4,8,1280]{2,1,0:T(8,128)S(1)}, u32[]{:S(2)}, u32[]{:S(2)}) collective-permute-start(f32[4,8,1280]{2,1,0:T(8,128)S(1)} %collective-permute-done.20.refs_2_), channel_id=1, source_target_pairs={{0,32},{1,33},{2,34},{3,35},{4,36},{5,37},{6,38},{7,39},{8,40},{9,... | collective-permute-start | bytes 491528 | tf_op jit(solution)/shard_map/ppermute | solution.py:40
  104.7 2.1 %assemble.1 = (f32[64,4096]{1,0:T(8,128)}, f32[64,1024]{1,0:T(8,128)}) custom-call(s32[4]{0:T(128)S(1)} %pad_add_fusion.pos, f32[4,8,1280]{2,1,0:T(8,128)S(1)} %gathered_row.1.refs_0_, f32[4,8,1280]{2,1,0:T(8,128)S(1)} %collective-permute-done.19.refs_1_, f32[4,8,1280]{2,1,0:T(8,128)S(1)} %collective-permute-done.20.refs_2_, ...), custom_call_target="tpu_custom_call" | custom-call | tf_op jit(solution)/shard_map/assemble/pallas_call | solution.py:226
  (45 shorter events, 20.7 us)
Async XLA Ops:
  5.7 10.7 %collective-permute-start.5 = (f32[2,4,8,4096]{3,2,1,0:T(8,128)S(1)}, f32[2,4,8,4096]{3,2,1,0:T(8,128)S(1)}, u32[]{:S(2)}, u32[]{:S(2)}) collective-permute-start(f32[2,4,8,4096]{3,2,1,0:T(8,128)S(1)} %for_sibling.7), channel_id=1, source_target_pairs={{0,32},{1,33},{2,34},{3,35},{4,36},{5,37},{6,38},{7,39},{8,40},{9,... | collective-permute-start | bytes 3145736 | tf_op jit(solution)/shard_map/ppermute | solution.py:40
  10.0 12.3 %collective-permute-start.1 = (f32[2,4,8,4096]{3,2,1,0:T(8,128)S(1)}, f32[2,4,8,4096]{3,2,1,0:T(8,128)S(1)}, u32[]{:S(2)}, u32[]{:S(2)}) collective-permute-start(f32[2,4,8,4096]{3,2,1,0:T(8,128)S(1)} %for_sibling.5), channel_id=1, source_target_pairs={{0,32},{1,33},{2,34},{3,35},{4,36},{5,37},{6,38},{7,39},{8,40},{9,... | collective-permute-start | bytes 3145736 | tf_op jit(solution)/shard_map/ppermute | solution.py:40
  12.9 12.5 %collective-permute-start.3 = (f32[2,4,8,4096]{3,2,1,0:T(8,128)S(1)}, f32[2,4,8,4096]{3,2,1,0:T(8,128)S(1)}, u32[]{:S(2)}, u32[]{:S(2)}) collective-permute-start(f32[2,4,8,4096]{3,2,1,0:T(8,128)S(1)} %for_sibling.6), channel_id=1, source_target_pairs={{0,32},{1,33},{2,34},{3,35},{4,36},{5,37},{6,38},{7,39},{8,40},{9,... | collective-permute-start | bytes 3145736 | tf_op jit(solution)/shard_map/ppermute | solution.py:40
  16.3 13.9 %collective-permute-start = (f32[2,4,8,4096]{3,2,1,0:T(8,128)S(1)}, f32[2,4,8,4096]{3,2,1,0:T(8,128)S(1)}, u32[]{:S(2)}, u32[]{:S(2)}) collective-permute-start(f32[2,4,8,4096]{3,2,1,0:T(8,128)S(1)} %for_sibling.4), channel_id=1, source_target_pairs={{0,32},{1,33},{2,34},{3,35},{4,36},{5,37},{6,38},{7,39},{8,40},{9,... | collective-permute-start | bytes 3145736 | tf_op jit(solution)/shard_map/ppermute | solution.py:40
  19.4 25.9 %collective-permute-start.6 = (f32[2,4,8,4096]{3,2,1,0:T(8,128)S(1)}, f32[2,4,8,4096]{3,2,1,0:T(8,128)S(1)}, u32[]{:S(2)}, u32[]{:S(2)}) collective-permute-start(f32[2,4,8,4096]{3,2,1,0:T(8,128)S(1)} %pair_sum.7), channel_id=1, source_target_pairs={{0,3},{1,0},{2,1},{3,2},{4,7},{5,4},{6,5},{7,6},{8,11},{9,8},{10,9... | collective-permute-start | bytes 3145736 | tf_op jit(solution)/shard_map/ppermute | solution.py:40
  25.4 26.5 %collective-permute-start.2 = (f32[2,4,8,4096]{3,2,1,0:T(8,128)S(1)}, f32[2,4,8,4096]{3,2,1,0:T(8,128)S(1)}, u32[]{:S(2)}, u32[]{:S(2)}) collective-permute-start(f32[2,4,8,4096]{3,2,1,0:T(8,128)S(1)} %pair_sum.5), channel_id=1, source_target_pairs={{0,1},{1,2},{2,3},{3,0},{4,5},{5,6},{6,7},{7,4},{8,9},{9,10},{10,1... | collective-permute-start | bytes 3145736 | tf_op jit(solution)/shard_map/ppermute | solution.py:40
  28.5 23.3 %collective-permute-start.4 = (f32[2,4,8,4096]{3,2,1,0:T(8,128)S(1)}, f32[2,4,8,4096]{3,2,1,0:T(8,128)S(1)}, u32[]{:S(2)}, u32[]{:S(2)}) collective-permute-start(f32[2,4,8,4096]{3,2,1,0:T(8,128)S(1)} %pair_sum.6), channel_id=1, source_target_pairs={{0,2},{1,3},{2,0},{3,1},{4,6},{5,7},{6,4},{7,5},{8,10},{9,11},{10,... | collective-permute-start | bytes 3145736 | tf_op jit(solution)/shard_map/ppermute | solution.py:40
  52.6 7.6 %collective-permute-start.7 = (f32[2,8,4096]{2,1,0:T(8,128)S(1)}, f32[2,8,4096]{2,1,0:T(8,128)S(1)}, u32[]{:S(2)}, u32[]{:S(2)}) collective-permute-start(f32[2,8,4096]{2,1,0:T(8,128)S(1)} %get-tuple-element.13), channel_id=1, source_target_pairs={{0,8},{1,9},{2,10},{3,11},{4,12},{5,13},{6,14},{7,15},{8,16},{9,17... | collective-permute-start | bytes 786440 | tf_op jit(solution)/shard_map/ppermute | solution.py:40
  54.0 10.2 %collective-permute-start.8 = (f32[2,8,4096]{2,1,0:T(8,128)S(1)}, f32[2,8,4096]{2,1,0:T(8,128)S(1)}, u32[]{:S(2)}, u32[]{:S(2)}) collective-permute-start(f32[2,8,4096]{2,1,0:T(8,128)S(1)} %get-tuple-element.14), channel_id=1, source_target_pairs={{0,16},{1,17},{2,18},{3,19},{4,20},{5,21},{6,22},{7,23},{8,24},{9,... | collective-permute-start | bytes 786440 | tf_op jit(solution)/shard_map/ppermute | solution.py:40
  57.3 6.9 %collective-permute-start.9 = (f32[2,8,4096]{2,1,0:T(8,128)S(1)}, f32[2,8,4096]{2,1,0:T(8,128)S(1)}, u32[]{:S(2)}, u32[]{:S(2)}) collective-permute-start(f32[2,8,4096]{2,1,0:T(8,128)S(1)} %get-tuple-element.15), channel_id=1, source_target_pairs={{0,24},{1,25},{2,26},{3,27},{4,28},{5,29},{6,30},{7,31},{8,0},{9,1... | collective-permute-start | bytes 786440 | tf_op jit(solution)/shard_map/ppermute | solution.py:40
  64.8 4.9 %collective-permute-start.10 = (f32[2,8,1024]{2,1,0:T(8,128)S(1)}, f32[2,8,1024]{2,1,0:T(8,128)S(1)}, u32[]{:S(2)}, u32[]{:S(2)}) collective-permute-start(f32[2,8,1024]{2,1,0:T(8,128)S(1)} %get-tuple-element.17), channel_id=1, source_target_pairs={{0,4},{1,5},{2,6},{3,7},{4,64},{5,65},{6,66},{7,67},{8,12},{9,13},... | collective-permute-start | bytes 196616 | tf_op jit(solution)/shard_map/ppermute | solution.py:40
  66.1 4.8 %collective-permute-start.11 = (f32[2,8,1024]{2,1,0:T(8,128)S(1)}, f32[2,8,1024]{2,1,0:T(8,128)S(1)}, u32[]{:S(2)}, u32[]{:S(2)}) collective-permute-start(f32[2,8,1024]{2,1,0:T(8,128)S(1)} %get-tuple-element.18), channel_id=1, source_target_pairs={{0,64},{1,65},{2,66},{3,67},{4,68},{5,69},{6,70},{7,71},{8,72},{9,... | collective-permute-start | bytes 196616 | tf_op jit(solution)/shard_map/ppermute | solution.py:40
  72.0 3.6 %collective-permute-start.15 = (f32[2,256]{1,0:T(2,128)S(1)}, f32[2,256]{1,0:T(2,128)S(1)}, u32[]{:S(2)}, u32[]{:S(2)}) collective-permute-start(f32[2,256]{1,0:T(2,128)S(1)} %get-tuple-element.21.a), channel_id=1, source_target_pairs={{0,3},{1,0},{2,1},{3,2},{4,7},{5,4},{6,5},{7,6},{8,11},{9,8},{10,9... | collective-permute-start | bytes 6152 | tf_op jit(solution)/shard_map/ppermute | solution.py:40
  74.0 3.9 %collective-permute-start.14 = (f32[2,256]{1,0:T(2,128)S(1)}, f32[2,256]{1,0:T(2,128)S(1)}, u32[]{:S(2)}, u32[]{:S(2)}) collective-permute-start(f32[2,256]{1,0:T(2,128)S(1)} %get-tuple-element.21.a), channel_id=1, source_target_pairs={{0,2},{1,3},{2,0},{3,1},{4,6},{5,7},{6,4},{7,5},{8,10},{9,11},{10,... | collective-permute-start | bytes 6152 | tf_op jit(solution)/shard_map/ppermute | solution.py:40
  74.8 3.6 %collective-permute-start.13 = (f32[2,256]{1,0:T(2,128)S(1)}, f32[2,256]{1,0:T(2,128)S(1)}, u32[]{:S(2)}, u32[]{:S(2)}) collective-permute-start(f32[2,256]{1,0:T(2,128)S(1)} %get-tuple-element.21.a), channel_id=1, source_target_pairs={{0,1},{1,2},{2,3},{3,0},{4,5},{5,6},{6,7},{7,4},{8,9},{9,10},{10,1... | collective-permute-start | bytes 6152 | tf_op jit(solution)/shard_map/ppermute | solution.py:40
  78.5 3.3 %collective-permute-start.18 = (f32[8,1280]{1,0:T(8,128)S(1)}, f32[8,1280]{1,0:T(8,128)S(1)}, u32[]{:S(2)}, u32[]{:S(2)}) collective-permute-start(f32[8,1280]{1,0:T(8,128)S(1)} %pack.1.a), channel_id=1, source_target_pairs={{0,24},{1,25},{2,26},{3,27},{4,28},{5,29},{6,30},{7,31},{8,0},{9,1... | collective-permute-start | bytes 122888 | tf_op jit(solution)/shard_map/ppermute | solution.py:40
  80.7 4.5 %collective-permute-start.17 = (f32[8,1280]{1,0:T(8,128)S(1)}, f32[8,1280]{1,0:T(8,128)S(1)}, u32[]{:S(2)}, u32[]{:S(2)}) collective-permute-start(f32[8,1280]{1,0:T(8,128)S(1)} %pack.1.a), channel_id=1, source_target_pairs={{0,16},{1,17},{2,18},{3,19},{4,20},{5,21},{6,22},{7,23},{8,24},{9,... | collective-permute-start | bytes 122888 | tf_op jit(solution)/shard_map/ppermute | solution.py:40
  80.7 4.5 %collective-permute-start.16 = (f32[8,1280]{1,0:T(8,128)S(1)}, f32[8,1280]{1,0:T(8,128)S(1)}, u32[]{:S(2)}, u32[]{:S(2)}) collective-permute-start(f32[8,1280]{1,0:T(8,128)S(1)} %pack.1.a), channel_id=1, source_target_pairs={{0,8},{1,9},{2,10},{3,11},{4,12},{5,13},{6,14},{7,15},{8,16},{9,17... | collective-permute-start | bytes 122888 | tf_op jit(solution)/shard_map/ppermute | solution.py:40
  85.2 11.3 %collective-permute-start.21 = (f32[4,8,1280]{2,1,0:T(8,128)S(1)}, f32[4,8,1280]{2,1,0:T(8,128)S(1)}, u32[]{:S(2)}, u32[]{:S(2)}) collective-permute-start(f32[4,8,1280]{2,1,0:T(8,128)S(1)} %gathered_row.1.refs_0_), channel_id=1, source_target_pairs={{0,68},{1,69},{2,70},{3,71},{4,0},{5,1},{6,2},{7,3},{8,76},{9,77},... | collective-permute-start | bytes 491528 | tf_op jit(solution)/shard_map/ppermute | solution.py:40
  85.8 13.3 %collective-permute-start.20 = (f32[4,8,1280]{2,1,0:T(8,128)S(1)}, f32[4,8,1280]{2,1,0:T(8,128)S(1)}, u32[]{:S(2)}, u32[]{:S(2)}) collective-permute-start(f32[4,8,1280]{2,1,0:T(8,128)S(1)} %gathered_row.1.refs_0_), channel_id=1, source_target_pairs={{0,64},{1,65},{2,66},{3,67},{4,68},{5,69},{6,70},{7,71},{8,72},{9,... | collective-permute-start | bytes 491528 | tf_op jit(solution)/shard_map/ppermute | solution.py:40
  86.8 15.3 %collective-permute-start.19 = (f32[4,8,1280]{2,1,0:T(8,128)S(1)}, f32[4,8,1280]{2,1,0:T(8,128)S(1)}, u32[]{:S(2)}, u32[]{:S(2)}) collective-permute-start(f32[4,8,1280]{2,1,0:T(8,128)S(1)} %gathered_row.1.refs_0_), channel_id=1, source_target_pairs={{0,4},{1,5},{2,6},{3,7},{4,64},{5,65},{6,66},{7,67},{8,12},{9,13},... | collective-permute-start | bytes 491528 | tf_op jit(solution)/shard_map/ppermute | solution.py:40
  87.6 16.1 %collective-permute-start.22 = (f32[4,8,1280]{2,1,0:T(8,128)S(1)}, f32[4,8,1280]{2,1,0:T(8,128)S(1)}, u32[]{:S(2)}, u32[]{:S(2)}) collective-permute-start(f32[4,8,1280]{2,1,0:T(8,128)S(1)} %gathered_row.1.refs_0_), channel_id=1, source_target_pairs={{0,32},{1,33},{2,34},{3,35},{4,36},{5,37},{6,38},{7,39},{8,40},{9,... | collective-permute-start | bytes 491528 | tf_op jit(solution)/shard_map/ppermute | solution.py:40
  96.5 7.2 %collective-permute-start.25 = (f32[4,8,1280]{2,1,0:T(8,128)S(1)}, f32[4,8,1280]{2,1,0:T(8,128)S(1)}, u32[]{:S(2)}, u32[]{:S(2)}) collective-permute-start(f32[4,8,1280]{2,1,0:T(8,128)S(1)} %collective-permute-done.21.refs_3_), channel_id=1, source_target_pairs={{0,32},{1,33},{2,34},{3,35},{4,36},{5,37},{6,38},{7,39},{8,40},{9,... | collective-permute-start | bytes 491528 | tf_op jit(solution)/shard_map/ppermute | solution.py:40
  99.1 4.6 %collective-permute-start.24 = (f32[4,8,1280]{2,1,0:T(8,128)S(1)}, f32[4,8,1280]{2,1,0:T(8,128)S(1)}, u32[]{:S(2)}, u32[]{:S(2)}) collective-permute-start(f32[4,8,1280]{2,1,0:T(8,128)S(1)} %collective-permute-done.20.refs_2_), channel_id=1, source_target_pairs={{0,32},{1,33},{2,34},{3,35},{4,36},{5,37},{6,38},{7,39},{8,40},{9,... | collective-permute-start | bytes 491528 | tf_op jit(solution)/shard_map/ppermute | solution.py:40
  (3 other events, 7.9 us)

commit v2 on v1

v2 whole, which is shorter than its diff:
```python
import functools

import jax
import jax.numpy as jnp
import numpy as np
from jax import lax
from jax.experimental import pallas as pl
from jax.experimental.pallas import tpu as pltpu
from jax.sharding import PartitionSpec as P

AXES = ("gx", "gy", "gz")
F32 = jnp.float32
VMEM_LIMIT = 48 * 1024 * 1024


def _coords(d):
    gx, gy, gz = d // 32, (d // 4) % 8, d % 4
    return (gx // 2) * 2 + gy % 2, gy // 2, gz, gx % 2


def _device(x, y, z, core):
    return ((x // 2) * 2 + core) * 32 + (y * 2 + x % 2) * 4 + z


def _shift(axis0, axis1, k):
    pairs = []
    for d in range(128):
        at = list(_coords(d))
        axis = (axis0, axis1)[at[3]]
        at[axis] = (at[axis] + k) % 4
        pairs.append((d, _device(*at)))
    return pairs


_SIBLING = [(d, d ^ 32) for d in range(128)]
X, Y, Z = 0, 1, 2


def _send(array, pairs):
    return lax.ppermute(array, AXES, pairs)


def _exchange(arrays, axis0, axis1):
    got = {k: _send(arrays[k], _shift(axis0, axis1, k)) for k in (1, 3, 2)}
    return [arrays[0], got[1], got[2], got[3]]


def _position():
    gx, gy, gz = (lax.axis_index(a) for a in AXES)
    core = gx % 2
    x, y = (gx // 2) * 2 + gy % 2, gy // 2
    first, second = jnp.where(core == 0, gz, y), jnp.where(core == 0, y, gz)
    return core, x, y, gz, first, second


def _shape(*dims):
    return jax.ShapeDtypeStruct(dims, F32)


def _params():
    return pltpu.CompilerParams(vmem_limit_bytes=VMEM_LIMIT)


def _block_kernel(k, own, *refs):
    if own:
        p, c, n, got, out, held, sems = refs
    else:
        p, c, n, out, held, sems = refs
    me, _, y, z, _, _ = _position()
    core = me if own else 1 - me
    a = (jnp.where(core == 0, z, y) + k) % 4
    copies = []
    for b in range(4):
        rows = pl.ds(pl.multiple_of(jnp.where(core == 0, a * 8 + b, b * 8 + 4 + a) * 8, 8), 8)
        copies.append([pltpu.make_async_copy(array.at[0, rows], held.at[i, b], sems.at[i, b]) for i, array in enumerate((p, c, n))])
        for copy in copies[b]:
            copy.start()
    for b in range(4):
        for copy in copies[b]:
            copy.wait()
        if own:
            out[0, b] = (held[0, b] + held[1, b]) + got[0, b]
            out[1, b] = held[2, b] + got[1, b]
        else:
            out[0, b] = held[0, b] + held[1, b]
            out[1, b] = held[2, b]


def _block(arrays, k, got=None):
    own = got is not None
    hbm, vmem = pl.BlockSpec(memory_space=pltpu.HBM), pl.BlockSpec(memory_space=pltpu.VMEM)
    return pl.pallas_call(
        functools.partial(_block_kernel, k, own),
        in_specs=[hbm] * 3 + [vmem] * own,
        out_specs=vmem,
        out_shape=_shape(2, 4, 8, 4096),
        scratch_shapes=[pltpu.VMEM((3, 4, 8, 4096), F32), pltpu.SemaphoreType.DMA((3, 4))],
        compiler_params=_params(),
        name="pair_sum" if own else "for_sibling",
    )(*arrays, *([got] if own else []))


def _second_kernel(a, b, c, d, *outs):
    second = _position()[5]
    for k in range(4):
        i = (second + k) % 4
        outs[k][...] = (a[:, i] + b[:, i]) + (c[:, i] + d[:, i])


def _second(parts):
    return pl.pallas_call(
        _second_kernel, out_shape=[_shape(2, 8, 4096)] * 4, compiler_params=_params(), name="first_axis_sum"
    )(*parts)


def _third_kernel(a, b, c, d, *outs):
    x = _position()[1]
    for k in range(4):
        at = pl.ds(pl.multiple_of(((x + k) % 4) * 1024, 1024), 1024)
        outs[k][...] = (a[:, :, at] + b[:, :, at]) + (c[:, :, at] + d[:, :, at])


def _third(parts):
    return pl.pallas_call(
        _third_kernel, out_shape=[_shape(2, 8, 1024)] * 4, compiler_params=_params(), name="second_axis_sum"
    )(*parts)


def _mean_kernel(a, b, c, d, mean, preview):
    both = (a[...] + b[...]) + (c[...] + d[...])
    grid = both[0] / (both[1] + 1.0)
    mean[...] = grid
    four = jnp.concatenate(
        [jnp.sum(grid[0:4], axis=0, keepdims=True), jnp.sum(grid[4:8], axis=0, keepdims=True)], axis=0
    )
    for j in range(2):
        row = lax.broadcasted_iota(jnp.int32, (512, 128), 0)
        column = lax.broadcasted_iota(jnp.int32, (512, 128), 1)
        pool = jnp.where(row // 4 == column, 0.0625, 0.0).astype(F32)
        preview[:, j * 128 : (j + 1) * 128] = jnp.dot(
            four[:, j * 512 : (j + 1) * 512], pool, precision=lax.Precision.HIGHEST, preferred_element_type=F32
        )


def _mean(parts):
    return pl.pallas_call(
        _mean_kernel,
        out_shape=[_shape(8, 1024), _shape(2, 256)],
        compiler_params=_params(),
        name="mean_and_preview",
    )(*parts)


def _pack_kernel(mean, a, b, c, d, out):
    out[:, :1024] = mean[...]
    for k, part in enumerate((a, b, c, d)):
        out[2 * k : 2 * k + 2, 1024:] = part[...]


def _pack(mean, previews):
    return pl.pallas_call(_pack_kernel, out_shape=_shape(8, 1280), compiler_params=_params(), name="pack")(mean, *previews)


def _row_kernel(a, b, c, d, out):
    for k, part in enumerate((a, b, c, d)):
        out[k] = part[...]


def _row(parts):
    return pl.pallas_call(_row_kernel, out_shape=_shape(4, 8, 1280), compiler_params=_params(), name="gathered_row")(*parts)


def _final_kernel(*refs):
    own, other, grid, preview, lines = refs[:4], refs[4:8], refs[8], refs[9], refs[10]
    core, x, y, z, _, _ = _position()
    for mine, parts in ((True, own), (False, other)):
        c = core if mine else 1 - core
        for k2 in range(4):
            for k1 in range(4):
                fy = (y - jnp.where(c == 0, k1, k2)) % 4
                fx = (x - jnp.where(c == 0, k2, k1)) % 4
                rows = pl.multiple_of((c * 4 + fy) * 8, 8)
                columns = pl.multiple_of(fx * 1024, 1024)
                grid[pl.ds(rows, 8), pl.ds(columns, 1024)] = parts[k2][k1, :, :1024]
                for k in range(4):
                    at = pl.ds(pl.multiple_of(fx * 256, 256), 256)
                    lines[(((z - k) % 4) * 2 + c) * 4 + fy, :, at] = parts[k2][k1, 2 * k : 2 * k + 2, 1024:]
    for i in range(8):
        preview[8 * i : 8 * i + 8, :] = jnp.concatenate([lines[4 * i + j] for j in range(4)], axis=0)


def _final(own, other):
    return pl.pallas_call(
        _final_kernel,
        out_shape=[_shape(64, 4096), _shape(64, 1024)],
        scratch_shapes=[pltpu.VMEM((32, 2, 1024), F32)],
        compiler_params=_params(),
        name="assemble",
    )(*own, *other)


def _local(p, c, n):
    arrays = [pltpu.with_memory_space_constraint(array, pltpu.HBM) for array in (p, c, n)]
    order = (1, 3, 2, 0)
    got = {k: _send(_block(arrays, k), _SIBLING) for k in order}
    parts = _exchange({k: _block(arrays, k, got[k]) for k in order}, Z, Y)
    parts = _exchange(_second(parts), Y, Z)
    parts = _exchange(_third(parts), X, X)
    mean, preview = _mean(parts)
    packed = _pack(mean, _exchange([preview] * 4, Z, Z))
    row = _row(_exchange([packed] * 4, Y, X))
    own = _exchange([row] * 4, X, Y)
    other = [_send(part, _SIBLING) for part in own]
    return _final(own, other)


def solution(mesh):
    return jax.shard_map(
        _local,
        mesh=mesh,
        in_specs=(P(AXES, None, None),) * 3,
        out_specs=(P("gz", None), P(None, None)),
        check_vma=False,
    )
```

time: 107 us -> 95.2 us (0.89)
  Pallas kernels: 27.1 us -> 14.8 us
  waiting for transfers between devices: 34.5 us -> 37.6 us
  local copies, waits for them, and re-layouts: 2.19 us -> 0 us
    pallas_call x11, Pallas kernels: 26.7 us -> 14.4 us  [the longest x8 12.6 us: _block(): pl.pallas_call(functools.partial(_block_kernel, k, own), in_specs=[hbm] *...]
    ppermute x26, waiting for transfers between devices: 34.5 us -> 37.6 us  [_send(): return lax.ppermute(array, AXES, pairs)]
    unnamed x2 -> x0, local copies, waits for them, and re-layouts: 2.19 us -> none
  transfers between devices with their start and end apart: 26 -> 26, of which waited for: 11 -> 12; matrix products, arithmetic and copies ran while one was open for 0% -> 0% of each run, Pallas kernels for 19% -> 12%
where the time goes in v2:
time: 95.2 us; the launch traced here: 94.9 us
  starting transfers between devices  41.7 us (44%)
  waiting for transfers between devices  37.6 us (39%)
  Pallas kernels  14.8 us (16%)
    ppermute x26, starting transfers between devices, _send(): return lax.ppermute(array, AXES, pairs)  41.7 us
    ppermute x26, waiting for transfers between devices, _send(): return lax.ppermute(array, AXES, pairs)  37.6 us
    pallas_call x8, Pallas kernels, _block(): pl.pallas_call(functools.partial(_block_kernel, k, own), in_specs=[hbm] *...  12.6 us
  transfers between devices with their start and end apart: 26, of which 12 were waited for; matrix products, arithmetic and copies ran while one was open for 0% of the time, Pallas kernels for 12%

profile of v2, /device:TPU:1, one launch (start us, length us, event | category | flops | bytes accessed | tf_op | source)
XLA Modules:
  0.0 94.9 jit_solution(2245686189434487129)
XLA Ops:
  0.6 1.6 %for_sibling.7 = f32[2,4,8,4096]{3,2,1,0:T(8,128)S(1)} custom-call(f32[1,256,4096]{2,1,0:T(8,128)} %refs_0_.15, f32[1,256,4096]{2,1,0:T(8,128)} %refs_1_.15, f32[1,256,4096]{2,1,0:T(8,128)} %refs_2_.15), custom_call_target="tpu_custom_call" | custom-call | tf_op jit(solution)/shard_map/for_sibling/pallas_call | solution.py:92
  3.7 1.6 %for_sibling.5 = f32[2,4,8,4096]{3,2,1,0:T(8,128)S(1)} custom-call(f32[1,256,4096]{2,1,0:T(8,128)} %refs_0_.15, f32[1,256,4096]{2,1,0:T(8,128)} %refs_1_.15, f32[1,256,4096]{2,1,0:T(8,128)} %refs_2_.15), custom_call_target="tpu_custom_call" | custom-call | tf_op jit(solution)/shard_map/for_sibling/pallas_call | solution.py:92
  5.4 1.6 %for_sibling.6 = f32[2,4,8,4096]{3,2,1,0:T(8,128)S(1)} custom-call(f32[1,256,4096]{2,1,0:T(8,128)} %refs_0_.15, f32[1,256,4096]{2,1,0:T(8,128)} %refs_1_.15, f32[1,256,4096]{2,1,0:T(8,128)} %refs_2_.15), custom_call_target="tpu_custom_call" | custom-call | tf_op jit(solution)/shard_map/for_sibling/pallas_call | solution.py:92
  7.5 1.6 %for_sibling.4 = f32[2,4,8,4096]{3,2,1,0:T(8,128)S(1)} custom-call(f32[1,256,4096]{2,1,0:T(8,128)} %refs_0_.15, f32[1,256,4096]{2,1,0:T(8,128)} %refs_1_.15, f32[1,256,4096]{2,1,0:T(8,128)} %refs_2_.15), custom_call_target="tpu_custom_call" | custom-call | tf_op jit(solution)/shard_map/for_sibling/pallas_call | solution.py:92
  9.2 1.6 %pair_sum.7 = f32[2,4,8,4096]{3,2,1,0:T(8,128)S(1)} custom-call(f32[1,256,4096]{2,1,0:T(8,128)} %refs_0_.15, f32[1,256,4096]{2,1,0:T(8,128)} %refs_1_.15, f32[1,256,4096]{2,1,0:T(8,128)} %refs_2_.15, f32[2,4,8,4096]{3,2,1,0:T(8,128)S(1)} %collective-permute-done.5.refs_3_), custom_call_target="tpu_custom_call" | custom-call | tf_op jit(solution)/shard_map/pair_sum/pallas_call | solution.py:92
  10.8 2.9 %collective-permute-start.6 = (f32[2,4,8,4096]{3,2,1,0:T(8,128)S(1)}, f32[2,4,8,4096]{3,2,1,0:T(8,128)S(1)}, u32[]{:S(2)}, u32[]{:S(2)}) collective-permute-start(f32[2,4,8,4096]{3,2,1,0:T(8,128)S(1)} %pair_sum.7), channel_id=1, source_target_pairs={{0,3},{1,0},{2,1},{3,2},{4,7},{5,4},{6,5},{7,6},{8,11},{9,8},{10,9... | collective-permute-start | bytes 3145736 | tf_op jit(solution)/shard_map/ppermute | solution.py:40
  13.7 1.6 %pair_sum.5 = f32[2,4,8,4096]{3,2,1,0:T(8,128)S(1)} custom-call(f32[1,256,4096]{2,1,0:T(8,128)} %refs_0_.15, f32[1,256,4096]{2,1,0:T(8,128)} %refs_1_.15, f32[1,256,4096]{2,1,0:T(8,128)} %refs_2_.15, f32[2,4,8,4096]{3,2,1,0:T(8,128)S(1)} %collective-permute-done.1.refs_3_), custom_call_target="tpu_custom_call" | custom-call | tf_op jit(solution)/shard_map/pair_sum/pallas_call | solution.py:92
  15.4 1.6 %pair_sum.6 = f32[2,4,8,4096]{3,2,1,0:T(8,128)S(1)} custom-call(f32[1,256,4096]{2,1,0:T(8,128)} %refs_0_.15, f32[1,256,4096]{2,1,0:T(8,128)} %refs_1_.15, f32[1,256,4096]{2,1,0:T(8,128)} %refs_2_.15, f32[2,4,8,4096]{3,2,1,0:T(8,128)S(1)} %collective-permute-done.3.refs_3_), custom_call_target="tpu_custom_call" | custom-call | tf_op jit(solution)/shard_map/pair_sum/pallas_call | solution.py:92
  17.0 1.7 %collective-permute-start.4 = (f32[2,4,8,4096]{3,2,1,0:T(8,128)S(1)}, f32[2,4,8,4096]{3,2,1,0:T(8,128)S(1)}, u32[]{:S(2)}, u32[]{:S(2)}) collective-permute-start(f32[2,4,8,4096]{3,2,1,0:T(8,128)S(1)} %pair_sum.6), channel_id=1, source_target_pairs={{0,2},{1,3},{2,0},{3,1},{4,6},{5,7},{6,4},{7,5},{8,10},{9,11},{10,... | collective-permute-start | bytes 3145736 | tf_op jit(solution)/shard_map/ppermute | solution.py:40
  18.7 1.6 %pair_sum.4.a = f32[2,4,8,4096]{3,2,1,0:T(8,128)S(1)} custom-call(f32[1,256,4096]{2,1,0:T(8,128)} %refs_0_.15, f32[1,256,4096]{2,1,0:T(8,128)} %refs_1_.15, f32[1,256,4096]{2,1,0:T(8,128)} %refs_2_.15, f32[2,4,8,4096]{3,2,1,0:T(8,128)S(1)} %collective-permute-done.refs_3_), custom_call_target="tpu_custom_call" | custom-call | tf_op jit(solution)/shard_map/pair_sum/pallas_call | solution.py:92
  20.3 16.4 %collective-permute-done.6.d = f32[2,4,8,4096]{3,2,1,0:T(8,128)S(1)} collective-permute-done((f32[2,4,8,4096]{3,2,1,0:T(8,128)S(1)}, f32[2,4,8,4096]{3,2,1,0:T(8,128)S(1)}, u32[]{:S(2)}, u32[]{:S(2)}) %collective-permute-start.6) | collective-permute-done | bytes 1048608 | tf_op jit(solution)/shard_map/ppermute | solution.py:40
  36.7 5.1 %collective-permute-done.2.b = f32[2,4,8,4096]{3,2,1,0:T(8,128)S(1)} collective-permute-done((f32[2,4,8,4096]{3,2,1,0:T(8,128)S(1)}, f32[2,4,8,4096]{3,2,1,0:T(8,128)S(1)}, u32[]{:S(2)}, u32[]{:S(2)}) %collective-permute-start.2) | collective-permute-done | bytes 1048608 | tf_op jit(solution)/shard_map/ppermute | solution.py:40
  43.4 3.3 %collective-permute-start.8 = (f32[2,8,4096]{2,1,0:T(8,128)S(1)}, f32[2,8,4096]{2,1,0:T(8,128)S(1)}, u32[]{:S(2)}, u32[]{:S(2)}) collective-permute-start(f32[2,8,4096]{2,1,0:T(8,128)S(1)} %get-tuple-element.14), channel_id=1, source_target_pairs={{0,16},{1,17},{2,18},{3,19},{4,20},{5,21},{6,22},{7,23},{8,24},{9,... | collective-permute-start | bytes 786440 | tf_op jit(solution)/shard_map/ppermute | solution.py:40
  47.4 2.1 %collective-permute-done.7.b = f32[2,8,4096]{2,1,0:T(8,128)S(1)} collective-permute-done((f32[2,8,4096]{2,1,0:T(8,128)S(1)}, f32[2,8,4096]{2,1,0:T(8,128)S(1)}, u32[]{:S(2)}, u32[]{:S(2)}) %collective-permute-start.7) | collective-permute-done | bytes 262176 | tf_op jit(solution)/shard_map/ppermute | solution.py:40
  49.6 4.0 %collective-permute-done.8.c = f32[2,8,4096]{2,1,0:T(8,128)S(1)} collective-permute-done((f32[2,8,4096]{2,1,0:T(8,128)S(1)}, f32[2,8,4096]{2,1,0:T(8,128)S(1)}, u32[]{:S(2)}, u32[]{:S(2)}) %collective-permute-start.8) | collective-permute-done | bytes 262176 | tf_op jit(solution)/shard_map/ppermute | solution.py:40
  54.9 2.5 %collective-permute-start.11 = (f32[2,8,1024]{2,1,0:T(8,128)S(1)}, f32[2,8,1024]{2,1,0:T(8,128)S(1)}, u32[]{:S(2)}, u32[]{:S(2)}) collective-permute-start(f32[2,8,1024]{2,1,0:T(8,128)S(1)} %get-tuple-element.18), channel_id=1, source_target_pairs={{0,64},{1,65},{2,66},{3,67},{4,68},{5,69},{6,70},{7,71},{8,72},{9,... | collective-permute-start | bytes 196616 | tf_op jit(solution)/shard_map/ppermute | solution.py:40
  60.8 2.3 %collective-permute-start.15 = (f32[2,256]{1,0:T(2,128)S(1)}, f32[2,256]{1,0:T(2,128)S(1)}, u32[]{:S(2)}, u32[]{:S(2)}) collective-permute-start(f32[2,256]{1,0:T(2,128)S(1)} %get-tuple-element.21.a), channel_id=1, source_target_pairs={{0,3},{1,0},{2,1},{3,2},{4,7},{5,4},{6,5},{7,6},{8,11},{9,8},{10,9... | collective-permute-start | bytes 6152 | tf_op jit(solution)/shard_map/ppermute | solution.py:40
  64.4 2.7 %collective-permute-done.14.c = f32[2,256]{1,0:T(2,128)S(1)} collective-permute-done((f32[2,256]{1,0:T(2,128)S(1)}, f32[2,256]{1,0:T(2,128)S(1)}, u32[]{:S(2)}, u32[]{:S(2)}) %collective-permute-start.14) | collective-permute-done | bytes 2080 | tf_op jit(solution)/shard_map/ppermute | solution.py:40
  67.3 2.2 %collective-permute-start.18 = (f32[8,1280]{1,0:T(8,128)S(1)}, f32[8,1280]{1,0:T(8,128)S(1)}, u32[]{:S(2)}, u32[]{:S(2)}) collective-permute-start(f32[8,1280]{1,0:T(8,128)S(1)} %pack.1.a), channel_id=1, source_target_pairs={{0,24},{1,25},{2,26},{3,27},{4,28},{5,29},{6,30},{7,31},{8,0},{9,1... | collective-permute-start | bytes 122888 | tf_op jit(solution)/shard_map/ppermute | solution.py:40
  70.5 3.3 %collective-permute-done.17.c = f32[8,1280]{1,0:T(8,128)S(1)} collective-permute-done((f32[8,1280]{1,0:T(8,128)S(1)}, f32[8,1280]{1,0:T(8,128)S(1)}, u32[]{:S(2)}, u32[]{:S(2)}) %collective-permute-start.17) | collective-permute-done | bytes 40992 | tf_op jit(solution)/shard_map/ppermute | solution.py:40
  75.8 9.3 %collective-permute-start.22 = (f32[4,8,1280]{2,1,0:T(8,128)S(1)}, f32[4,8,1280]{2,1,0:T(8,128)S(1)}, u32[]{:S(2)}, u32[]{:S(2)}) collective-permute-start(f32[4,8,1280]{2,1,0:T(8,128)S(1)} %gathered_row.1.refs_0_), channel_id=1, source_target_pairs={{0,32},{1,33},{2,34},{3,35},{4,36},{5,37},{6,38},{7,39},{8,40},{9,... | collective-permute-start | bytes 491528 | tf_op jit(solution)/shard_map/ppermute | solution.py:40
  85.1 3.6 %collective-permute-start.25 = (f32[4,8,1280]{2,1,0:T(8,128)S(1)}, f32[4,8,1280]{2,1,0:T(8,128)S(1)}, u32[]{:S(2)}, u32[]{:S(2)}) collective-permute-start(f32[4,8,1280]{2,1,0:T(8,128)S(1)} %collective-permute-done.21.refs_3_), channel_id=1, source_target_pairs={{0,32},{1,33},{2,34},{3,35},{4,36},{5,37},{6,38},{7,39},{8,40},{9,... | collective-permute-start | bytes 491528 | tf_op jit(solution)/shard_map/ppermute | solution.py:40
  88.7 2.3 %collective-permute-start.24 = (f32[4,8,1280]{2,1,0:T(8,128)S(1)}, f32[4,8,1280]{2,1,0:T(8,128)S(1)}, u32[]{:S(2)}, u32[]{:S(2)}) collective-permute-start(f32[4,8,1280]{2,1,0:T(8,128)S(1)} %collective-permute-done.20.refs_2_), channel_id=1, source_target_pairs={{0,32},{1,33},{2,34},{3,35},{4,36},{5,37},{6,38},{7,39},{8,40},{9,... | collective-permute-start | bytes 491528 | tf_op jit(solution)/shard_map/ppermute | solution.py:40
  93.4 1.5 %assemble.1 = (f32[64,4096]{1,0:T(8,128)}, f32[64,1024]{1,0:T(8,128)}) custom-call(f32[4,8,1280]{2,1,0:T(8,128)S(1)} %gathered_row.1.refs_0_, f32[4,8,1280]{2,1,0:T(8,128)S(1)} %collective-permute-done.19.refs_1_, f32[4,8,1280]{2,1,0:T(8,128)S(1)} %collective-permute-done.20.refs_2_, f32[4,8,1280]{2,1,0:T(8,128)S(1)} %collective-permute-done.21.refs_3_, ...), custom_call_target="tpu_custom_call" | custom-call | tf_op jit(solution)/shard_map/assemble/pallas_call | solution.py:193
  (42 shorter events, 16.5 us)
Async XLA Ops:
  2.2 7.0 %collective-permute-start.5 = (f32[2,4,8,4096]{3,2,1,0:T(8,128)S(1)}, f32[2,4,8,4096]{3,2,1,0:T(8,128)S(1)}, u32[]{:S(2)}, u32[]{:S(2)}) collective-permute-start(f32[2,4,8,4096]{3,2,1,0:T(8,128)S(1)} %for_sibling.7), channel_id=1, source_target_pairs={{0,32},{1,33},{2,34},{3,35},{4,36},{5,37},{6,38},{7,39},{8,40},{9,... | collective-permute-start | bytes 3145736 | tf_op jit(solution)/shard_map/ppermute | solution.py:40
  5.3 8.4 %collective-permute-start.1 = (f32[2,4,8,4096]{3,2,1,0:T(8,128)S(1)}, f32[2,4,8,4096]{3,2,1,0:T(8,128)S(1)}, u32[]{:S(2)}, u32[]{:S(2)}) collective-permute-start(f32[2,4,8,4096]{3,2,1,0:T(8,128)S(1)} %for_sibling.5), channel_id=1, source_target_pairs={{0,32},{1,33},{2,34},{3,35},{4,36},{5,37},{6,38},{7,39},{8,40},{9,... | collective-permute-start | bytes 3145736 | tf_op jit(solution)/shard_map/ppermute | solution.py:40
  7.0 8.4 %collective-permute-start.3 = (f32[2,4,8,4096]{3,2,1,0:T(8,128)S(1)}, f32[2,4,8,4096]{3,2,1,0:T(8,128)S(1)}, u32[]{:S(2)}, u32[]{:S(2)}) collective-permute-start(f32[2,4,8,4096]{3,2,1,0:T(8,128)S(1)} %for_sibling.6), channel_id=1, source_target_pairs={{0,32},{1,33},{2,34},{3,35},{4,36},{5,37},{6,38},{7,39},{8,40},{9,... | collective-permute-start | bytes 3145736 | tf_op jit(solution)/shard_map/ppermute | solution.py:40
  9.1 9.6 %collective-permute-start = (f32[2,4,8,4096]{3,2,1,0:T(8,128)S(1)}, f32[2,4,8,4096]{3,2,1,0:T(8,128)S(1)}, u32[]{:S(2)}, u32[]{:S(2)}) collective-permute-start(f32[2,4,8,4096]{3,2,1,0:T(8,128)S(1)} %for_sibling.4), channel_id=1, source_target_pairs={{0,32},{1,33},{2,34},{3,35},{4,36},{5,37},{6,38},{7,39},{8,40},{9,... | collective-permute-start | bytes 3145736 | tf_op jit(solution)/shard_map/ppermute | solution.py:40
  10.8 25.9 %collective-permute-start.6 = (f32[2,4,8,4096]{3,2,1,0:T(8,128)S(1)}, f32[2,4,8,4096]{3,2,1,0:T(8,128)S(1)}, u32[]{:S(2)}, u32[]{:S(2)}) collective-permute-start(f32[2,4,8,4096]{3,2,1,0:T(8,128)S(1)} %pair_sum.7), channel_id=1, source_target_pairs={{0,3},{1,0},{2,1},{3,2},{4,7},{5,4},{6,5},{7,6},{8,11},{9,8},{10,9... | collective-permute-start | bytes 3145736 | tf_op jit(solution)/shard_map/ppermute | solution.py:40
  15.3 26.5 %collective-permute-start.2 = (f32[2,4,8,4096]{3,2,1,0:T(8,128)S(1)}, f32[2,4,8,4096]{3,2,1,0:T(8,128)S(1)}, u32[]{:S(2)}, u32[]{:S(2)}) collective-permute-start(f32[2,4,8,4096]{3,2,1,0:T(8,128)S(1)} %pair_sum.5), channel_id=1, source_target_pairs={{0,1},{1,2},{2,3},{3,0},{4,5},{5,6},{6,7},{7,4},{8,9},{9,10},{10,1... | collective-permute-start | bytes 3145736 | tf_op jit(solution)/shard_map/ppermute | solution.py:40
  17.0 24.8 %collective-permute-start.4 = (f32[2,4,8,4096]{3,2,1,0:T(8,128)S(1)}, f32[2,4,8,4096]{3,2,1,0:T(8,128)S(1)}, u32[]{:S(2)}, u32[]{:S(2)}) collective-permute-start(f32[2,4,8,4096]{3,2,1,0:T(8,128)S(1)} %pair_sum.6), channel_id=1, source_target_pairs={{0,2},{1,3},{2,0},{3,1},{4,6},{5,7},{6,4},{7,5},{8,10},{9,11},{10,... | collective-permute-start | bytes 3145736 | tf_op jit(solution)/shard_map/ppermute | solution.py:40
  42.0 7.6 %collective-permute-start.7 = (f32[2,8,4096]{2,1,0:T(8,128)S(1)}, f32[2,8,4096]{2,1,0:T(8,128)S(1)}, u32[]{:S(2)}, u32[]{:S(2)}) collective-permute-start(f32[2,8,4096]{2,1,0:T(8,128)S(1)} %get-tuple-element.13), channel_id=1, source_target_pairs={{0,8},{1,9},{2,10},{3,11},{4,12},{5,13},{6,14},{7,15},{8,16},{9,17... | collective-permute-start | bytes 786440 | tf_op jit(solution)/shard_map/ppermute | solution.py:40
  43.4 10.2 %collective-permute-start.8 = (f32[2,8,4096]{2,1,0:T(8,128)S(1)}, f32[2,8,4096]{2,1,0:T(8,128)S(1)}, u32[]{:S(2)}, u32[]{:S(2)}) collective-permute-start(f32[2,8,4096]{2,1,0:T(8,128)S(1)} %get-tuple-element.14), channel_id=1, source_target_pairs={{0,16},{1,17},{2,18},{3,19},{4,20},{5,21},{6,22},{7,23},{8,24},{9,... | collective-permute-start | bytes 786440 | tf_op jit(solution)/shard_map/ppermute | solution.py:40
  46.7 6.9 %collective-permute-start.9 = (f32[2,8,4096]{2,1,0:T(8,128)S(1)}, f32[2,8,4096]{2,1,0:T(8,128)S(1)}, u32[]{:S(2)}, u32[]{:S(2)}) collective-permute-start(f32[2,8,4096]{2,1,0:T(8,128)S(1)} %get-tuple-element.15), channel_id=1, source_target_pairs={{0,24},{1,25},{2,26},{3,27},{4,28},{5,29},{6,30},{7,31},{8,0},{9,1... | collective-permute-start | bytes 786440 | tf_op jit(solution)/shard_map/ppermute | solution.py:40
  53.6 4.9 %collective-permute-start.10 = (f32[2,8,1024]{2,1,0:T(8,128)S(1)}, f32[2,8,1024]{2,1,0:T(8,128)S(1)}, u32[]{:S(2)}, u32[]{:S(2)}) collective-permute-start(f32[2,8,1024]{2,1,0:T(8,128)S(1)} %get-tuple-element.17), channel_id=1, source_target_pairs={{0,4},{1,5},{2,6},{3,7},{4,64},{5,65},{6,66},{7,67},{8,12},{9,13},... | collective-permute-start | bytes 196616 | tf_op jit(solution)/shard_map/ppermute | solution.py:40
  54.9 4.8 %collective-permute-start.11 = (f32[2,8,1024]{2,1,0:T(8,128)S(1)}, f32[2,8,1024]{2,1,0:T(8,128)S(1)}, u32[]{:S(2)}, u32[]{:S(2)}) collective-permute-start(f32[2,8,1024]{2,1,0:T(8,128)S(1)} %get-tuple-element.18), channel_id=1, source_target_pairs={{0,64},{1,65},{2,66},{3,67},{4,68},{5,69},{6,70},{7,71},{8,72},{9,... | collective-permute-start | bytes 196616 | tf_op jit(solution)/shard_map/ppermute | solution.py:40
  60.8 3.5 %collective-permute-start.15 = (f32[2,256]{1,0:T(2,128)S(1)}, f32[2,256]{1,0:T(2,128)S(1)}, u32[]{:S(2)}, u32[]{:S(2)}) collective-permute-start(f32[2,256]{1,0:T(2,128)S(1)} %get-tuple-element.21.a), channel_id=1, source_target_pairs={{0,3},{1,0},{2,1},{3,2},{4,7},{5,4},{6,5},{7,6},{8,11},{9,8},{10,9... | collective-permute-start | bytes 6152 | tf_op jit(solution)/shard_map/ppermute | solution.py:40
  63.1 3.9 %collective-permute-start.14 = (f32[2,256]{1,0:T(2,128)S(1)}, f32[2,256]{1,0:T(2,128)S(1)}, u32[]{:S(2)}, u32[]{:S(2)}) collective-permute-start(f32[2,256]{1,0:T(2,128)S(1)} %get-tuple-element.21.a), channel_id=1, source_target_pairs={{0,2},{1,3},{2,0},{3,1},{4,6},{5,7},{6,4},{7,5},{8,10},{9,11},{10,... | collective-permute-start | bytes 6152 | tf_op jit(solution)/shard_map/ppermute | solution.py:40
  63.6 3.6 %collective-permute-start.13 = (f32[2,256]{1,0:T(2,128)S(1)}, f32[2,256]{1,0:T(2,128)S(1)}, u32[]{:S(2)}, u32[]{:S(2)}) collective-permute-start(f32[2,256]{1,0:T(2,128)S(1)} %get-tuple-element.21.a), channel_id=1, source_target_pairs={{0,1},{1,2},{2,3},{3,0},{4,5},{5,6},{6,7},{7,4},{8,9},{9,10},{10,1... | collective-permute-start | bytes 6152 | tf_op jit(solution)/shard_map/ppermute | solution.py:40
  67.3 3.3 %collective-permute-start.18 = (f32[8,1280]{1,0:T(8,128)S(1)}, f32[8,1280]{1,0:T(8,128)S(1)}, u32[]{:S(2)}, u32[]{:S(2)}) collective-permute-start(f32[8,1280]{1,0:T(8,128)S(1)} %pack.1.a), channel_id=1, source_target_pairs={{0,24},{1,25},{2,26},{3,27},{4,28},{5,29},{6,30},{7,31},{8,0},{9,1... | collective-permute-start | bytes 122888 | tf_op jit(solution)/shard_map/ppermute | solution.py:40
  69.4 4.4 %collective-permute-start.17 = (f32[8,1280]{1,0:T(8,128)S(1)}, f32[8,1280]{1,0:T(8,128)S(1)}, u32[]{:S(2)}, u32[]{:S(2)}) collective-permute-start(f32[8,1280]{1,0:T(8,128)S(1)} %pack.1.a), channel_id=1, source_target_pairs={{0,16},{1,17},{2,18},{3,19},{4,20},{5,21},{6,22},{7,23},{8,24},{9,... | collective-permute-start | bytes 122888 | tf_op jit(solution)/shard_map/ppermute | solution.py:40
  69.7 4.5 %collective-permute-start.16 = (f32[8,1280]{1,0:T(8,128)S(1)}, f32[8,1280]{1,0:T(8,128)S(1)}, u32[]{:S(2)}, u32[]{:S(2)}) collective-permute-start(f32[8,1280]{1,0:T(8,128)S(1)} %pack.1.a), channel_id=1, source_target_pairs={{0,8},{1,9},{2,10},{3,11},{4,12},{5,13},{6,14},{7,15},{8,16},{9,17... | collective-permute-start | bytes 122888 | tf_op jit(solution)/shard_map/ppermute | solution.py:40
  74.2 10.8 %collective-permute-start.21 = (f32[4,8,1280]{2,1,0:T(8,128)S(1)}, f32[4,8,1280]{2,1,0:T(8,128)S(1)}, u32[]{:S(2)}, u32[]{:S(2)}) collective-permute-start(f32[4,8,1280]{2,1,0:T(8,128)S(1)} %gathered_row.1.refs_0_), channel_id=1, source_target_pairs={{0,68},{1,69},{2,70},{3,71},{4,0},{5,1},{6,2},{7,3},{8,76},{9,77},... | collective-permute-start | bytes 491528 | tf_op jit(solution)/shard_map/ppermute | solution.py:40
  74.3 14.4 %collective-permute-start.20 = (f32[4,8,1280]{2,1,0:T(8,128)S(1)}, f32[4,8,1280]{2,1,0:T(8,128)S(1)}, u32[]{:S(2)}, u32[]{:S(2)}) collective-permute-start(f32[4,8,1280]{2,1,0:T(8,128)S(1)} %gathered_row.1.refs_0_), channel_id=1, source_target_pairs={{0,64},{1,65},{2,66},{3,67},{4,68},{5,69},{6,70},{7,71},{8,72},{9,... | collective-permute-start | bytes 491528 | tf_op jit(solution)/shard_map/ppermute | solution.py:40
  74.5 16.5 %collective-permute-start.19 = (f32[4,8,1280]{2,1,0:T(8,128)S(1)}, f32[4,8,1280]{2,1,0:T(8,128)S(1)}, u32[]{:S(2)}, u32[]{:S(2)}) collective-permute-start(f32[4,8,1280]{2,1,0:T(8,128)S(1)} %gathered_row.1.refs_0_), channel_id=1, source_target_pairs={{0,4},{1,5},{2,6},{3,7},{4,64},{5,65},{6,66},{7,67},{8,12},{9,13},... | collective-permute-start | bytes 491528 | tf_op jit(solution)/shard_map/ppermute | solution.py:40
  75.8 16.6 %collective-permute-start.22 = (f32[4,8,1280]{2,1,0:T(8,128)S(1)}, f32[4,8,1280]{2,1,0:T(8,128)S(1)}, u32[]{:S(2)}, u32[]{:S(2)}) collective-permute-start(f32[4,8,1280]{2,1,0:T(8,128)S(1)} %gathered_row.1.refs_0_), channel_id=1, source_target_pairs={{0,32},{1,33},{2,34},{3,35},{4,36},{5,37},{6,38},{7,39},{8,40},{9,... | collective-permute-start | bytes 491528 | tf_op jit(solution)/shard_map/ppermute | solution.py:40
  85.1 7.3 %collective-permute-start.25 = (f32[4,8,1280]{2,1,0:T(8,128)S(1)}, f32[4,8,1280]{2,1,0:T(8,128)S(1)}, u32[]{:S(2)}, u32[]{:S(2)}) collective-permute-start(f32[4,8,1280]{2,1,0:T(8,128)S(1)} %collective-permute-done.21.refs_3_), channel_id=1, source_target_pairs={{0,32},{1,33},{2,34},{3,35},{4,36},{5,37},{6,38},{7,39},{8,40},{9,... | collective-permute-start | bytes 491528 | tf_op jit(solution)/shard_map/ppermute | solution.py:40
  88.7 3.7 %collective-permute-start.24 = (f32[4,8,1280]{2,1,0:T(8,128)S(1)}, f32[4,8,1280]{2,1,0:T(8,128)S(1)}, u32[]{:S(2)}, u32[]{:S(2)}) collective-permute-start(f32[4,8,1280]{2,1,0:T(8,128)S(1)} %collective-permute-done.20.refs_2_), channel_id=1, source_target_pairs={{0,32},{1,33},{2,34},{3,35},{4,36},{5,37},{6,38},{7,39},{8,40},{9,... | collective-permute-start | bytes 491528 | tf_op jit(solution)/shard_map/ppermute | solution.py:40
  (2 other events, 5.5 us)

commit v3 on v2

--- a/solution.py
+++ b/solution.py
@@ -10,7 +10,8 @@
 
 AXES = ("gx", "gy", "gz")
 F32 = jnp.float32
-VMEM_LIMIT = 48 * 1024 * 1024
+COST = pl.CostEstimate(flops=1, bytes_accessed=1, transcendentals=0)
+VMEM_LIMIT = 20 * 1024 * 1024
 
 
 def _coords(d):
@@ -22,7 +23,13 @@
     return ((x // 2) * 2 + core) * 32 + (y * 2 + x % 2) * 4 + z
 
 
-def _shift(axis0, axis1, k):
+X, Y, Z = 0, 1, 2
+
+
+X, Y, Z = 0, 1, 2
+
+
+def _shift(k, axis0, axis1):
     pairs = []
     for d in range(128):
         at = list(_coords(d))
@@ -33,15 +40,14 @@
 
 
 _SIBLING = [(d, d ^ 32) for d in range(128)]
-X, Y, Z = 0, 1, 2
 
 
 def _send(array, pairs):
     return lax.ppermute(array, AXES, pairs)
 
 
-def _exchange(arrays, axis0, axis1):
-    got = {k: _send(arrays[k], _shift(axis0, axis1, k)) for k in (1, 3, 2)}
+def _exchange(arrays, *axes):
+    got = {k: _send(arrays[k], _shift(k, *axes)) for k in (1, 3, 2)}
     return [arrays[0], got[1], got[2], got[3]]
 
 
@@ -61,55 +67,79 @@
     return pltpu.CompilerParams(vmem_limit_bytes=VMEM_LIMIT)
 
 
-def _block_kernel(k, own, *refs):
-    if own:
-        p, c, n, got, out, held, sems = refs
-    else:
-        p, c, n, out, held, sems = refs
+def _blocks_kernel(wanted, *refs):
+    p, c, n = refs[:3]
+    outs, held, sems = refs[-2 - len(wanted) : -2], refs[-2], refs[-1]
     me, _, y, z, _, _ = _position()
-    core = me if own else 1 - me
-    a = (jnp.where(core == 0, z, y) + k) % 4
     copies = []
-    for b in range(4):
-        rows = pl.ds(pl.multiple_of(jnp.where(core == 0, a * 8 + b, b * 8 + 4 + a) * 8, 8), 8)
-        copies.append([pltpu.make_async_copy(array.at[0, rows], held.at[i, b], sems.at[i, b]) for i, array in enumerate((p, c, n))])
-        for copy in copies[b]:
-            copy.start()
-    for b in range(4):
-        for copy in copies[b]:
-            copy.wait()
-        if own:
-            out[0, b] = (held[0, b] + held[1, b]) + got[0, b]
-            out[1, b] = held[2, b] + got[1, b]
-        else:
-            out[0, b] = held[0, b] + held[1, b]
-            out[1, b] = held[2, b]
-
-
-def _block(arrays, k, got=None):
-    own = got is not None
-    hbm, vmem = pl.BlockSpec(memory_space=pltpu.HBM), pl.BlockSpec(memory_space=pltpu.VMEM)
-    return pl.pallas_call(
-        functools.partial(_block_kernel, k, own),
-        in_specs=[hbm] * 3 + [vmem] * own,
-        out_specs=vmem,
-        out_shape=_shape(2, 4, 8, 4096),
-        scratch_shapes=[pltpu.VMEM((3, 4, 8, 4096), F32), pltpu.SemaphoreType.DMA((3, 4))],
-        compiler_params=_params(),
-        name="pair_sum" if own else "for_sibling",
-    )(*arrays, *([got] if own else []))
-
-
-def _second_kernel(a, b, c, d, *outs):
+    for j, (k, own) in enumerate(wanted):
+        core = me if own else 1 - me
+        a = (jnp.where(core == 0, z, y) + k) % 4
+        for b in range(4):
+            rows = pl.ds(pl.multiple_of(jnp.where(core == 0, a * 8 + b, b * 8 + 4 + a) * 8, 8), 8)
+            for i, array in enumerate((p, c, n)):
+                copy = pltpu.make_async_copy(array.at[0, rows], held.at[i, j, b], sems.at[i, j, b])
+                copy.start()
+                copies.append((i, j, b, copy))
+    for i, j, b, copy in copies:
+        copy.wait()
+        if i == 2:
+            outs[j][0, b] = held[0, j, b] + held[1, j, b]
+            outs[j][1, b] = held[2, j, b]
+
+
+def _blocks(arrays, wanted, after=()):
+    return pl.pallas_call(
+        functools.partial(_blocks_kernel, wanted),
+        in_specs=[pl.BlockSpec(memory_space=pltpu.HBM)] * 3 + [pl.BlockSpec(memory_space=pl.ANY)] * len(after),
+        out_shape=[_shape(2, 4, 8, 4096)] * len(wanted),
+        scratch_shapes=[pltpu.VMEM((3, len(wanted), 4, 8, 4096), F32), pltpu.SemaphoreType.DMA((3, len(wanted), 4))],
+        compiler_params=_params(),
+        cost_estimate=COST,
+        name="local_blocks",
+    )(*arrays, *after)
+
+
+LOW, HIGH = slice(0, 2), slice(2, 4)
+
+
+def _sums_kernel(terms, *refs):
+    outs = refs[len(refs) - len(terms) :]
+    for out, pairs in zip(outs, terms):
+        total = refs[pairs[0][0]][:, pairs[0][1]]
+        for i, part in pairs[1:]:
+            total = total + refs[i][:, part]
+        out[...] = total
+
+
+def _sums(inputs, terms, name, after=()):
+    return pl.pallas_call(
+        functools.partial(_sums_kernel, terms),
+        in_specs=[pl.BlockSpec()] * len(inputs) + [pl.BlockSpec(memory_space=pl.ANY)] * len(after),
+        out_shape=[_shape(2, 2, 8, 4096)] * len(terms),
+        compiler_params=_params(),
+        cost_estimate=COST,
+        name=name,
+    )(*inputs, *after)
+
+
+def _second_kernel(low, high, got, low1, high3, *outs):
     second = _position()[5]
     for k in range(4):
         i = (second + k) % 4
-        outs[k][...] = (a[:, i] + b[:, i]) + (c[:, i] + d[:, i])
-
-
-def _second(parts):
-    return pl.pallas_call(
-        _second_kernel, out_shape=[_shape(2, 8, 4096)] * 4, compiler_params=_params(), name="first_axis_sum"
+
+        @pl.when(i < 2)
+        def _():
+            outs[k][...] = (low[:, i] + got[:, i]) + low1[:, i]
+
+        @pl.when(i >= 2)
+        def _():
+            outs[k][...] = (high[:, i - 2] + got[:, i]) + high3[:, i - 2]
+
+
+def _second(*parts):
+    return pl.pallas_call(
+        _second_kernel, out_shape=[_shape(2, 8, 4096)] * 4, compiler_params=_params(), cost_estimate=COST, name="first_axis_sum"
     )(*parts)
 
 
@@ -122,7 +152,7 @@
 
 def _third(parts):
     return pl.pallas_call(
-        _third_kernel, out_shape=[_shape(2, 8, 1024)] * 4, compiler_params=_params(), name="second_axis_sum"
+        _third_kernel, out_shape=[_shape(2, 8, 1024)] * 4, compiler_params=_params(), cost_estimate=COST, name="second_axis_sum"
     )(*parts)
 
 
@@ -147,6 +177,7 @@
         _mean_kernel,
         out_shape=[_shape(8, 1024), _shape(2, 256)],
         compiler_params=_params(),
+        cost_estimate=COST,
         name="mean_and_preview",
     )(*parts)
 
@@ -158,7 +189,7 @@
 
 
 def _pack(mean, previews):
-    return pl.pallas_call(_pack_kernel, out_shape=_shape(8, 1280), compiler_params=_params(), name="pack")(mean, *previews)
+    return pl.pallas_call(_pack_kernel, out_shape=_shape(8, 1280), compiler_params=_params(), cost_estimate=COST, name="pack")(mean, *previews)
 
 
 def _row_kernel(a, b, c, d, out):
@@ -167,7 +198,7 @@
 
 
 def _row(parts):
-    return pl.pallas_call(_row_kernel, out_shape=_shape(4, 8, 1280), compiler_params=_params(), name="gathered_row")(*parts)
+    return pl.pallas_call(_row_kernel, out_shape=_shape(4, 8, 1280), compiler_params=_params(), cost_estimate=COST, name="gathered_row")(*parts)
 
 
 def _final_kernel(*refs):
@@ -195,16 +226,40 @@
         out_shape=[_shape(64, 4096), _shape(64, 1024)],
         scratch_shapes=[pltpu.VMEM((32, 2, 1024), F32)],
         compiler_params=_params(),
+        cost_estimate=COST,
         name="assemble",
     )(*own, *other)
 
 
+def _first_axis(arrays):
+    up, down = _shift(1, Z, Y), _shift(3, Z, Y)
+    whole = slice(None)
+    sent2, own2 = _blocks(arrays, ((2, False), (2, True)))
+    got2 = _send(sent2, _SIBLING)
+    sent1, sent3 = _blocks(arrays, ((1, False), (3, False)), (own2,))
+    got1, got3 = _send(sent1, _SIBLING), _send(sent3, _SIBLING)
+    low2, high2 = _sums((own2, got2), [[(0, LOW), (1, LOW)], [(0, HIGH), (1, HIGH)]], "opposite_pair", (sent1,))
+    low, high = _send(low2, up), _send(high2, down)
+    own1, own3, sent0, own0 = _blocks(arrays, ((1, True), (3, True), (0, False), (0, True)), (low2,))
+    low1, high1, low3, high3 = _sums(
+        (own1, got1, own3, got3),
+        [[(0, LOW), (1, LOW)], [(0, HIGH), (1, HIGH)], [(2, LOW), (3, LOW)], [(2, HIGH), (3, HIGH)]],
+        "neighbour_pairs",
+    )
+    got0 = _send(sent0, _SIBLING)
+    high1, low3 = _send(high1, up), _send(low3, down)
+    low1, high3 = _sums((low1, low, high3, high), [[(0, whole), (1, whole)], [(2, whole), (3, whole)]], "passed_on")
+    low, high = _sums(
+        (own0, low3, high1),
+        [[(0, LOW), (1, whole)], [(0, HIGH), (2, whole)]],
+        "early_sum",
+    )
+    return _second(low, high, got0, _send(low1, up), _send(high3, down))
+
+
 def _local(p, c, n):
     arrays = [pltpu.with_memory_space_constraint(array, pltpu.HBM) for array in (p, c, n)]
-    order = (1, 3, 2, 0)
-    got = {k: _send(_block(arrays, k), _SIBLING) for k in order}
-    parts = _exchange({k: _block(arrays, k, got[k]) for k in order}, Z, Y)
-    parts = _exchange(_second(parts), Y, Z)
+    parts = _exchange(_first_axis(arrays), Y, Z)
     parts = _exchange(_third(parts), X, X)
     mean, preview = _mean(parts)
     packed = _pack(mean, _exchange([preview] * 4, Z, Z))

time: 95.2 us -> 85.2 us (0.89)
  waiting for transfers between devices: 37.6 us -> 29.3 us
  Pallas kernels: 14.8 us -> 10.3 us
  starting transfers between devices: 41.7 us -> 44.6 us
    ppermute x26 -> x29, waiting for transfers between devices: 37.6 us -> 29.3 us  [_send(): return lax.ppermute(array, AXES, pairs)]
    pallas_call x8 -> x7, Pallas kernels: 12.6 us -> 8.16 us  [the longest x3 7.62 us: _blocks(): pl.pallas_call(functools.partial(_blocks_kernel, wanted), in_specs=[pl.Bl...]
    ppermute x26 -> x29, starting transfers between devices: 41.7 us -> 44.6 us  [_send(): return lax.ppermute(array, AXES, pairs)]
  transfers between devices with their start and end apart: 26 -> 29, of which waited for: 12 -> 13; matrix products, arithmetic and copies ran while one was open for 0% -> 0% of each run, Pallas kernels for 12% -> 7%
where the time goes in v3:
time: 85.2 us; the launch traced here: 85 us
  starting transfers between devices  44.6 us (52%)
  waiting for transfers between devices  29.3 us (34%)
  Pallas kernels  10.3 us (12%)
    ppermute x29, starting transfers between devices, _send(): return lax.ppermute(array, AXES, pairs)  44.6 us
    ppermute x29, waiting for transfers between devices, _send(): return lax.ppermute(array, AXES, pairs)  29.3 us
    pallas_call x3, Pallas kernels, _blocks(): pl.pallas_call(functools.partial(_blocks_kernel, wanted), in_specs=[pl.Bl...  7.62 us
  transfers between devices with their start and end apart: 29, of which 13 were waited for; matrix products, arithmetic and copies ran while one was open for 0% of the time, Pallas kernels for 7%

profile of v3, /device:TPU:1, one launch (start us, length us, event | category | flops | bytes accessed | tf_op | source)
XLA Modules:
  0.0 85.0 jit_solution(3925483484255068059)
XLA Ops:
  0.6 2.2 %local_blocks.3 = (f32[2,4,8,4096]{3,2,1,0:T(8,128)S(1)}, f32[2,4,8,4096]{3,2,1,0:T(8,128)S(1)}) custom-call(f32[1,256,4096]{2,1,0:T(8,128)} %refs_0_.5, f32[1,256,4096]{2,1,0:T(8,128)} %refs_1_.5, f32[1,256,4096]{2,1,0:T(8,128)} %refs_2_.5), custom_call_target="tpu_custom_call" | custom-call | flops 1 | bytes 1 | tf_op jit(solution)/shard_map/local_blocks/pallas_call | solution.py:92
  2.8 1.5 %collective-permute-start = (f32[2,4,8,4096]{3,2,1,0:T(8,128)S(1)}, f32[2,4,8,4096]{3,2,1,0:T(8,128)S(1)}, u32[]{:S(2)}, u32[]{:S(2)}) collective-permute-start(f32[2,4,8,4096]{3,2,1,0:T(8,128)S(1)} %get-tuple-element.31), channel_id=1, source_target_pairs={{0,32},{1,33},{2,34},{3,35},{4,36},{5,37},{6,38},{7,39},{8,40},{9,... | collective-permute-start | bytes 3145736 | tf_op jit(solution)/shard_map/ppermute | solution.py:46
  4.3 2.1 %local_blocks.4 = (f32[2,4,8,4096]{3,2,1,0:T(8,128)S(1)}, f32[2,4,8,4096]{3,2,1,0:T(8,128)S(1)}) custom-call(f32[1,256,4096]{2,1,0:T(8,128)} %refs_0_.5, f32[1,256,4096]{2,1,0:T(8,128)} %refs_1_.5, f32[1,256,4096]{2,1,0:T(8,128)} %refs_2_.5, f32[2,4,8,4096]{3,2,1,0:T(8,128)S(1)} %get-tuple-element.30.refs_3_.refs_0_), custom_call_target="tpu_custom_call" | custom-call | flops 1 | bytes 1 | tf_op jit(solution)/shard_map/local_blocks/pallas_call | solution.py:92
  7.2 2.9 %collective-permute-start.7 = (f32[2,2,8,4096]{3,2,1,0:T(8,128)S(1)}, f32[2,2,8,4096]{3,2,1,0:T(8,128)S(1)}, u32[]{:S(2)}, u32[]{:S(2)}) collective-permute-start(f32[2,2,8,4096]{3,2,1,0:T(8,128)S(1)} %get-tuple-element.45), channel_id=1, source_target_pairs={{0,3},{1,0},{2,1},{3,2},{4,7},{5,4},{6,5},{7,6},{8,11},{9,8},{10,9... | collective-permute-start | bytes 1572872 | tf_op jit(solution)/shard_map/ppermute | solution.py:46
  10.1 3.3 %local_blocks.5 = (f32[2,4,8,4096]{3,2,1,0:T(8,128)S(1)}, f32[2,4,8,4096]{3,2,1,0:T(8,128)S(1)}, f32[2,4,8,4096]{3,2,1,0:T(8,128)S(1)}, f32[2,4,8,4096]{3,2,1,0:T(8,128)S(1)}) custom-call(f32[1,256,4096]{2,1,0:T(8,128)} %refs_0_.5, f32[1,256,4096]{2,1,0:T(8,128)} %refs_1_.5, f32[1,256,4096]{2,1,0:T(8,128)} %refs_2_.5, ...), custom_call_target="tpu_custom_call" | custom-call | flops 1 | bytes 1 | tf_op jit(solution)/shard_map/local_blocks/pallas_call | solution.py:92
  15.1 2.8 %collective-permute-start.3 = (f32[2,2,8,4096]{3,2,1,0:T(8,128)S(1)}, f32[2,2,8,4096]{3,2,1,0:T(8,128)S(1)}, u32[]{:S(2)}, u32[]{:S(2)}) collective-permute-start(f32[2,2,8,4096]{3,2,1,0:T(8,128)S(1)} %get-tuple-element.38), channel_id=1, source_target_pairs={{0,3},{1,0},{2,1},{3,2},{4,7},{5,4},{6,5},{7,6},{8,11},{9,8},{10,9... | collective-permute-start | bytes 1572872 | tf_op jit(solution)/shard_map/ppermute | solution.py:46
  17.9 1.7 %collective-permute-done.6.refs_1_ = f32[2,2,8,4096]{3,2,1,0:T(8,128)S(1)} collective-permute-done((f32[2,2,8,4096]{3,2,1,0:T(8,128)S(1)}, f32[2,2,8,4096]{3,2,1,0:T(8,128)S(1)}, u32[]{:S(2)}, u32[]{:S(2)}) %collective-permute-start.6) | collective-permute-done | bytes 524320 | tf_op jit(solution)/shard_map/ppermute | solution.py:46
  19.8 2.7 %collective-permute-start.9 = (f32[2,2,8,4096]{3,2,1,0:T(8,128)S(1)}, f32[2,2,8,4096]{3,2,1,0:T(8,128)S(1)}, u32[]{:S(2)}, u32[]{:S(2)}) collective-permute-start(f32[2,2,8,4096]{3,2,1,0:T(8,128)S(1)} %get-tuple-element.47), channel_id=1, source_target_pairs={{0,3},{1,0},{2,1},{3,2},{4,7},{5,4},{6,5},{7,6},{8,11},{9,8},{10,9... | collective-permute-start | bytes 1572872 | tf_op jit(solution)/shard_map/ppermute | solution.py:46
  22.5 1.5 %collective-permute-done.3.refs_1_ = f32[2,2,8,4096]{3,2,1,0:T(8,128)S(1)} collective-permute-done((f32[2,2,8,4096]{3,2,1,0:T(8,128)S(1)}, f32[2,2,8,4096]{3,2,1,0:T(8,128)S(1)}, u32[]{:S(2)}, u32[]{:S(2)}) %collective-permute-start.3) | collective-permute-done | bytes 524320 | tf_op jit(solution)/shard_map/ppermute | solution.py:46
  24.0 3.4 %collective-permute-done.4.refs_2_ = f32[2,2,8,4096]{3,2,1,0:T(8,128)S(1)} collective-permute-done((f32[2,2,8,4096]{3,2,1,0:T(8,128)S(1)}, f32[2,2,8,4096]{3,2,1,0:T(8,128)S(1)}, u32[]{:S(2)}, u32[]{:S(2)}) %collective-permute-start.4) | collective-permute-done | bytes 524320 | tf_op jit(solution)/shard_map/ppermute | solution.py:46
  27.5 5.5 %collective-permute-done.8.low1 = f32[2,2,8,4096]{3,2,1,0:T(8,128)S(1)} collective-permute-done((f32[2,2,8,4096]{3,2,1,0:T(8,128)S(1)}, f32[2,2,8,4096]{3,2,1,0:T(8,128)S(1)}, u32[]{:S(2)}, u32[]{:S(2)}) %collective-permute-start.8) | collective-permute-done | bytes 524320 | tf_op jit(solution)/shard_map/ppermute | solution.py:46
  33.3 3.8 %collective-permute-start.11 = (f32[2,8,4096]{2,1,0:T(8,128)S(1)}, f32[2,8,4096]{2,1,0:T(8,128)S(1)}, u32[]{:S(2)}, u32[]{:S(2)}) collective-permute-start(f32[2,8,4096]{2,1,0:T(8,128)S(1)} %get-tuple-element.50), channel_id=1, source_target_pairs={{0,16},{1,17},{2,18},{3,19},{4,20},{5,21},{6,22},{7,23},{8,24},{9,... | collective-permute-start | bytes 786440 | tf_op jit(solution)/shard_map/ppermute | solution.py:46
  37.3 2.8 %collective-permute-done.10.b = f32[2,8,4096]{2,1,0:T(8,128)S(1)} collective-permute-done((f32[2,8,4096]{2,1,0:T(8,128)S(1)}, f32[2,8,4096]{2,1,0:T(8,128)S(1)}, u32[]{:S(2)}, u32[]{:S(2)}) %collective-permute-start.10) | collective-permute-done | bytes 262176 | tf_op jit(solution)/shard_map/ppermute | solution.py:46
  40.0 4.0 %collective-permute-done.11.c = f32[2,8,4096]{2,1,0:T(8,128)S(1)} collective-permute-done((f32[2,8,4096]{2,1,0:T(8,128)S(1)}, f32[2,8,4096]{2,1,0:T(8,128)S(1)}, u32[]{:S(2)}, u32[]{:S(2)}) %collective-permute-start.11) | collective-permute-done | bytes 262176 | tf_op jit(solution)/shard_map/ppermute | solution.py:46
  45.3 2.5 %collective-permute-start.14 = (f32[2,8,1024]{2,1,0:T(8,128)S(1)}, f32[2,8,1024]{2,1,0:T(8,128)S(1)}, u32[]{:S(2)}, u32[]{:S(2)}) collective-permute-start(f32[2,8,1024]{2,1,0:T(8,128)S(1)} %get-tuple-element.54), channel_id=1, source_target_pairs={{0,64},{1,65},{2,66},{3,67},{4,68},{5,69},{6,70},{7,71},{8,72},{9,... | collective-permute-start | bytes 196616 | tf_op jit(solution)/shard_map/ppermute | solution.py:46
  51.6 2.4 %collective-permute-start.18 = (f32[2,256]{1,0:T(2,128)S(1)}, f32[2,256]{1,0:T(2,128)S(1)}, u32[]{:S(2)}, u32[]{:S(2)}) collective-permute-start(f32[2,256]{1,0:T(2,128)S(1)} %get-tuple-element.57.a), channel_id=1, source_target_pairs={{0,3},{1,0},{2,1},{3,2},{4,7},{5,4},{6,5},{7,6},{8,11},{9,8},{10,9... | collective-permute-start | bytes 6152 | tf_op jit(solution)/shard_map/ppermute | solution.py:46
  54.7 3.2 %collective-permute-done.17.c = f32[2,256]{1,0:T(2,128)S(1)} collective-permute-done((f32[2,256]{1,0:T(2,128)S(1)}, f32[2,256]{1,0:T(2,128)S(1)}, u32[]{:S(2)}, u32[]{:S(2)}) %collective-permute-start.17) | collective-permute-done | bytes 2080 | tf_op jit(solution)/shard_map/ppermute | solution.py:46
  57.9 2.4 %collective-permute-start.21 = (f32[8,1280]{1,0:T(8,128)S(1)}, f32[8,1280]{1,0:T(8,128)S(1)}, u32[]{:S(2)}, u32[]{:S(2)}) collective-permute-start(f32[8,1280]{1,0:T(8,128)S(1)} %pack.1.a), channel_id=1, source_target_pairs={{0,24},{1,25},{2,26},{3,27},{4,28},{5,29},{6,30},{7,31},{8,0},{9,1... | collective-permute-start | bytes 122888 | tf_op jit(solution)/shard_map/ppermute | solution.py:46
  61.4 3.4 %collective-permute-done.20.c = f32[8,1280]{1,0:T(8,128)S(1)} collective-permute-done((f32[8,1280]{1,0:T(8,128)S(1)}, f32[8,1280]{1,0:T(8,128)S(1)}, u32[]{:S(2)}, u32[]{:S(2)}) %collective-permute-start.20) | collective-permute-done | bytes 40992 | tf_op jit(solution)/shard_map/ppermute | solution.py:46
  66.4 9.3 %collective-permute-start.25 = (f32[4,8,1280]{2,1,0:T(8,128)S(1)}, f32[4,8,1280]{2,1,0:T(8,128)S(1)}, u32[]{:S(2)}, u32[]{:S(2)}) collective-permute-start(f32[4,8,1280]{2,1,0:T(8,128)S(1)} %gathered_row.1.refs_0_), channel_id=1, source_target_pairs={{0,32},{1,33},{2,34},{3,35},{4,36},{5,37},{6,38},{7,39},{8,40},{9,... | collective-permute-start | bytes 491528 | tf_op jit(solution)/shard_map/ppermute | solution.py:46
  75.7 2.2 %collective-permute-start.28 = (f32[4,8,1280]{2,1,0:T(8,128)S(1)}, f32[4,8,1280]{2,1,0:T(8,128)S(1)}, u32[]{:S(2)}, u32[]{:S(2)}) collective-permute-start(f32[4,8,1280]{2,1,0:T(8,128)S(1)} %collective-permute-done.24.refs_3_), channel_id=1, source_target_pairs={{0,32},{1,33},{2,34},{3,35},{4,36},{5,37},{6,38},{7,39},{8,40},{9,... | collective-permute-start | bytes 491528 | tf_op jit(solution)/shard_map/ppermute | solution.py:46
  77.9 2.9 %collective-permute-start.27 = (f32[4,8,1280]{2,1,0:T(8,128)S(1)}, f32[4,8,1280]{2,1,0:T(8,128)S(1)}, u32[]{:S(2)}, u32[]{:S(2)}) collective-permute-start(f32[4,8,1280]{2,1,0:T(8,128)S(1)} %collective-permute-done.23.refs_2_), channel_id=1, source_target_pairs={{0,32},{1,33},{2,34},{3,35},{4,36},{5,37},{6,38},{7,39},{8,40},{9,... | collective-permute-start | bytes 491528 | tf_op jit(solution)/shard_map/ppermute | solution.py:46
  80.8 1.6 %collective-permute-start.26 = (f32[4,8,1280]{2,1,0:T(8,128)S(1)}, f32[4,8,1280]{2,1,0:T(8,128)S(1)}, u32[]{:S(2)}, u32[]{:S(2)}) collective-permute-start(f32[4,8,1280]{2,1,0:T(8,128)S(1)} %collective-permute-done.22.refs_1_), channel_id=1, source_target_pairs={{0,32},{1,33},{2,34},{3,35},{4,36},{5,37},{6,38},{7,39},{8,40},{9,... | collective-permute-start | bytes 491528 | tf_op jit(solution)/shard_map/ppermute | solution.py:46
  83.5 1.5 %assemble.1 = (f32[64,4096]{1,0:T(8,128)}, f32[64,1024]{1,0:T(8,128)}) custom-call(f32[4,8,1280]{2,1,0:T(8,128)S(1)} %gathered_row.1.refs_0_, f32[4,8,1280]{2,1,0:T(8,128)S(1)} %collective-permute-done.22.refs_1_, f32[4,8,1280]{2,1,0:T(8,128)S(1)} %collective-permute-done.23.refs_2_, f32[4,8,1280]{2,1,0:T(8,128)S(1)} %collective-permute-done.24.refs_3_, ...), custom_call_target="tpu_custom_call" | custom-call | flops 1 | bytes 1 | tf_op jit(solution)/shard_map/assemble/pallas_call | solution.py:224
  (47 shorter events, 12.6 us)
Async XLA Ops:
  2.8 4.2 %collective-permute-start = (f32[2,4,8,4096]{3,2,1,0:T(8,128)S(1)}, f32[2,4,8,4096]{3,2,1,0:T(8,128)S(1)}, u32[]{:S(2)}, u32[]{:S(2)}) collective-permute-start(f32[2,4,8,4096]{3,2,1,0:T(8,128)S(1)} %get-tuple-element.31), channel_id=1, source_target_pairs={{0,32},{1,33},{2,34},{3,35},{4,36},{5,37},{6,38},{7,39},{8,40},{9,... | collective-permute-start | bytes 3145736 | tf_op jit(solution)/shard_map/ppermute | solution.py:46
  6.5 8.4 %collective-permute-start.2 = (f32[2,4,8,4096]{3,2,1,0:T(8,128)S(1)}, f32[2,4,8,4096]{3,2,1,0:T(8,128)S(1)}, u32[]{:S(2)}, u32[]{:S(2)}) collective-permute-start(f32[2,4,8,4096]{3,2,1,0:T(8,128)S(1)} %get-tuple-element.37), channel_id=1, source_target_pairs={{0,32},{1,33},{2,34},{3,35},{4,36},{5,37},{6,38},{7,39},{8,40},{9,... | collective-permute-start | bytes 3145736 | tf_op jit(solution)/shard_map/ppermute | solution.py:46
  6.6 8.3 %collective-permute-start.1 = (f32[2,4,8,4096]{3,2,1,0:T(8,128)S(1)}, f32[2,4,8,4096]{3,2,1,0:T(8,128)S(1)}, u32[]{:S(2)}, u32[]{:S(2)}) collective-permute-start(f32[2,4,8,4096]{3,2,1,0:T(8,128)S(1)} %get-tuple-element.32.refs_2_), channel_id=1, source_target_pairs={{0,32},{1,33},{2,34},{3,35},{4,36},{5,37},{6,38},{7,39},{8,40},{9,... | collective-permute-start | bytes 3145736 | tf_op jit(solution)/shard_map/ppermute | solution.py:46
  7.2 10.7 %collective-permute-start.7 = (f32[2,2,8,4096]{3,2,1,0:T(8,128)S(1)}, f32[2,2,8,4096]{3,2,1,0:T(8,128)S(1)}, u32[]{:S(2)}, u32[]{:S(2)}) collective-permute-start(f32[2,2,8,4096]{3,2,1,0:T(8,128)S(1)} %get-tuple-element.45), channel_id=1, source_target_pairs={{0,3},{1,0},{2,1},{3,2},{4,7},{5,4},{6,5},{7,6},{8,11},{9,8},{10,9... | collective-permute-start | bytes 1572872 | tf_op jit(solution)/shard_map/ppermute | solution.py:46
  10.1 9.5 %collective-permute-start.6 = (f32[2,2,8,4096]{3,2,1,0:T(8,128)S(1)}, f32[2,2,8,4096]{3,2,1,0:T(8,128)S(1)}, u32[]{:S(2)}, u32[]{:S(2)}) collective-permute-start(f32[2,2,8,4096]{3,2,1,0:T(8,128)S(1)} %get-tuple-element.33.refs_3_), channel_id=1, source_target_pairs={{0,1},{1,2},{2,3},{3,0},{4,5},{5,6},{6,7},{7,4},{8,9},{9,10},{10,1... | collective-permute-start | bytes 1572872 | tf_op jit(solution)/shard_map/ppermute | solution.py:46
  13.4 19.7 %collective-permute-start.5 = (f32[2,4,8,4096]{3,2,1,0:T(8,128)S(1)}, f32[2,4,8,4096]{3,2,1,0:T(8,128)S(1)}, u32[]{:S(2)}, u32[]{:S(2)}) collective-permute-start(f32[2,4,8,4096]{3,2,1,0:T(8,128)S(1)} %get-tuple-element.42), channel_id=1, source_target_pairs={{0,32},{1,33},{2,34},{3,35},{4,36},{5,37},{6,38},{7,39},{8,40},{9,... | collective-permute-start | bytes 3145736 | tf_op jit(solution)/shard_map/ppermute | solution.py:46
  15.1 8.9 %collective-permute-start.3 = (f32[2,2,8,4096]{3,2,1,0:T(8,128)S(1)}, f32[2,2,8,4096]{3,2,1,0:T(8,128)S(1)}, u32[]{:S(2)}, u32[]{:S(2)}) collective-permute-start(f32[2,2,8,4096]{3,2,1,0:T(8,128)S(1)} %get-tuple-element.38), channel_id=1, source_target_pairs={{0,3},{1,0},{2,1},{3,2},{4,7},{5,4},{6,5},{7,6},{8,11},{9,8},{10,9... | collective-permute-start | bytes 1572872 | tf_op jit(solution)/shard_map/ppermute | solution.py:46
  17.9 9.5 %collective-permute-start.4 = (f32[2,2,8,4096]{3,2,1,0:T(8,128)S(1)}, f32[2,2,8,4096]{3,2,1,0:T(8,128)S(1)}, u32[]{:S(2)}, u32[]{:S(2)}) collective-permute-start(f32[2,2,8,4096]{3,2,1,0:T(8,128)S(1)} %get-tuple-element.39), channel_id=1, source_target_pairs={{0,1},{1,2},{2,3},{3,0},{4,5},{5,6},{6,7},{7,4},{8,9},{9,10},{10,1... | collective-permute-start | bytes 1572872 | tf_op jit(solution)/shard_map/ppermute | solution.py:46
  19.7 13.3 %collective-permute-start.8 = (f32[2,2,8,4096]{3,2,1,0:T(8,128)S(1)}, f32[2,2,8,4096]{3,2,1,0:T(8,128)S(1)}, u32[]{:S(2)}, u32[]{:S(2)}) collective-permute-start(f32[2,2,8,4096]{3,2,1,0:T(8,128)S(1)} %get-tuple-element.46), channel_id=1, source_target_pairs={{0,1},{1,2},{2,3},{3,0},{4,5},{5,6},{6,7},{7,4},{8,9},{9,10},{10,1... | collective-permute-start | bytes 1572872 | tf_op jit(solution)/shard_map/ppermute | solution.py:46
  19.8 13.2 %collective-permute-start.9 = (f32[2,2,8,4096]{3,2,1,0:T(8,128)S(1)}, f32[2,2,8,4096]{3,2,1,0:T(8,128)S(1)}, u32[]{:S(2)}, u32[]{:S(2)}) collective-permute-start(f32[2,2,8,4096]{3,2,1,0:T(8,128)S(1)} %get-tuple-element.47), channel_id=1, source_target_pairs={{0,3},{1,0},{2,1},{3,2},{4,7},{5,4},{6,5},{7,6},{8,11},{9,8},{10,9... | collective-permute-start | bytes 1572872 | tf_op jit(solution)/shard_map/ppermute | solution.py:46
  33.2 6.8 %collective-permute-start.10 = (f32[2,8,4096]{2,1,0:T(8,128)S(1)}, f32[2,8,4096]{2,1,0:T(8,128)S(1)}, u32[]{:S(2)}, u32[]{:S(2)}) collective-permute-start(f32[2,8,4096]{2,1,0:T(8,128)S(1)} %get-tuple-element.49), channel_id=1, source_target_pairs={{0,8},{1,9},{2,10},{3,11},{4,12},{5,13},{6,14},{7,15},{8,16},{9,17... | collective-permute-start | bytes 786440 | tf_op jit(solution)/shard_map/ppermute | solution.py:46
  33.3 10.7 %collective-permute-start.11 = (f32[2,8,4096]{2,1,0:T(8,128)S(1)}, f32[2,8,4096]{2,1,0:T(8,128)S(1)}, u32[]{:S(2)}, u32[]{:S(2)}) collective-permute-start(f32[2,8,4096]{2,1,0:T(8,128)S(1)} %get-tuple-element.50), channel_id=1, source_target_pairs={{0,16},{1,17},{2,18},{3,19},{4,20},{5,21},{6,22},{7,23},{8,24},{9,... | collective-permute-start | bytes 786440 | tf_op jit(solution)/shard_map/ppermute | solution.py:46
  37.1 6.9 %collective-permute-start.12 = (f32[2,8,4096]{2,1,0:T(8,128)S(1)}, f32[2,8,4096]{2,1,0:T(8,128)S(1)}, u32[]{:S(2)}, u32[]{:S(2)}) collective-permute-start(f32[2,8,4096]{2,1,0:T(8,128)S(1)} %get-tuple-element.51), channel_id=1, source_target_pairs={{0,24},{1,25},{2,26},{3,27},{4,28},{5,29},{6,30},{7,31},{8,0},{9,1... | collective-permute-start | bytes 786440 | tf_op jit(solution)/shard_map/ppermute | solution.py:46
  44.1 4.9 %collective-permute-start.13 = (f32[2,8,1024]{2,1,0:T(8,128)S(1)}, f32[2,8,1024]{2,1,0:T(8,128)S(1)}, u32[]{:S(2)}, u32[]{:S(2)}) collective-permute-start(f32[2,8,1024]{2,1,0:T(8,128)S(1)} %get-tuple-element.53), channel_id=1, source_target_pairs={{0,4},{1,5},{2,6},{3,7},{4,64},{5,65},{6,66},{7,67},{8,12},{9,13},... | collective-permute-start | bytes 196616 | tf_op jit(solution)/shard_map/ppermute | solution.py:46
  45.3 4.8 %collective-permute-start.14 = (f32[2,8,1024]{2,1,0:T(8,128)S(1)}, f32[2,8,1024]{2,1,0:T(8,128)S(1)}, u32[]{:S(2)}, u32[]{:S(2)}) collective-permute-start(f32[2,8,1024]{2,1,0:T(8,128)S(1)} %get-tuple-element.54), channel_id=1, source_target_pairs={{0,64},{1,65},{2,66},{3,67},{4,68},{5,69},{6,70},{7,71},{8,72},{9,... | collective-permute-start | bytes 196616 | tf_op jit(solution)/shard_map/ppermute | solution.py:46
  53.9 3.9 %collective-permute-start.17 = (f32[2,256]{1,0:T(2,128)S(1)}, f32[2,256]{1,0:T(2,128)S(1)}, u32[]{:S(2)}, u32[]{:S(2)}) collective-permute-start(f32[2,256]{1,0:T(2,128)S(1)} %get-tuple-element.57.a), channel_id=1, source_target_pairs={{0,2},{1,3},{2,0},{3,1},{4,6},{5,7},{6,4},{7,5},{8,10},{9,11},{10,... | collective-permute-start | bytes 6152 | tf_op jit(solution)/shard_map/ppermute | solution.py:46
  60.3 4.5 %collective-permute-start.20 = (f32[8,1280]{1,0:T(8,128)S(1)}, f32[8,1280]{1,0:T(8,128)S(1)}, u32[]{:S(2)}, u32[]{:S(2)}) collective-permute-start(f32[8,1280]{1,0:T(8,128)S(1)} %pack.1.a), channel_id=1, source_target_pairs={{0,16},{1,17},{2,18},{3,19},{4,20},{5,21},{6,22},{7,23},{8,24},{9,... | collective-permute-start | bytes 122888 | tf_op jit(solution)/shard_map/ppermute | solution.py:46
  60.3 4.5 %collective-permute-start.19 = (f32[8,1280]{1,0:T(8,128)S(1)}, f32[8,1280]{1,0:T(8,128)S(1)}, u32[]{:S(2)}, u32[]{:S(2)}) collective-permute-start(f32[8,1280]{1,0:T(8,128)S(1)} %pack.1.a), channel_id=1, source_target_pairs={{0,8},{1,9},{2,10},{3,11},{4,12},{5,13},{6,14},{7,15},{8,16},{9,17... | collective-permute-start | bytes 122888 | tf_op jit(solution)/shard_map/ppermute | solution.py:46
  64.8 10.9 %collective-permute-start.24 = (f32[4,8,1280]{2,1,0:T(8,128)S(1)}, f32[4,8,1280]{2,1,0:T(8,128)S(1)}, u32[]{:S(2)}, u32[]{:S(2)}) collective-permute-start(f32[4,8,1280]{2,1,0:T(8,128)S(1)} %gathered_row.1.refs_0_), channel_id=1, source_target_pairs={{0,68},{1,69},{2,70},{3,71},{4,0},{5,1},{6,2},{7,3},{8,76},{9,77},... | collective-permute-start | bytes 491528 | tf_op jit(solution)/shard_map/ppermute | solution.py:46
  64.9 13.0 %collective-permute-start.23 = (f32[4,8,1280]{2,1,0:T(8,128)S(1)}, f32[4,8,1280]{2,1,0:T(8,128)S(1)}, u32[]{:S(2)}, u32[]{:S(2)}) collective-permute-start(f32[4,8,1280]{2,1,0:T(8,128)S(1)} %gathered_row.1.refs_0_), channel_id=1, source_target_pairs={{0,64},{1,65},{2,66},{3,67},{4,68},{5,69},{6,70},{7,71},{8,72},{9,... | collective-permute-start | bytes 491528 | tf_op jit(solution)/shard_map/ppermute | solution.py:46
  65.4 15.4 %collective-permute-start.22 = (f32[4,8,1280]{2,1,0:T(8,128)S(1)}, f32[4,8,1280]{2,1,0:T(8,128)S(1)}, u32[]{:S(2)}, u32[]{:S(2)}) collective-permute-start(f32[4,8,1280]{2,1,0:T(8,128)S(1)} %gathered_row.1.refs_0_), channel_id=1, source_target_pairs={{0,4},{1,5},{2,6},{3,7},{4,64},{5,65},{6,66},{7,67},{8,12},{9,13},... | collective-permute-start | bytes 491528 | tf_op jit(solution)/shard_map/ppermute | solution.py:46
  66.4 16.1 %collective-permute-start.25 = (f32[4,8,1280]{2,1,0:T(8,128)S(1)}, f32[4,8,1280]{2,1,0:T(8,128)S(1)}, u32[]{:S(2)}, u32[]{:S(2)}) collective-permute-start(f32[4,8,1280]{2,1,0:T(8,128)S(1)} %gathered_row.1.refs_0_), channel_id=1, source_target_pairs={{0,32},{1,33},{2,34},{3,35},{4,36},{5,37},{6,38},{7,39},{8,40},{9,... | collective-permute-start | bytes 491528 | tf_op jit(solution)/shard_map/ppermute | solution.py:46
  75.7 6.8 %collective-permute-start.28 = (f32[4,8,1280]{2,1,0:T(8,128)S(1)}, f32[4,8,1280]{2,1,0:T(8,128)S(1)}, u32[]{:S(2)}, u32[]{:S(2)}) collective-permute-start(f32[4,8,1280]{2,1,0:T(8,128)S(1)} %collective-permute-done.24.refs_3_), channel_id=1, source_target_pairs={{0,32},{1,33},{2,34},{3,35},{4,36},{5,37},{6,38},{7,39},{8,40},{9,... | collective-permute-start | bytes 491528 | tf_op jit(solution)/shard_map/ppermute | solution.py:46
  77.9 4.6 %collective-permute-start.27 = (f32[4,8,1280]{2,1,0:T(8,128)S(1)}, f32[4,8,1280]{2,1,0:T(8,128)S(1)}, u32[]{:S(2)}, u32[]{:S(2)}) collective-permute-start(f32[4,8,1280]{2,1,0:T(8,128)S(1)} %collective-permute-done.23.refs_2_), channel_id=1, source_target_pairs={{0,32},{1,33},{2,34},{3,35},{4,36},{5,37},{6,38},{7,39},{8,40},{9,... | collective-permute-start | bytes 491528 | tf_op jit(solution)/shard_map/ppermute | solution.py:46
  (5 other events, 16.6 us)

commit v4 on v3

--- a/solution.py
+++ b/solution.py
@@ -124,50 +124,63 @@
 
 
 def _second_kernel(low, high, got, low1, high3, *outs):
-    second = _position()[5]
+    core, x, y, _, _, _ = _position()
     for k in range(4):
-        i = (second + k) % 4
-
-        @pl.when(i < 2)
+        i = (y + k) % 4
+
+        @pl.when((core == 0) & (i < 2))
         def _():
-            outs[k][...] = (low[:, i] + got[:, i]) + low1[:, i]
-
-        @pl.when(i >= 2)
+            total = (low[:, i] + got[:, i]) + low1[:, i]
+            for j in range(4):
+                outs[k][:, j] = total[:, :, j * 1024 : (j + 1) * 1024]
+
+        @pl.when((core == 0) & (i >= 2))
         def _():
-            outs[k][...] = (high[:, i - 2] + got[:, i]) + high3[:, i - 2]
+            total = (high[:, i - 2] + got[:, i]) + high3[:, i - 2]
+            for j in range(4):
+                outs[k][:, j] = total[:, :, j * 1024 : (j + 1) * 1024]
+
+        @pl.when(core == 1)
+        def _():
+            at = pl.ds(pl.multiple_of(((x + k) % 4) * 1024, 1024), 1024)
+            for j in range(2):
+                outs[k][:, j] = (low[:, j, :, at] + got[:, j, :, at]) + low1[:, j, :, at]
+                outs[k][:, j + 2] = (high[:, j, :, at] + got[:, j + 2, :, at]) + high3[:, j, :, at]
 
 
 def _second(*parts):
     return pl.pallas_call(
-        _second_kernel, out_shape=[_shape(2, 8, 4096)] * 4, compiler_params=_params(), cost_estimate=COST, name="first_axis_sum"
-    )(*parts)
-
-
-def _third_kernel(a, b, c, d, *outs):
-    x = _position()[1]
-    for k in range(4):
-        at = pl.ds(pl.multiple_of(((x + k) % 4) * 1024, 1024), 1024)
-        outs[k][...] = (a[:, :, at] + b[:, :, at]) + (c[:, :, at] + d[:, :, at])
+        _second_kernel, out_shape=[_shape(2, 4, 8, 1024)] * 4, compiler_params=_params(), cost_estimate=COST, name="first_axis_sum"
+    )(*parts)
+
+
+def _third_kernel(a, b, c, d, out):
+    out[...] = (a[...] + b[...]) + (c[...] + d[...])
 
 
 def _third(parts):
     return pl.pallas_call(
-        _third_kernel, out_shape=[_shape(2, 8, 1024)] * 4, compiler_params=_params(), cost_estimate=COST, name="second_axis_sum"
-    )(*parts)
-
-
-def _mean_kernel(a, b, c, d, mean, preview):
-    both = (a[...] + b[...]) + (c[...] + d[...])
-    grid = both[0] / (both[1] + 1.0)
-    mean[...] = grid
-    four = jnp.concatenate(
-        [jnp.sum(grid[0:4], axis=0, keepdims=True), jnp.sum(grid[4:8], axis=0, keepdims=True)], axis=0
-    )
+        _third_kernel, out_shape=_shape(2, 4, 8, 1024), compiler_params=_params(), cost_estimate=COST, name="second_axis_sum"
+    )(*parts)
+
+
+def _mean_kernel(a, b, c, d, out, means):
+    core, _, _, z, _, _ = _position()
+    lines = []
+    for j in range(4):
+        total = (a[0, j] + b[0, j]) + (c[0, j] + d[0, j])
+        count = (a[1, j] + b[1, j]) + (c[1, j] + d[1, j])
+        means[j] = total / (count + 1.0)
+        lines += [jnp.sum(means[j, 0:4], axis=0, keepdims=True), jnp.sum(means[j, 4:8], axis=0, keepdims=True)]
+    four = jnp.concatenate(lines, axis=0)
+    row = lax.broadcasted_iota(jnp.int32, (512, 128), 0)
+    column = lax.broadcasted_iota(jnp.int32, (512, 128), 1)
+    pool = jnp.where(row // 4 == column, 0.0625, 0.0).astype(F32)
+    for j in range(4):
+        out[j, :, :1024] = means[jnp.where(core == 0, j, (z + j) % 4)]
+        out[j, :, 1024:] = jnp.zeros((8, 256), F32)
     for j in range(2):
-        row = lax.broadcasted_iota(jnp.int32, (512, 128), 0)
-        column = lax.broadcasted_iota(jnp.int32, (512, 128), 1)
-        pool = jnp.where(row // 4 == column, 0.0625, 0.0).astype(F32)
-        preview[:, j * 128 : (j + 1) * 128] = jnp.dot(
+        out[0, :, 1024 + j * 128 : 1024 + (j + 1) * 128] = jnp.dot(
             four[:, j * 512 : (j + 1) * 512], pool, precision=lax.Precision.HIGHEST, preferred_element_type=F32
         )
 
@@ -175,52 +188,60 @@
 def _mean(parts):
     return pl.pallas_call(
         _mean_kernel,
-        out_shape=[_shape(8, 1024), _shape(2, 256)],
+        out_shape=_shape(4, 8, 1280),
+        scratch_shapes=[pltpu.VMEM((4, 8, 1024), F32)],
         compiler_params=_params(),
         cost_estimate=COST,
         name="mean_and_preview",
     )(*parts)
-
-
-def _pack_kernel(mean, a, b, c, d, out):
-    out[:, :1024] = mean[...]
-    for k, part in enumerate((a, b, c, d)):
-        out[2 * k : 2 * k + 2, 1024:] = part[...]
-
-
-def _pack(mean, previews):
-    return pl.pallas_call(_pack_kernel, out_shape=_shape(8, 1280), compiler_params=_params(), cost_estimate=COST, name="pack")(mean, *previews)
 
 
 def _row_kernel(a, b, c, d, out):
     for k, part in enumerate((a, b, c, d)):
-        out[k] = part[...]
+        out[k] = part[0]
 
 
 def _row(parts):
-    return pl.pallas_call(_row_kernel, out_shape=_shape(4, 8, 1280), compiler_params=_params(), cost_estimate=COST, name="gathered_row")(*parts)
+    return pl.pallas_call(
+        _row_kernel, out_shape=_shape(4, 8, 1280), compiler_params=_params(), cost_estimate=COST, name="gathered_row"
+    )(*parts)
 
 
 def _final_kernel(*refs):
-    own, other, grid, preview, lines = refs[:4], refs[4:8], refs[8], refs[9], refs[10]
-    core, x, y, z, _, _ = _position()
-    for mine, parts in ((True, own), (False, other)):
-        c = core if mine else 1 - core
-        for k2 in range(4):
-            for k1 in range(4):
-                fy = (y - jnp.where(c == 0, k1, k2)) % 4
-                fx = (x - jnp.where(c == 0, k2, k1)) % 4
-                rows = pl.multiple_of((c * 4 + fy) * 8, 8)
-                columns = pl.multiple_of(fx * 1024, 1024)
-                grid[pl.ds(rows, 8), pl.ds(columns, 1024)] = parts[k2][k1, :, :1024]
-                for k in range(4):
-                    at = pl.ds(pl.multiple_of(fx * 256, 256), 256)
-                    lines[(((z - k) % 4) * 2 + c) * 4 + fy, :, at] = parts[k2][k1, 2 * k : 2 * k + 2, 1024:]
+    own_rows, other_rows, own, other = (refs[4 * i : 4 * i + 4] for i in range(4))
+    grid, preview, lines = refs[16:]
+    me, x, y, z, _, _ = _position()
+
+    def place(rows0, last0, last1):
+        for k in range(4):
+            fy = (y - k) % 4
+            for j in range(4):
+                grid[pl.ds(pl.multiple_of(fy * 8, 8), 8), j * 1024 : (j + 1) * 1024] = rows0[k][j, :, :1024]
+            fz = (z - k) % 4
+            for i in range(4):
+                for j in range(4):
+                    lines[fz * 8 + (y - i) % 4, :, j * 256 : (j + 1) * 256] = last0[k][i, 2 * j : 2 * j + 2, 1024:]
+            for i in range(4):
+                fx = (x - i) % 4
+                columns = pl.ds(pl.multiple_of(fx * 1024, 1024), 1024)
+                grid[pl.ds(pl.multiple_of(32 + fy * 8, 8), 8), columns] = last1[k][i, :, :1024]
+                at = pl.ds(pl.multiple_of(fx * 256, 256), 256)
+                for j in range(4):
+                    lines[j * 8 + 4 + fy, :, at] = last1[k][i, 2 * j : 2 * j + 2, 1024:]
+
+    @pl.when(me == 0)
+    def _():
+        place(own_rows, own, other)
+
+    @pl.when(me == 1)
+    def _():
+        place(other_rows, other, own)
+
     for i in range(8):
         preview[8 * i : 8 * i + 8, :] = jnp.concatenate([lines[4 * i + j] for j in range(4)], axis=0)
 
 
-def _final(own, other):
+def _final(own_rows, other_rows, own, other):
     return pl.pallas_call(
         _final_kernel,
         out_shape=[_shape(64, 4096), _shape(64, 1024)],
@@ -228,7 +249,7 @@
         compiler_params=_params(),
         cost_estimate=COST,
         name="assemble",
-    )(*own, *other)
+    )(*own_rows, *other_rows, *own, *other)
 
 
 def _first_axis(arrays):
@@ -259,14 +280,11 @@
 
 def _local(p, c, n):
     arrays = [pltpu.with_memory_space_constraint(array, pltpu.HBM) for array in (p, c, n)]
-    parts = _exchange(_first_axis(arrays), Y, Z)
-    parts = _exchange(_third(parts), X, X)
-    mean, preview = _mean(parts)
-    packed = _pack(mean, _exchange([preview] * 4, Z, Z))
-    row = _row(_exchange([packed] * 4, Y, X))
-    own = _exchange([row] * 4, X, Y)
-    other = [_send(part, _SIBLING) for part in own]
-    return _final(own, other)
+    both = _third(_exchange(_first_axis(arrays), Y, X))
+    packed = _mean(_exchange([both] * 4, X, Z))
+    rows = _exchange([packed] * 4, Y, X)
+    last = _exchange([_row(rows)] * 4, Z, Y)
+    return _final(rows, [_send(part, _SIBLING) for part in rows], last, [_send(part, _SIBLING) for part in last])
 
 
 def solution(mesh):

time: 85.2 us -> 83.5 us (0.980)
  waiting for transfers between devices: 29.3 us -> 28 us
    ppermute x29 -> x30, waiting for transfers between devices: 29.3 us -> 28 us  [_send(): return lax.ppermute(array, AXES, pairs)]
    ppermute x29 -> x30, starting transfers between devices: 44.6 us -> 44.5 us  [_send(): return lax.ppermute(array, AXES, pairs)]
  transfers between devices with their start and end apart: 29 -> 30, of which waited for: 13 -> 11; matrix products, arithmetic and copies ran while one was open for 0% -> 0% of each run, Pallas kernels for 7% -> 7%
where the time goes in v4:
time: 83.5 us; the launch traced here: 83.4 us
  starting transfers between devices  44.5 us (53%)
  waiting for transfers between devices  28 us (34%)
  Pallas kernels  10.1 us (12%)
    ppermute x30, starting transfers between devices, _send(): return lax.ppermute(array, AXES, pairs)  44.5 us
    ppermute x30, waiting for transfers between devices, _send(): return lax.ppermute(array, AXES, pairs)  28 us
    pallas_call x3, Pallas kernels, _blocks(): pl.pallas_call(functools.partial(_blocks_kernel, wanted), in_specs=[pl.Bl...  7.62 us
  transfers between devices with their start and end apart: 30, of which 11 were waited for; matrix products, arithmetic and copies ran while one was open for 0% of the time, Pallas kernels for 7%

profile of v4, /device:TPU:1, one launch (start us, length us, event | category | flops | bytes accessed | tf_op | source)
XLA Modules:
  0.0 83.4 jit_solution(8185154930279555240)
XLA Ops:
  0.6 2.2 %local_blocks.3 = (f32[2,4,8,4096]{3,2,1,0:T(8,128)S(1)}, f32[2,4,8,4096]{3,2,1,0:T(8,128)S(1)}) custom-call(f32[1,256,4096]{2,1,0:T(8,128)} %refs_0_.5, f32[1,256,4096]{2,1,0:T(8,128)} %refs_1_.5, f32[1,256,4096]{2,1,0:T(8,128)} %refs_2_.5), custom_call_target="tpu_custom_call" | custom-call | flops 1 | bytes 1 | tf_op jit(solution)/shard_map/local_blocks/pallas_call | solution.py:92
  4.3 2.1 %local_blocks.4 = (f32[2,4,8,4096]{3,2,1,0:T(8,128)S(1)}, f32[2,4,8,4096]{3,2,1,0:T(8,128)S(1)}) custom-call(f32[1,256,4096]{2,1,0:T(8,128)} %refs_0_.5, f32[1,256,4096]{2,1,0:T(8,128)} %refs_1_.5, f32[1,256,4096]{2,1,0:T(8,128)} %refs_2_.5, f32[2,4,8,4096]{3,2,1,0:T(8,128)S(1)} %get-tuple-element.24.refs_3_.refs_0_), custom_call_target="tpu_custom_call" | custom-call | flops 1 | bytes 1 | tf_op jit(solution)/shard_map/local_blocks/pallas_call | solution.py:92
  7.2 2.9 %collective-permute-start.7 = (f32[2,2,8,4096]{3,2,1,0:T(8,128)S(1)}, f32[2,2,8,4096]{3,2,1,0:T(8,128)S(1)}, u32[]{:S(2)}, u32[]{:S(2)}) collective-permute-start(f32[2,2,8,4096]{3,2,1,0:T(8,128)S(1)} %get-tuple-element.39), channel_id=1, source_target_pairs={{0,3},{1,0},{2,1},{3,2},{4,7},{5,4},{6,5},{7,6},{8,11},{9,8},{10,9... | collective-permute-start | bytes 1572872 | tf_op jit(solution)/shard_map/ppermute | solution.py:46
  10.1 3.3 %local_blocks.5 = (f32[2,4,8,4096]{3,2,1,0:T(8,128)S(1)}, f32[2,4,8,4096]{3,2,1,0:T(8,128)S(1)}, f32[2,4,8,4096]{3,2,1,0:T(8,128)S(1)}, f32[2,4,8,4096]{3,2,1,0:T(8,128)S(1)}) custom-call(f32[1,256,4096]{2,1,0:T(8,128)} %refs_0_.5, f32[1,256,4096]{2,1,0:T(8,128)} %refs_1_.5, f32[1,256,4096]{2,1,0:T(8,128)} %refs_2_.5, ...), custom_call_target="tpu_custom_call" | custom-call | flops 1 | bytes 1 | tf_op jit(solution)/shard_map/local_blocks/pallas_call | solution.py:92
  15.1 2.8 %collective-permute-start.3 = (f32[2,2,8,4096]{3,2,1,0:T(8,128)S(1)}, f32[2,2,8,4096]{3,2,1,0:T(8,128)S(1)}, u32[]{:S(2)}, u32[]{:S(2)}) collective-permute-start(f32[2,2,8,4096]{3,2,1,0:T(8,128)S(1)} %get-tuple-element.32), channel_id=1, source_target_pairs={{0,3},{1,0},{2,1},{3,2},{4,7},{5,4},{6,5},{7,6},{8,11},{9,8},{10,9... | collective-permute-start | bytes 1572872 | tf_op jit(solution)/shard_map/ppermute | solution.py:46
  17.9 1.7 %collective-permute-done.6.refs_1_ = f32[2,2,8,4096]{3,2,1,0:T(8,128)S(1)} collective-permute-done((f32[2,2,8,4096]{3,2,1,0:T(8,128)S(1)}, f32[2,2,8,4096]{3,2,1,0:T(8,128)S(1)}, u32[]{:S(2)}, u32[]{:S(2)}) %collective-permute-start.6) | collective-permute-done | bytes 524320 | tf_op jit(solution)/shard_map/ppermute | solution.py:46
  19.8 2.7 %collective-permute-start.9 = (f32[2,2,8,4096]{3,2,1,0:T(8,128)S(1)}, f32[2,2,8,4096]{3,2,1,0:T(8,128)S(1)}, u32[]{:S(2)}, u32[]{:S(2)}) collective-permute-start(f32[2,2,8,4096]{3,2,1,0:T(8,128)S(1)} %get-tuple-element.41), channel_id=1, source_target_pairs={{0,3},{1,0},{2,1},{3,2},{4,7},{5,4},{6,5},{7,6},{8,11},{9,8},{10,9... | collective-permute-start | bytes 1572872 | tf_op jit(solution)/shard_map/ppermute | solution.py:46
  22.5 1.5 %collective-permute-done.3.refs_1_ = f32[2,2,8,4096]{3,2,1,0:T(8,128)S(1)} collective-permute-done((f32[2,2,8,4096]{3,2,1,0:T(8,128)S(1)}, f32[2,2,8,4096]{3,2,1,0:T(8,128)S(1)}, u32[]{:S(2)}, u32[]{:S(2)}) %collective-permute-start.3) | collective-permute-done | bytes 524320 | tf_op jit(solution)/shard_map/ppermute | solution.py:46
  24.0 3.4 %collective-permute-done.4.refs_2_ = f32[2,2,8,4096]{3,2,1,0:T(8,128)S(1)} collective-permute-done((f32[2,2,8,4096]{3,2,1,0:T(8,128)S(1)}, f32[2,2,8,4096]{3,2,1,0:T(8,128)S(1)}, u32[]{:S(2)}, u32[]{:S(2)}) %collective-permute-start.4) | collective-permute-done | bytes 524320 | tf_op jit(solution)/shard_map/ppermute | solution.py:46
  27.5 5.5 %collective-permute-done.8.low1 = f32[2,2,8,4096]{3,2,1,0:T(8,128)S(1)} collective-permute-done((f32[2,2,8,4096]{3,2,1,0:T(8,128)S(1)}, f32[2,2,8,4096]{3,2,1,0:T(8,128)S(1)}, u32[]{:S(2)}, u32[]{:S(2)}) %collective-permute-start.8) | collective-permute-done | bytes 524320 | tf_op jit(solution)/shard_map/ppermute | solution.py:46
  34.6 2.5 %collective-permute-start.11 = (f32[2,4,8,1024]{3,2,1,0:T(8,128)S(1)}, f32[2,4,8,1024]{3,2,1,0:T(8,128)S(1)}, u32[]{:S(2)}, u32[]{:S(2)}) collective-permute-start(f32[2,4,8,1024]{3,2,1,0:T(8,128)S(1)} %get-tuple-element.44), channel_id=1, source_target_pairs={{0,16},{1,17},{2,18},{3,19},{4,20},{5,21},{6,22},{7,23},{8,24},{9,... | collective-permute-start | bytes 786440 | tf_op jit(solution)/shard_map/ppermute | solution.py:46
  38.2 1.9 %collective-permute-done.10.b = f32[2,4,8,1024]{3,2,1,0:T(8,128)S(1)} collective-permute-done((f32[2,4,8,1024]{3,2,1,0:T(8,128)S(1)}, f32[2,4,8,1024]{3,2,1,0:T(8,128)S(1)}, u32[]{:S(2)}, u32[]{:S(2)}) %collective-permute-start.10) | collective-permute-done | bytes 262176 | tf_op jit(solution)/shard_map/ppermute | solution.py:46
  40.1 3.8 %collective-permute-done.11.c = f32[2,4,8,1024]{3,2,1,0:T(8,128)S(1)} collective-permute-done((f32[2,4,8,1024]{3,2,1,0:T(8,128)S(1)}, f32[2,4,8,1024]{3,2,1,0:T(8,128)S(1)}, u32[]{:S(2)}, u32[]{:S(2)}) %collective-permute-start.11) | collective-permute-done | bytes 262176 | tf_op jit(solution)/shard_map/ppermute | solution.py:46
  43.9 2.7 %collective-permute-start.15 = (f32[2,4,8,1024]{3,2,1,0:T(8,128)S(1)}, f32[2,4,8,1024]{3,2,1,0:T(8,128)S(1)}, u32[]{:S(2)}, u32[]{:S(2)}) collective-permute-start(f32[2,4,8,1024]{3,2,1,0:T(8,128)S(1)} %second_axis_sum.1.a), channel_id=1, source_target_pairs={{0,68},{1,69},{2,70},{3,71},{4,0},{5,1},{6,2},{7,3},{8,76},{9,77},... | collective-permute-start | bytes 786440 | tf_op jit(solution)/shard_map/ppermute | solution.py:46
  47.3 5.5 %collective-permute-done.15.d = f32[2,4,8,1024]{3,2,1,0:T(8,128)S(1)} collective-permute-done((f32[2,4,8,1024]{3,2,1,0:T(8,128)S(1)}, f32[2,4,8,1024]{3,2,1,0:T(8,128)S(1)}, u32[]{:S(2)}, u32[]{:S(2)}) %collective-permute-start.15) | collective-permute-done | bytes 262176 | tf_op jit(solution)/shard_map/ppermute | solution.py:46
  53.5 2.7 %collective-permute-done.13.b = f32[2,4,8,1024]{3,2,1,0:T(8,128)S(1)} collective-permute-done((f32[2,4,8,1024]{3,2,1,0:T(8,128)S(1)}, f32[2,4,8,1024]{3,2,1,0:T(8,128)S(1)}, u32[]{:S(2)}, u32[]{:S(2)}) %collective-permute-start.13) | collective-permute-done | bytes 262176 | tf_op jit(solution)/shard_map/ppermute | solution.py:46
  56.6 2.0 %collective-permute-start.18 = (f32[4,8,1280]{2,1,0:T(8,128)S(1)}, f32[4,8,1280]{2,1,0:T(8,128)S(1)}, u32[]{:S(2)}, u32[]{:S(2)}) collective-permute-start(f32[4,8,1280]{2,1,0:T(8,128)S(1)} %mean_and_preview.1.a.refs_0_), channel_id=1, source_target_pairs={{0,24},{1,25},{2,26},{3,27},{4,28},{5,29},{6,30},{7,31},{8,0},{9,1... | collective-permute-start | bytes 491528 | tf_op jit(solution)/shard_map/ppermute | solution.py:46
  59.6 5.1 %collective-permute-start.19 = (f32[4,8,1280]{2,1,0:T(8,128)S(1)}, f32[4,8,1280]{2,1,0:T(8,128)S(1)}, u32[]{:S(2)}, u32[]{:S(2)}) collective-permute-start(f32[4,8,1280]{2,1,0:T(8,128)S(1)} %mean_and_preview.1.a.refs_0_), channel_id=1, source_target_pairs={{0,32},{1,33},{2,34},{3,35},{4,36},{5,37},{6,38},{7,39},{8,40},{9,... | collective-permute-start | bytes 491528 | tf_op jit(solution)/shard_map/ppermute | solution.py:46
  64.7 2.6 %collective-permute-start.22 = (f32[4,8,1280]{2,1,0:T(8,128)S(1)}, f32[4,8,1280]{2,1,0:T(8,128)S(1)}, u32[]{:S(2)}, u32[]{:S(2)}) collective-permute-start(f32[4,8,1280]{2,1,0:T(8,128)S(1)} %collective-permute-done.18.d.refs_3_), channel_id=1, source_target_pairs={{0,32},{1,33},{2,34},{3,35},{4,36},{5,37},{6,38},{7,39},{8,40},{9,... | collective-permute-start | bytes 491528 | tf_op jit(solution)/shard_map/ppermute | solution.py:46
  67.3 2.3 %collective-permute-start.21 = (f32[4,8,1280]{2,1,0:T(8,128)S(1)}, f32[4,8,1280]{2,1,0:T(8,128)S(1)}, u32[]{:S(2)}, u32[]{:S(2)}) collective-permute-start(f32[4,8,1280]{2,1,0:T(8,128)S(1)} %collective-permute-done.17.c.refs_2_), channel_id=1, source_target_pairs={{0,32},{1,33},{2,34},{3,35},{4,36},{5,37},{6,38},{7,39},{8,40},{9,... | collective-permute-start | bytes 491528 | tf_op jit(solution)/shard_map/ppermute | solution.py:46
  71.7 1.8 %collective-permute-start.26 = (f32[4,8,1280]{2,1,0:T(8,128)S(1)}, f32[4,8,1280]{2,1,0:T(8,128)S(1)}, u32[]{:S(2)}, u32[]{:S(2)}) collective-permute-start(f32[4,8,1280]{2,1,0:T(8,128)S(1)} %gathered_row.1.refs_8_), channel_id=1, source_target_pairs={{0,32},{1,33},{2,34},{3,35},{4,36},{5,37},{6,38},{7,39},{8,40},{9,... | collective-permute-start | bytes 491528 | tf_op jit(solution)/shard_map/ppermute | solution.py:46
  73.9 2.8 %collective-permute-start.29 = (f32[4,8,1280]{2,1,0:T(8,128)S(1)}, f32[4,8,1280]{2,1,0:T(8,128)S(1)}, u32[]{:S(2)}, u32[]{:S(2)}) collective-permute-start(f32[4,8,1280]{2,1,0:T(8,128)S(1)} %collective-permute-done.25.refs_11_), channel_id=1, source_target_pairs={{0,32},{1,33},{2,34},{3,35},{4,36},{5,37},{6,38},{7,39},{8,40},{9,... | collective-permute-start | bytes 491528 | tf_op jit(solution)/shard_map/ppermute | solution.py:46
  76.7 2.8 %collective-permute-start.28 = (f32[4,8,1280]{2,1,0:T(8,128)S(1)}, f32[4,8,1280]{2,1,0:T(8,128)S(1)}, u32[]{:S(2)}, u32[]{:S(2)}) collective-permute-start(f32[4,8,1280]{2,1,0:T(8,128)S(1)} %collective-permute-done.24.refs_10_), channel_id=1, source_target_pairs={{0,32},{1,33},{2,34},{3,35},{4,36},{5,37},{6,38},{7,39},{8,40},{9,... | collective-permute-start | bytes 491528 | tf_op jit(solution)/shard_map/ppermute | solution.py:46
  79.5 1.6 %collective-permute-start.27 = (f32[4,8,1280]{2,1,0:T(8,128)S(1)}, f32[4,8,1280]{2,1,0:T(8,128)S(1)}, u32[]{:S(2)}, u32[]{:S(2)}) collective-permute-start(f32[4,8,1280]{2,1,0:T(8,128)S(1)} %collective-permute-done.23.refs_9_), channel_id=1, source_target_pairs={{0,32},{1,33},{2,34},{3,35},{4,36},{5,37},{6,38},{7,39},{8,40},{9,... | collective-permute-start | bytes 491528 | tf_op jit(solution)/shard_map/ppermute | solution.py:46
  (48 shorter events, 14.3 us)
Async XLA Ops:
  6.5 8.4 %collective-permute-start.2 = (f32[2,4,8,4096]{3,2,1,0:T(8,128)S(1)}, f32[2,4,8,4096]{3,2,1,0:T(8,128)S(1)}, u32[]{:S(2)}, u32[]{:S(2)}) collective-permute-start(f32[2,4,8,4096]{3,2,1,0:T(8,128)S(1)} %get-tuple-element.31), channel_id=1, source_target_pairs={{0,32},{1,33},{2,34},{3,35},{4,36},{5,37},{6,38},{7,39},{8,40},{9,... | collective-permute-start | bytes 3145736 | tf_op jit(solution)/shard_map/ppermute | solution.py:46
  6.6 8.3 %collective-permute-start.1 = (f32[2,4,8,4096]{3,2,1,0:T(8,128)S(1)}, f32[2,4,8,4096]{3,2,1,0:T(8,128)S(1)}, u32[]{:S(2)}, u32[]{:S(2)}) collective-permute-start(f32[2,4,8,4096]{3,2,1,0:T(8,128)S(1)} %get-tuple-element.26.refs_2_), channel_id=1, source_target_pairs={{0,32},{1,33},{2,34},{3,35},{4,36},{5,37},{6,38},{7,39},{8,40},{9,... | collective-permute-start | bytes 3145736 | tf_op jit(solution)/shard_map/ppermute | solution.py:46
  7.2 10.7 %collective-permute-start.7 = (f32[2,2,8,4096]{3,2,1,0:T(8,128)S(1)}, f32[2,2,8,4096]{3,2,1,0:T(8,128)S(1)}, u32[]{:S(2)}, u32[]{:S(2)}) collective-permute-start(f32[2,2,8,4096]{3,2,1,0:T(8,128)S(1)} %get-tuple-element.39), channel_id=1, source_target_pairs={{0,3},{1,0},{2,1},{3,2},{4,7},{5,4},{6,5},{7,6},{8,11},{9,8},{10,9... | collective-permute-start | bytes 1572872 | tf_op jit(solution)/shard_map/ppermute | solution.py:46
  10.1 9.5 %collective-permute-start.6 = (f32[2,2,8,4096]{3,2,1,0:T(8,128)S(1)}, f32[2,2,8,4096]{3,2,1,0:T(8,128)S(1)}, u32[]{:S(2)}, u32[]{:S(2)}) collective-permute-start(f32[2,2,8,4096]{3,2,1,0:T(8,128)S(1)} %get-tuple-element.27.refs_3_), channel_id=1, source_target_pairs={{0,1},{1,2},{2,3},{3,0},{4,5},{5,6},{6,7},{7,4},{8,9},{9,10},{10,1... | collective-permute-start | bytes 1572872 | tf_op jit(solution)/shard_map/ppermute | solution.py:46
  13.4 19.7 %collective-permute-start.5 = (f32[2,4,8,4096]{3,2,1,0:T(8,128)S(1)}, f32[2,4,8,4096]{3,2,1,0:T(8,128)S(1)}, u32[]{:S(2)}, u32[]{:S(2)}) collective-permute-start(f32[2,4,8,4096]{3,2,1,0:T(8,128)S(1)} %get-tuple-element.36), channel_id=1, source_target_pairs={{0,32},{1,33},{2,34},{3,35},{4,36},{5,37},{6,38},{7,39},{8,40},{9,... | collective-permute-start | bytes 3145736 | tf_op jit(solution)/shard_map/ppermute | solution.py:46
  15.1 8.9 %collective-permute-start.3 = (f32[2,2,8,4096]{3,2,1,0:T(8,128)S(1)}, f32[2,2,8,4096]{3,2,1,0:T(8,128)S(1)}, u32[]{:S(2)}, u32[]{:S(2)}) collective-permute-start(f32[2,2,8,4096]{3,2,1,0:T(8,128)S(1)} %get-tuple-element.32), channel_id=1, source_target_pairs={{0,3},{1,0},{2,1},{3,2},{4,7},{5,4},{6,5},{7,6},{8,11},{9,8},{10,9... | collective-permute-start | bytes 1572872 | tf_op jit(solution)/shard_map/ppermute | solution.py:46
  17.9 9.5 %collective-permute-start.4 = (f32[2,2,8,4096]{3,2,1,0:T(8,128)S(1)}, f32[2,2,8,4096]{3,2,1,0:T(8,128)S(1)}, u32[]{:S(2)}, u32[]{:S(2)}) collective-permute-start(f32[2,2,8,4096]{3,2,1,0:T(8,128)S(1)} %get-tuple-element.33), channel_id=1, source_target_pairs={{0,1},{1,2},{2,3},{3,0},{4,5},{5,6},{6,7},{7,4},{8,9},{9,10},{10,1... | collective-permute-start | bytes 1572872 | tf_op jit(solution)/shard_map/ppermute | solution.py:46
  19.7 13.3 %collective-permute-start.8 = (f32[2,2,8,4096]{3,2,1,0:T(8,128)S(1)}, f32[2,2,8,4096]{3,2,1,0:T(8,128)S(1)}, u32[]{:S(2)}, u32[]{:S(2)}) collective-permute-start(f32[2,2,8,4096]{3,2,1,0:T(8,128)S(1)} %get-tuple-element.40), channel_id=1, source_target_pairs={{0,1},{1,2},{2,3},{3,0},{4,5},{5,6},{6,7},{7,4},{8,9},{9,10},{10,1... | collective-permute-start | bytes 1572872 | tf_op jit(solution)/shard_map/ppermute | solution.py:46
  19.8 13.2 %collective-permute-start.9 = (f32[2,2,8,4096]{3,2,1,0:T(8,128)S(1)}, f32[2,2,8,4096]{3,2,1,0:T(8,128)S(1)}, u32[]{:S(2)}, u32[]{:S(2)}) collective-permute-start(f32[2,2,8,4096]{3,2,1,0:T(8,128)S(1)} %get-tuple-element.41), channel_id=1, source_target_pairs={{0,3},{1,0},{2,1},{3,2},{4,7},{5,4},{6,5},{7,6},{8,11},{9,8},{10,9... | collective-permute-start | bytes 1572872 | tf_op jit(solution)/shard_map/ppermute | solution.py:46
  33.3 6.8 %collective-permute-start.10 = (f32[2,4,8,1024]{3,2,1,0:T(8,128)S(1)}, f32[2,4,8,1024]{3,2,1,0:T(8,128)S(1)}, u32[]{:S(2)}, u32[]{:S(2)}) collective-permute-start(f32[2,4,8,1024]{3,2,1,0:T(8,128)S(1)} %get-tuple-element.43), channel_id=1, source_target_pairs={{0,8},{1,9},{2,10},{3,11},{4,12},{5,13},{6,14},{7,15},{8,16},{9,17... | collective-permute-start | bytes 786440 | tf_op jit(solution)/shard_map/ppermute | solution.py:46
  34.6 9.3 %collective-permute-start.11 = (f32[2,4,8,1024]{3,2,1,0:T(8,128)S(1)}, f32[2,4,8,1024]{3,2,1,0:T(8,128)S(1)}, u32[]{:S(2)}, u32[]{:S(2)}) collective-permute-start(f32[2,4,8,1024]{3,2,1,0:T(8,128)S(1)} %get-tuple-element.44), channel_id=1, source_target_pairs={{0,16},{1,17},{2,18},{3,19},{4,20},{5,21},{6,22},{7,23},{8,24},{9,... | collective-permute-start | bytes 786440 | tf_op jit(solution)/shard_map/ppermute | solution.py:46
  37.0 6.9 %collective-permute-start.12 = (f32[2,4,8,1024]{3,2,1,0:T(8,128)S(1)}, f32[2,4,8,1024]{3,2,1,0:T(8,128)S(1)}, u32[]{:S(2)}, u32[]{:S(2)}) collective-permute-start(f32[2,4,8,1024]{3,2,1,0:T(8,128)S(1)} %get-tuple-element.45), channel_id=1, source_target_pairs={{0,24},{1,25},{2,26},{3,27},{4,28},{5,29},{6,30},{7,31},{8,0},{9,1... | collective-permute-start | bytes 786440 | tf_op jit(solution)/shard_map/ppermute | solution.py:46
  43.9 8.9 %collective-permute-start.15 = (f32[2,4,8,1024]{3,2,1,0:T(8,128)S(1)}, f32[2,4,8,1024]{3,2,1,0:T(8,128)S(1)}, u32[]{:S(2)}, u32[]{:S(2)}) collective-permute-start(f32[2,4,8,1024]{3,2,1,0:T(8,128)S(1)} %second_axis_sum.1.a), channel_id=1, source_target_pairs={{0,68},{1,69},{2,70},{3,71},{4,0},{5,1},{6,2},{7,3},{8,76},{9,77},... | collective-permute-start | bytes 786440 | tf_op jit(solution)/shard_map/ppermute | solution.py:46
  46.6 6.8 %collective-permute-start.14 = (f32[2,4,8,1024]{3,2,1,0:T(8,128)S(1)}, f32[2,4,8,1024]{3,2,1,0:T(8,128)S(1)}, u32[]{:S(2)}, u32[]{:S(2)}) collective-permute-start(f32[2,4,8,1024]{3,2,1,0:T(8,128)S(1)} %second_axis_sum.1.a), channel_id=1, source_target_pairs={{0,64},{1,65},{2,66},{3,67},{4,68},{5,69},{6,70},{7,71},{8,72},{9,... | collective-permute-start | bytes 786440 | tf_op jit(solution)/shard_map/ppermute | solution.py:46
  46.6 9.5 %collective-permute-start.13 = (f32[2,4,8,1024]{3,2,1,0:T(8,128)S(1)}, f32[2,4,8,1024]{3,2,1,0:T(8,128)S(1)}, u32[]{:S(2)}, u32[]{:S(2)}) collective-permute-start(f32[2,4,8,1024]{3,2,1,0:T(8,128)S(1)} %second_axis_sum.1.a), channel_id=1, source_target_pairs={{0,4},{1,5},{2,6},{3,7},{4,64},{5,65},{6,66},{7,67},{8,12},{9,13},... | collective-permute-start | bytes 786440 | tf_op jit(solution)/shard_map/ppermute | solution.py:46
  56.6 8.1 %collective-permute-start.18 = (f32[4,8,1280]{2,1,0:T(8,128)S(1)}, f32[4,8,1280]{2,1,0:T(8,128)S(1)}, u32[]{:S(2)}, u32[]{:S(2)}) collective-permute-start(f32[4,8,1280]{2,1,0:T(8,128)S(1)} %mean_and_preview.1.a.refs_0_), channel_id=1, source_target_pairs={{0,24},{1,25},{2,26},{3,27},{4,28},{5,29},{6,30},{7,31},{8,0},{9,1... | collective-permute-start | bytes 491528 | tf_op jit(solution)/shard_map/ppermute | solution.py:46
  58.7 8.7 %collective-permute-start.17 = (f32[4,8,1280]{2,1,0:T(8,128)S(1)}, f32[4,8,1280]{2,1,0:T(8,128)S(1)}, u32[]{:S(2)}, u32[]{:S(2)}) collective-permute-start(f32[4,8,1280]{2,1,0:T(8,128)S(1)} %mean_and_preview.1.a.refs_0_), channel_id=1, source_target_pairs={{0,16},{1,17},{2,18},{3,19},{4,20},{5,21},{6,22},{7,23},{8,24},{9,... | collective-permute-start | bytes 491528 | tf_op jit(solution)/shard_map/ppermute | solution.py:46
  59.4 10.2 %collective-permute-start.16 = (f32[4,8,1280]{2,1,0:T(8,128)S(1)}, f32[4,8,1280]{2,1,0:T(8,128)S(1)}, u32[]{:S(2)}, u32[]{:S(2)}) collective-permute-start(f32[4,8,1280]{2,1,0:T(8,128)S(1)} %mean_and_preview.1.a.refs_0_), channel_id=1, source_target_pairs={{0,8},{1,9},{2,10},{3,11},{4,12},{5,13},{6,14},{7,15},{8,16},{9,17... | collective-permute-start | bytes 491528 | tf_op jit(solution)/shard_map/ppermute | solution.py:46
  59.6 11.7 %collective-permute-start.19 = (f32[4,8,1280]{2,1,0:T(8,128)S(1)}, f32[4,8,1280]{2,1,0:T(8,128)S(1)}, u32[]{:S(2)}, u32[]{:S(2)}) collective-permute-start(f32[4,8,1280]{2,1,0:T(8,128)S(1)} %mean_and_preview.1.a.refs_0_), channel_id=1, source_target_pairs={{0,32},{1,33},{2,34},{3,35},{4,36},{5,37},{6,38},{7,39},{8,40},{9,... | collective-permute-start | bytes 491528 | tf_op jit(solution)/shard_map/ppermute | solution.py:46
  64.7 7.0 %collective-permute-start.22 = (f32[4,8,1280]{2,1,0:T(8,128)S(1)}, f32[4,8,1280]{2,1,0:T(8,128)S(1)}, u32[]{:S(2)}, u32[]{:S(2)}) collective-permute-start(f32[4,8,1280]{2,1,0:T(8,128)S(1)} %collective-permute-done.18.d.refs_3_), channel_id=1, source_target_pairs={{0,32},{1,33},{2,34},{3,35},{4,36},{5,37},{6,38},{7,39},{8,40},{9,... | collective-permute-start | bytes 491528 | tf_op jit(solution)/shard_map/ppermute | solution.py:46
  71.3 8.2 %collective-permute-start.23 = (f32[4,8,1280]{2,1,0:T(8,128)S(1)}, f32[4,8,1280]{2,1,0:T(8,128)S(1)}, u32[]{:S(2)}, u32[]{:S(2)}) collective-permute-start(f32[4,8,1280]{2,1,0:T(8,128)S(1)} %gathered_row.1.refs_8_), channel_id=1, source_target_pairs={{0,1},{1,2},{2,3},{3,0},{4,5},{5,6},{6,7},{7,4},{8,9},{9,10},{10,1... | collective-permute-start | bytes 491528 | tf_op jit(solution)/shard_map/ppermute | solution.py:46
  71.7 9.4 %collective-permute-start.26 = (f32[4,8,1280]{2,1,0:T(8,128)S(1)}, f32[4,8,1280]{2,1,0:T(8,128)S(1)}, u32[]{:S(2)}, u32[]{:S(2)}) collective-permute-start(f32[4,8,1280]{2,1,0:T(8,128)S(1)} %gathered_row.1.refs_8_), channel_id=1, source_target_pairs={{0,32},{1,33},{2,34},{3,35},{4,36},{5,37},{6,38},{7,39},{8,40},{9,... | collective-permute-start | bytes 491528 | tf_op jit(solution)/shard_map/ppermute | solution.py:46
  73.6 7.6 %collective-permute-start.20 = (f32[4,8,1280]{2,1,0:T(8,128)S(1)}, f32[4,8,1280]{2,1,0:T(8,128)S(1)}, u32[]{:S(2)}, u32[]{:S(2)}) collective-permute-start(f32[4,8,1280]{2,1,0:T(8,128)S(1)} %collective-permute-done.16.b.refs_1_), channel_id=1, source_target_pairs={{0,32},{1,33},{2,34},{3,35},{4,36},{5,37},{6,38},{7,39},{8,40},{9,... | collective-permute-start | bytes 491528 | tf_op jit(solution)/shard_map/ppermute | solution.py:46
  73.9 7.3 %collective-permute-start.29 = (f32[4,8,1280]{2,1,0:T(8,128)S(1)}, f32[4,8,1280]{2,1,0:T(8,128)S(1)}, u32[]{:S(2)}, u32[]{:S(2)}) collective-permute-start(f32[4,8,1280]{2,1,0:T(8,128)S(1)} %collective-permute-done.25.refs_11_), channel_id=1, source_target_pairs={{0,32},{1,33},{2,34},{3,35},{4,36},{5,37},{6,38},{7,39},{8,40},{9,... | collective-permute-start | bytes 491528 | tf_op jit(solution)/shard_map/ppermute | solution.py:46
  (6 other events, 27.7 us)

commit v5 on v4

--- a/solution.py
+++ b/solution.py
@@ -46,8 +46,17 @@
     return lax.ppermute(array, AXES, pairs)
 
 
-def _exchange(arrays, *axes):
-    got = {k: _send(arrays[k], _shift(k, *axes)) for k in (1, 3, 2)}
+def _partner(k, axis0, axis1):
+    pairs = []
+    for d in range(128):
+        at = list(_coords(d))
+        at[(axis0, axis1)[at[3]]] ^= k
+        pairs.append((d, _device(*at)))
+    return pairs
+
+
+def _exchange(arrays, axis0, axis1, pairs=_partner):
+    got = {k: _send(arrays[k], pairs(k, axis0, axis1)) for k in (1, 3, 2)}
     return [arrays[0], got[1], got[2], got[3]]
 
 
@@ -177,10 +186,9 @@
     column = lax.broadcasted_iota(jnp.int32, (512, 128), 1)
     pool = jnp.where(row // 4 == column, 0.0625, 0.0).astype(F32)
     for j in range(4):
-        out[j, :, :1024] = means[jnp.where(core == 0, j, (z + j) % 4)]
-        out[j, :, 1024:] = jnp.zeros((8, 256), F32)
+        out[:, j * 1024 : (j + 1) * 1024] = means[jnp.where(core == 0, j, z ^ j)]
     for j in range(2):
-        out[0, :, 1024 + j * 128 : 1024 + (j + 1) * 128] = jnp.dot(
+        out[:, 4096 + j * 128 : 4096 + (j + 1) * 128] = jnp.dot(
             four[:, j * 512 : (j + 1) * 512], pool, precision=lax.Precision.HIGHEST, preferred_element_type=F32
         )
 
@@ -188,7 +196,7 @@
 def _mean(parts):
     return pl.pallas_call(
         _mean_kernel,
-        out_shape=_shape(4, 8, 1280),
+        out_shape=_shape(8, 4352),
         scratch_shapes=[pltpu.VMEM((4, 8, 1024), F32)],
         compiler_params=_params(),
         cost_estimate=COST,
@@ -198,7 +206,8 @@
 
 def _row_kernel(a, b, c, d, out):
     for k, part in enumerate((a, b, c, d)):
-        out[k] = part[0]
+        out[k, :, :1024] = part[:, :1024]
+        out[k, :, 1024:] = part[:, 4096:]
 
 
 def _row(parts):
@@ -214,15 +223,13 @@
 
     def place(rows0, last0, last1):
         for k in range(4):
-            fy = (y - k) % 4
-            for j in range(4):
-                grid[pl.ds(pl.multiple_of(fy * 8, 8), 8), j * 1024 : (j + 1) * 1024] = rows0[k][j, :, :1024]
-            fz = (z - k) % 4
+            fy, fz = y ^ k, z ^ k
+            grid[pl.ds(pl.multiple_of(fy * 8, 8), 8), :] = rows0[k][:, :4096]
             for i in range(4):
                 for j in range(4):
-                    lines[fz * 8 + (y - i) % 4, :, j * 256 : (j + 1) * 256] = last0[k][i, 2 * j : 2 * j + 2, 1024:]
+                    lines[fz * 8 + (y ^ i), :, j * 256 : (j + 1) * 256] = last0[k][i, 2 * j : 2 * j + 2, 1024:]
             for i in range(4):
-                fx = (x - i) % 4
+                fx = x ^ i
                 columns = pl.ds(pl.multiple_of(fx * 1024, 1024), 1024)
                 grid[pl.ds(pl.multiple_of(32 + fy * 8, 8), 8), columns] = last1[k][i, :, :1024]
                 at = pl.ds(pl.multiple_of(fx * 256, 256), 256)
@@ -280,7 +287,7 @@
 
 def _local(p, c, n):
     arrays = [pltpu.with_memory_space_constraint(array, pltpu.HBM) for array in (p, c, n)]
-    both = _third(_exchange(_first_axis(arrays), Y, X))
+    both = _third(_exchange(_first_axis(arrays), Y, X, _shift))
     packed = _mean(_exchange([both] * 4, X, Z))
     rows = _exchange([packed] * 4, Y, X)
     last = _exchange([_row(rows)] * 4, Z, Y)

time: 83.5 us -> 80.1 us (0.959)
  starting transfers between devices: 44.5 us -> 41.9 us
    ppermute x30, starting transfers between devices: 44.5 us -> 41.9 us  [_send(): return lax.ppermute(array, AXES, pairs)]
where the time goes in v5:
time: 80.1 us; the launch traced here: 80 us
  starting transfers between devices  41.9 us (52%)
  waiting for transfers between devices  27.2 us (34%)
  Pallas kernels  10.1 us (13%)
    ppermute x30, starting transfers between devices, _send(): return lax.ppermute(array, AXES, pairs)  41.9 us
    ppermute x30, waiting for transfers between devices, _send(): return lax.ppermute(array, AXES, pairs)  27.2 us
    pallas_call x3, Pallas kernels, _blocks(): pl.pallas_call(functools.partial(_blocks_kernel, wanted), in_specs=[pl.Bl...  7.62 us
  transfers between devices with their start and end apart: 30, of which 11 were waited for; matrix products, arithmetic and copies ran while one was open for 0% of the time, Pallas kernels for 7%

profile of v5, /device:TPU:1, one launch (start us, length us, event | category | flops | bytes accessed | tf_op | source)
XLA Modules:
  0.0 80.0 jit_solution(16034916542967339809)
XLA Ops:
  0.6 2.2 %local_blocks.3 = (f32[2,4,8,4096]{3,2,1,0:T(8,128)S(1)}, f32[2,4,8,4096]{3,2,1,0:T(8,128)S(1)}) custom-call(f32[1,256,4096]{2,1,0:T(8,128)} %refs_0_.5, f32[1,256,4096]{2,1,0:T(8,128)} %refs_1_.5, f32[1,256,4096]{2,1,0:T(8,128)} %refs_2_.5), custom_call_target="tpu_custom_call" | custom-call | flops 1 | bytes 1 | tf_op jit(solution)/shard_map/local_blocks/pallas_call | solution.py:101
  2.8 1.5 %collective-permute-start = (f32[2,4,8,4096]{3,2,1,0:T(8,128)S(1)}, f32[2,4,8,4096]{3,2,1,0:T(8,128)S(1)}, u32[]{:S(2)}, u32[]{:S(2)}) collective-permute-start(f32[2,4,8,4096]{3,2,1,0:T(8,128)S(1)} %get-tuple-element.25), channel_id=1, source_target_pairs={{0,32},{1,33},{2,34},{3,35},{4,36},{5,37},{6,38},{7,39},{8,40},{9,... | collective-permute-start | bytes 3145736 | tf_op jit(solution)/shard_map/ppermute | solution.py:46
  4.3 2.1 %local_blocks.4 = (f32[2,4,8,4096]{3,2,1,0:T(8,128)S(1)}, f32[2,4,8,4096]{3,2,1,0:T(8,128)S(1)}) custom-call(f32[1,256,4096]{2,1,0:T(8,128)} %refs_0_.5, f32[1,256,4096]{2,1,0:T(8,128)} %refs_1_.5, f32[1,256,4096]{2,1,0:T(8,128)} %refs_2_.5, f32[2,4,8,4096]{3,2,1,0:T(8,128)S(1)} %get-tuple-element.24.refs_3_.refs_0_), custom_call_target="tpu_custom_call" | custom-call | flops 1 | bytes 1 | tf_op jit(solution)/shard_map/local_blocks/pallas_call | solution.py:101
  7.2 2.9 %collective-permute-start.7 = (f32[2,2,8,4096]{3,2,1,0:T(8,128)S(1)}, f32[2,2,8,4096]{3,2,1,0:T(8,128)S(1)}, u32[]{:S(2)}, u32[]{:S(2)}) collective-permute-start(f32[2,2,8,4096]{3,2,1,0:T(8,128)S(1)} %get-tuple-element.39), channel_id=1, source_target_pairs={{0,3},{1,0},{2,1},{3,2},{4,7},{5,4},{6,5},{7,6},{8,11},{9,8},{10,9... | collective-permute-start | bytes 1572872 | tf_op jit(solution)/shard_map/ppermute | solution.py:46
  10.1 3.3 %local_blocks.5 = (f32[2,4,8,4096]{3,2,1,0:T(8,128)S(1)}, f32[2,4,8,4096]{3,2,1,0:T(8,128)S(1)}, f32[2,4,8,4096]{3,2,1,0:T(8,128)S(1)}, f32[2,4,8,4096]{3,2,1,0:T(8,128)S(1)}) custom-call(f32[1,256,4096]{2,1,0:T(8,128)} %refs_0_.5, f32[1,256,4096]{2,1,0:T(8,128)} %refs_1_.5, f32[1,256,4096]{2,1,0:T(8,128)} %refs_2_.5, ...), custom_call_target="tpu_custom_call" | custom-call | flops 1 | bytes 1 | tf_op jit(solution)/shard_map/local_blocks/pallas_call | solution.py:101
  13.4 1.5 %collective-permute-start.5 = (f32[2,4,8,4096]{3,2,1,0:T(8,128)S(1)}, f32[2,4,8,4096]{3,2,1,0:T(8,128)S(1)}, u32[]{:S(2)}, u32[]{:S(2)}) collective-permute-start(f32[2,4,8,4096]{3,2,1,0:T(8,128)S(1)} %get-tuple-element.36), channel_id=1, source_target_pairs={{0,32},{1,33},{2,34},{3,35},{4,36},{5,37},{6,38},{7,39},{8,40},{9,... | collective-permute-start | bytes 3145736 | tf_op jit(solution)/shard_map/ppermute | solution.py:46
  15.1 2.8 %collective-permute-start.3 = (f32[2,2,8,4096]{3,2,1,0:T(8,128)S(1)}, f32[2,2,8,4096]{3,2,1,0:T(8,128)S(1)}, u32[]{:S(2)}, u32[]{:S(2)}) collective-permute-start(f32[2,2,8,4096]{3,2,1,0:T(8,128)S(1)} %get-tuple-element.32), channel_id=1, source_target_pairs={{0,3},{1,0},{2,1},{3,2},{4,7},{5,4},{6,5},{7,6},{8,11},{9,8},{10,9... | collective-permute-start | bytes 1572872 | tf_op jit(solution)/shard_map/ppermute | solution.py:46
  17.9 1.7 %collective-permute-done.6.refs_1_ = f32[2,2,8,4096]{3,2,1,0:T(8,128)S(1)} collective-permute-done((f32[2,2,8,4096]{3,2,1,0:T(8,128)S(1)}, f32[2,2,8,4096]{3,2,1,0:T(8,128)S(1)}, u32[]{:S(2)}, u32[]{:S(2)}) %collective-permute-start.6) | collective-permute-done | bytes 524320 | tf_op jit(solution)/shard_map/ppermute | solution.py:46
  19.8 2.7 %collective-permute-start.9 = (f32[2,2,8,4096]{3,2,1,0:T(8,128)S(1)}, f32[2,2,8,4096]{3,2,1,0:T(8,128)S(1)}, u32[]{:S(2)}, u32[]{:S(2)}) collective-permute-start(f32[2,2,8,4096]{3,2,1,0:T(8,128)S(1)} %get-tuple-element.41), channel_id=1, source_target_pairs={{0,3},{1,0},{2,1},{3,2},{4,7},{5,4},{6,5},{7,6},{8,11},{9,8},{10,9... | collective-permute-start | bytes 1572872 | tf_op jit(solution)/shard_map/ppermute | solution.py:46
  22.5 1.5 %collective-permute-done.3.refs_1_ = f32[2,2,8,4096]{3,2,1,0:T(8,128)S(1)} collective-permute-done((f32[2,2,8,4096]{3,2,1,0:T(8,128)S(1)}, f32[2,2,8,4096]{3,2,1,0:T(8,128)S(1)}, u32[]{:S(2)}, u32[]{:S(2)}) %collective-permute-start.3) | collective-permute-done | bytes 524320 | tf_op jit(solution)/shard_map/ppermute | solution.py:46
  24.0 3.4 %collective-permute-done.4.refs_2_ = f32[2,2,8,4096]{3,2,1,0:T(8,128)S(1)} collective-permute-done((f32[2,2,8,4096]{3,2,1,0:T(8,128)S(1)}, f32[2,2,8,4096]{3,2,1,0:T(8,128)S(1)}, u32[]{:S(2)}, u32[]{:S(2)}) %collective-permute-start.4) | collective-permute-done | bytes 524320 | tf_op jit(solution)/shard_map/ppermute | solution.py:46
  27.5 5.5 %collective-permute-done.8.low1 = f32[2,2,8,4096]{3,2,1,0:T(8,128)S(1)} collective-permute-done((f32[2,2,8,4096]{3,2,1,0:T(8,128)S(1)}, f32[2,2,8,4096]{3,2,1,0:T(8,128)S(1)}, u32[]{:S(2)}, u32[]{:S(2)}) %collective-permute-start.8) | collective-permute-done | bytes 524320 | tf_op jit(solution)/shard_map/ppermute | solution.py:46
  34.6 2.5 %collective-permute-start.11 = (f32[2,4,8,1024]{3,2,1,0:T(8,128)S(1)}, f32[2,4,8,1024]{3,2,1,0:T(8,128)S(1)}, u32[]{:S(2)}, u32[]{:S(2)}) collective-permute-start(f32[2,4,8,1024]{3,2,1,0:T(8,128)S(1)} %get-tuple-element.44), channel_id=1, source_target_pairs={{0,16},{1,17},{2,18},{3,19},{4,20},{5,21},{6,22},{7,23},{8,24},{9,... | collective-permute-start | bytes 786440 | tf_op jit(solution)/shard_map/ppermute | solution.py:46
  38.2 1.9 %collective-permute-done.10.b = f32[2,4,8,1024]{3,2,1,0:T(8,128)S(1)} collective-permute-done((f32[2,4,8,1024]{3,2,1,0:T(8,128)S(1)}, f32[2,4,8,1024]{3,2,1,0:T(8,128)S(1)}, u32[]{:S(2)}, u32[]{:S(2)}) %collective-permute-start.10) | collective-permute-done | bytes 262176 | tf_op jit(solution)/shard_map/ppermute | solution.py:46
  40.1 3.8 %collective-permute-done.11.c = f32[2,4,8,1024]{3,2,1,0:T(8,128)S(1)} collective-permute-done((f32[2,4,8,1024]{3,2,1,0:T(8,128)S(1)}, f32[2,4,8,1024]{3,2,1,0:T(8,128)S(1)}, u32[]{:S(2)}, u32[]{:S(2)}) %collective-permute-start.11) | collective-permute-done | bytes 262176 | tf_op jit(solution)/shard_map/ppermute | solution.py:46
  43.9 2.7 %collective-permute-start.15 = (f32[2,4,8,1024]{3,2,1,0:T(8,128)S(1)}, f32[2,4,8,1024]{3,2,1,0:T(8,128)S(1)}, u32[]{:S(2)}, u32[]{:S(2)}) collective-permute-start(f32[2,4,8,1024]{3,2,1,0:T(8,128)S(1)} %second_axis_sum.1.a), channel_id=1, source_target_pairs={{0,68},{1,69},{2,70},{3,71},{4,64},{5,65},{6,66},{7,67},{8,76},{9,... | collective-permute-start | bytes 786440 | tf_op jit(solution)/shard_map/ppermute | solution.py:46
  47.3 5.5 %collective-permute-done.15.d = f32[2,4,8,1024]{3,2,1,0:T(8,128)S(1)} collective-permute-done((f32[2,4,8,1024]{3,2,1,0:T(8,128)S(1)}, f32[2,4,8,1024]{3,2,1,0:T(8,128)S(1)}, u32[]{:S(2)}, u32[]{:S(2)}) %collective-permute-start.15) | collective-permute-done | bytes 262176 | tf_op jit(solution)/shard_map/ppermute | solution.py:46
  54.7 2.1 %collective-permute-start.18 = (f32[8,4352]{1,0:T(8,128)S(1)}, f32[8,4352]{1,0:T(8,128)S(1)}, u32[]{:S(2)}, u32[]{:S(2)}) collective-permute-start(f32[8,4352]{1,0:T(8,128)S(1)} %mean_and_preview.1.a.refs_0_), channel_id=1, source_target_pairs={{0,24},{1,25},{2,26},{3,27},{4,28},{5,29},{6,30},{7,31},{8,16},{9,... | collective-permute-start | bytes 417800 | tf_op jit(solution)/shard_map/ppermute | solution.py:46
  58.0 5.0 %collective-permute-start.19 = (f32[8,4352]{1,0:T(8,128)S(1)}, f32[8,4352]{1,0:T(8,128)S(1)}, u32[]{:S(2)}, u32[]{:S(2)}) collective-permute-start(f32[8,4352]{1,0:T(8,128)S(1)} %mean_and_preview.1.a.refs_0_), channel_id=1, source_target_pairs={{0,32},{1,33},{2,34},{3,35},{4,36},{5,37},{6,38},{7,39},{8,40},{9,... | collective-permute-start | bytes 417800 | tf_op jit(solution)/shard_map/ppermute | solution.py:46
  63.1 2.3 %collective-permute-start.25 = (f32[4,8,1280]{2,1,0:T(8,128)S(1)}, f32[4,8,1280]{2,1,0:T(8,128)S(1)}, u32[]{:S(2)}, u32[]{:S(2)}) collective-permute-start(f32[4,8,1280]{2,1,0:T(8,128)S(1)} %gathered_row.1.refs_8_), channel_id=1, source_target_pairs={{0,3},{1,2},{2,1},{3,0},{4,7},{5,6},{6,5},{7,4},{8,11},{9,10},{10,... | collective-permute-start | bytes 491528 | tf_op jit(solution)/shard_map/ppermute | solution.py:46
  65.4 1.6 %collective-permute-start.24 = (f32[4,8,1280]{2,1,0:T(8,128)S(1)}, f32[4,8,1280]{2,1,0:T(8,128)S(1)}, u32[]{:S(2)}, u32[]{:S(2)}) collective-permute-start(f32[4,8,1280]{2,1,0:T(8,128)S(1)} %gathered_row.1.refs_8_), channel_id=1, source_target_pairs={{0,2},{1,3},{2,0},{3,1},{4,6},{5,7},{6,4},{7,5},{8,10},{9,11},{10,... | collective-permute-start | bytes 491528 | tf_op jit(solution)/shard_map/ppermute | solution.py:46
  67.0 5.3 %collective-permute-start.22 = (f32[8,4352]{1,0:T(8,128)S(1)}, f32[8,4352]{1,0:T(8,128)S(1)}, u32[]{:S(2)}, u32[]{:S(2)}) collective-permute-start(f32[8,4352]{1,0:T(8,128)S(1)} %collective-permute-done.18.d.refs_3_), channel_id=1, source_target_pairs={{0,32},{1,33},{2,34},{3,35},{4,36},{5,37},{6,38},{7,39},{8,40},{9,... | collective-permute-start | bytes 417800 | tf_op jit(solution)/shard_map/ppermute | solution.py:46
  73.6 2.8 %collective-permute-start.29 = (f32[4,8,1280]{2,1,0:T(8,128)S(1)}, f32[4,8,1280]{2,1,0:T(8,128)S(1)}, u32[]{:S(2)}, u32[]{:S(2)}) collective-permute-start(f32[4,8,1280]{2,1,0:T(8,128)S(1)} %collective-permute-done.25.refs_11_), channel_id=1, source_target_pairs={{0,32},{1,33},{2,34},{3,35},{4,36},{5,37},{6,38},{7,39},{8,40},{9,... | collective-permute-start | bytes 491528 | tf_op jit(solution)/shard_map/ppermute | solution.py:46
  77.3 1.4 %collective-permute-done.20.refs_5_ = f32[8,4352]{1,0:T(8,128)S(1)} collective-permute-done((f32[8,4352]{1,0:T(8,128)S(1)}, f32[8,4352]{1,0:T(8,128)S(1)}, u32[]{:S(2)}, u32[]{:S(2)}) %collective-permute-start.20) | collective-permute-done | bytes 139296 | tf_op jit(solution)/shard_map/ppermute | solution.py:46
  (48 shorter events, 11.3 us)
Async XLA Ops:
  6.5 8.4 %collective-permute-start.2 = (f32[2,4,8,4096]{3,2,1,0:T(8,128)S(1)}, f32[2,4,8,4096]{3,2,1,0:T(8,128)S(1)}, u32[]{:S(2)}, u32[]{:S(2)}) collective-permute-start(f32[2,4,8,4096]{3,2,1,0:T(8,128)S(1)} %get-tuple-element.31), channel_id=1, source_target_pairs={{0,32},{1,33},{2,34},{3,35},{4,36},{5,37},{6,38},{7,39},{8,40},{9,... | collective-permute-start | bytes 3145736 | tf_op jit(solution)/shard_map/ppermute | solution.py:46
  6.6 8.3 %collective-permute-start.1 = (f32[2,4,8,4096]{3,2,1,0:T(8,128)S(1)}, f32[2,4,8,4096]{3,2,1,0:T(8,128)S(1)}, u32[]{:S(2)}, u32[]{:S(2)}) collective-permute-start(f32[2,4,8,4096]{3,2,1,0:T(8,128)S(1)} %get-tuple-element.26.refs_2_), channel_id=1, source_target_pairs={{0,32},{1,33},{2,34},{3,35},{4,36},{5,37},{6,38},{7,39},{8,40},{9,... | collective-permute-start | bytes 3145736 | tf_op jit(solution)/shard_map/ppermute | solution.py:46
  7.2 10.7 %collective-permute-start.7 = (f32[2,2,8,4096]{3,2,1,0:T(8,128)S(1)}, f32[2,2,8,4096]{3,2,1,0:T(8,128)S(1)}, u32[]{:S(2)}, u32[]{:S(2)}) collective-permute-start(f32[2,2,8,4096]{3,2,1,0:T(8,128)S(1)} %get-tuple-element.39), channel_id=1, source_target_pairs={{0,3},{1,0},{2,1},{3,2},{4,7},{5,4},{6,5},{7,6},{8,11},{9,8},{10,9... | collective-permute-start | bytes 1572872 | tf_op jit(solution)/shard_map/ppermute | solution.py:46
  10.1 9.5 %collective-permute-start.6 = (f32[2,2,8,4096]{3,2,1,0:T(8,128)S(1)}, f32[2,2,8,4096]{3,2,1,0:T(8,128)S(1)}, u32[]{:S(2)}, u32[]{:S(2)}) collective-permute-start(f32[2,2,8,4096]{3,2,1,0:T(8,128)S(1)} %get-tuple-element.27.refs_3_), channel_id=1, source_target_pairs={{0,1},{1,2},{2,3},{3,0},{4,5},{5,6},{6,7},{7,4},{8,9},{9,10},{10,1... | collective-permute-start | bytes 1572872 | tf_op jit(solution)/shard_map/ppermute | solution.py:46
  13.4 19.7 %collective-permute-start.5 = (f32[2,4,8,4096]{3,2,1,0:T(8,128)S(1)}, f32[2,4,8,4096]{3,2,1,0:T(8,128)S(1)}, u32[]{:S(2)}, u32[]{:S(2)}) collective-permute-start(f32[2,4,8,4096]{3,2,1,0:T(8,128)S(1)} %get-tuple-element.36), channel_id=1, source_target_pairs={{0,32},{1,33},{2,34},{3,35},{4,36},{5,37},{6,38},{7,39},{8,40},{9,... | collective-permute-start | bytes 3145736 | tf_op jit(solution)/shard_map/ppermute | solution.py:46
  15.1 8.9 %collective-permute-start.3 = (f32[2,2,8,4096]{3,2,1,0:T(8,128)S(1)}, f32[2,2,8,4096]{3,2,1,0:T(8,128)S(1)}, u32[]{:S(2)}, u32[]{:S(2)}) collective-permute-start(f32[2,2,8,4096]{3,2,1,0:T(8,128)S(1)} %get-tuple-element.32), channel_id=1, source_target_pairs={{0,3},{1,0},{2,1},{3,2},{4,7},{5,4},{6,5},{7,6},{8,11},{9,8},{10,9... | collective-permute-start | bytes 1572872 | tf_op jit(solution)/shard_map/ppermute | solution.py:46
  17.9 9.5 %collective-permute-start.4 = (f32[2,2,8,4096]{3,2,1,0:T(8,128)S(1)}, f32[2,2,8,4096]{3,2,1,0:T(8,128)S(1)}, u32[]{:S(2)}, u32[]{:S(2)}) collective-permute-start(f32[2,2,8,4096]{3,2,1,0:T(8,128)S(1)} %get-tuple-element.33), channel_id=1, source_target_pairs={{0,1},{1,2},{2,3},{3,0},{4,5},{5,6},{6,7},{7,4},{8,9},{9,10},{10,1... | collective-permute-start | bytes 1572872 | tf_op jit(solution)/shard_map/ppermute | solution.py:46
  19.7 13.3 %collective-permute-start.8 = (f32[2,2,8,4096]{3,2,1,0:T(8,128)S(1)}, f32[2,2,8,4096]{3,2,1,0:T(8,128)S(1)}, u32[]{:S(2)}, u32[]{:S(2)}) collective-permute-start(f32[2,2,8,4096]{3,2,1,0:T(8,128)S(1)} %get-tuple-element.40), channel_id=1, source_target_pairs={{0,1},{1,2},{2,3},{3,0},{4,5},{5,6},{6,7},{7,4},{8,9},{9,10},{10,1... | collective-permute-start | bytes 1572872 | tf_op jit(solution)/shard_map/ppermute | solution.py:46
  19.8 13.2 %collective-permute-start.9 = (f32[2,2,8,4096]{3,2,1,0:T(8,128)S(1)}, f32[2,2,8,4096]{3,2,1,0:T(8,128)S(1)}, u32[]{:S(2)}, u32[]{:S(2)}) collective-permute-start(f32[2,2,8,4096]{3,2,1,0:T(8,128)S(1)} %get-tuple-element.41), channel_id=1, source_target_pairs={{0,3},{1,0},{2,1},{3,2},{4,7},{5,4},{6,5},{7,6},{8,11},{9,8},{10,9... | collective-permute-start | bytes 1572872 | tf_op jit(solution)/shard_map/ppermute | solution.py:46
  33.3 6.8 %collective-permute-start.10 = (f32[2,4,8,1024]{3,2,1,0:T(8,128)S(1)}, f32[2,4,8,1024]{3,2,1,0:T(8,128)S(1)}, u32[]{:S(2)}, u32[]{:S(2)}) collective-permute-start(f32[2,4,8,1024]{3,2,1,0:T(8,128)S(1)} %get-tuple-element.43), channel_id=1, source_target_pairs={{0,8},{1,9},{2,10},{3,11},{4,12},{5,13},{6,14},{7,15},{8,16},{9,17... | collective-permute-start | bytes 786440 | tf_op jit(solution)/shard_map/ppermute | solution.py:46
  34.6 9.3 %collective-permute-start.11 = (f32[2,4,8,1024]{3,2,1,0:T(8,128)S(1)}, f32[2,4,8,1024]{3,2,1,0:T(8,128)S(1)}, u32[]{:S(2)}, u32[]{:S(2)}) collective-permute-start(f32[2,4,8,1024]{3,2,1,0:T(8,128)S(1)} %get-tuple-element.44), channel_id=1, source_target_pairs={{0,16},{1,17},{2,18},{3,19},{4,20},{5,21},{6,22},{7,23},{8,24},{9,... | collective-permute-start | bytes 786440 | tf_op jit(solution)/shard_map/ppermute | solution.py:46
  37.0 6.9 %collective-permute-start.12 = (f32[2,4,8,1024]{3,2,1,0:T(8,128)S(1)}, f32[2,4,8,1024]{3,2,1,0:T(8,128)S(1)}, u32[]{:S(2)}, u32[]{:S(2)}) collective-permute-start(f32[2,4,8,1024]{3,2,1,0:T(8,128)S(1)} %get-tuple-element.45), channel_id=1, source_target_pairs={{0,24},{1,25},{2,26},{3,27},{4,28},{5,29},{6,30},{7,31},{8,0},{9,1... | collective-permute-start | bytes 786440 | tf_op jit(solution)/shard_map/ppermute | solution.py:46
  43.9 8.9 %collective-permute-start.15 = (f32[2,4,8,1024]{3,2,1,0:T(8,128)S(1)}, f32[2,4,8,1024]{3,2,1,0:T(8,128)S(1)}, u32[]{:S(2)}, u32[]{:S(2)}) collective-permute-start(f32[2,4,8,1024]{3,2,1,0:T(8,128)S(1)} %second_axis_sum.1.a), channel_id=1, source_target_pairs={{0,68},{1,69},{2,70},{3,71},{4,64},{5,65},{6,66},{7,67},{8,76},{9,... | collective-permute-start | bytes 786440 | tf_op jit(solution)/shard_map/ppermute | solution.py:46
  46.7 6.7 %collective-permute-start.14 = (f32[2,4,8,1024]{3,2,1,0:T(8,128)S(1)}, f32[2,4,8,1024]{3,2,1,0:T(8,128)S(1)}, u32[]{:S(2)}, u32[]{:S(2)}) collective-permute-start(f32[2,4,8,1024]{3,2,1,0:T(8,128)S(1)} %second_axis_sum.1.a), channel_id=1, source_target_pairs={{0,64},{1,65},{2,66},{3,67},{4,68},{5,69},{6,70},{7,71},{8,72},{9,... | collective-permute-start | bytes 786440 | tf_op jit(solution)/shard_map/ppermute | solution.py:46
  46.7 7.6 %collective-permute-start.13 = (f32[2,4,8,1024]{3,2,1,0:T(8,128)S(1)}, f32[2,4,8,1024]{3,2,1,0:T(8,128)S(1)}, u32[]{:S(2)}, u32[]{:S(2)}) collective-permute-start(f32[2,4,8,1024]{3,2,1,0:T(8,128)S(1)} %second_axis_sum.1.a), channel_id=1, source_target_pairs={{0,4},{1,5},{2,6},{3,7},{4,0},{5,1},{6,2},{7,3},{8,12},{9,13},{10,... | collective-permute-start | bytes 786440 | tf_op jit(solution)/shard_map/ppermute | solution.py:46
  54.7 8.4 %collective-permute-start.18 = (f32[8,4352]{1,0:T(8,128)S(1)}, f32[8,4352]{1,0:T(8,128)S(1)}, u32[]{:S(2)}, u32[]{:S(2)}) collective-permute-start(f32[8,4352]{1,0:T(8,128)S(1)} %mean_and_preview.1.a.refs_0_), channel_id=1, source_target_pairs={{0,24},{1,25},{2,26},{3,27},{4,28},{5,29},{6,30},{7,31},{8,16},{9,... | collective-permute-start | bytes 417800 | tf_op jit(solution)/shard_map/ppermute | solution.py:46
  56.7 6.3 %collective-permute-start.17 = (f32[8,4352]{1,0:T(8,128)S(1)}, f32[8,4352]{1,0:T(8,128)S(1)}, u32[]{:S(2)}, u32[]{:S(2)}) collective-permute-start(f32[8,4352]{1,0:T(8,128)S(1)} %mean_and_preview.1.a.refs_0_), channel_id=1, source_target_pairs={{0,16},{1,17},{2,18},{3,19},{4,20},{5,21},{6,22},{7,23},{8,24},{9,... | collective-permute-start | bytes 417800 | tf_op jit(solution)/shard_map/ppermute | solution.py:46
  57.6 5.5 %collective-permute-start.16 = (f32[8,4352]{1,0:T(8,128)S(1)}, f32[8,4352]{1,0:T(8,128)S(1)}, u32[]{:S(2)}, u32[]{:S(2)}) collective-permute-start(f32[8,4352]{1,0:T(8,128)S(1)} %mean_and_preview.1.a.refs_0_), channel_id=1, source_target_pairs={{0,8},{1,9},{2,10},{3,11},{4,12},{5,13},{6,14},{7,15},{8,0},{9,1},... | collective-permute-start | bytes 417800 | tf_op jit(solution)/shard_map/ppermute | solution.py:46
  58.0 14.3 %collective-permute-start.19 = (f32[8,4352]{1,0:T(8,128)S(1)}, f32[8,4352]{1,0:T(8,128)S(1)}, u32[]{:S(2)}, u32[]{:S(2)}) collective-permute-start(f32[8,4352]{1,0:T(8,128)S(1)} %mean_and_preview.1.a.refs_0_), channel_id=1, source_target_pairs={{0,32},{1,33},{2,34},{3,35},{4,36},{5,37},{6,38},{7,39},{8,40},{9,... | collective-permute-start | bytes 417800 | tf_op jit(solution)/shard_map/ppermute | solution.py:46
  63.1 10.6 %collective-permute-start.25 = (f32[4,8,1280]{2,1,0:T(8,128)S(1)}, f32[4,8,1280]{2,1,0:T(8,128)S(1)}, u32[]{:S(2)}, u32[]{:S(2)}) collective-permute-start(f32[4,8,1280]{2,1,0:T(8,128)S(1)} %gathered_row.1.refs_8_), channel_id=1, source_target_pairs={{0,3},{1,2},{2,1},{3,0},{4,7},{5,6},{6,5},{7,4},{8,11},{9,10},{10,... | collective-permute-start | bytes 491528 | tf_op jit(solution)/shard_map/ppermute | solution.py:46
  65.4 11.1 %collective-permute-start.24 = (f32[4,8,1280]{2,1,0:T(8,128)S(1)}, f32[4,8,1280]{2,1,0:T(8,128)S(1)}, u32[]{:S(2)}, u32[]{:S(2)}) collective-permute-start(f32[4,8,1280]{2,1,0:T(8,128)S(1)} %gathered_row.1.refs_8_), channel_id=1, source_target_pairs={{0,2},{1,3},{2,0},{3,1},{4,6},{5,7},{6,4},{7,5},{8,10},{9,11},{10,... | collective-permute-start | bytes 491528 | tf_op jit(solution)/shard_map/ppermute | solution.py:46
  67.0 9.5 %collective-permute-start.23 = (f32[4,8,1280]{2,1,0:T(8,128)S(1)}, f32[4,8,1280]{2,1,0:T(8,128)S(1)}, u32[]{:S(2)}, u32[]{:S(2)}) collective-permute-start(f32[4,8,1280]{2,1,0:T(8,128)S(1)} %gathered_row.1.refs_8_), channel_id=1, source_target_pairs={{0,1},{1,0},{2,3},{3,2},{4,5},{5,4},{6,7},{7,6},{8,9},{9,8},{10,11... | collective-permute-start | bytes 491528 | tf_op jit(solution)/shard_map/ppermute | solution.py:46
  67.0 6.3 %collective-permute-start.22 = (f32[8,4352]{1,0:T(8,128)S(1)}, f32[8,4352]{1,0:T(8,128)S(1)}, u32[]{:S(2)}, u32[]{:S(2)}) collective-permute-start(f32[8,4352]{1,0:T(8,128)S(1)} %collective-permute-done.18.d.refs_3_), channel_id=1, source_target_pairs={{0,32},{1,33},{2,34},{3,35},{4,36},{5,37},{6,38},{7,39},{8,40},{9,... | collective-permute-start | bytes 417800 | tf_op jit(solution)/shard_map/ppermute | solution.py:46
  73.3 5.4 %collective-permute-start.26 = (f32[4,8,1280]{2,1,0:T(8,128)S(1)}, f32[4,8,1280]{2,1,0:T(8,128)S(1)}, u32[]{:S(2)}, u32[]{:S(2)}) collective-permute-start(f32[4,8,1280]{2,1,0:T(8,128)S(1)} %gathered_row.1.refs_8_), channel_id=1, source_target_pairs={{0,32},{1,33},{2,34},{3,35},{4,36},{5,37},{6,38},{7,39},{8,40},{9,... | collective-permute-start | bytes 491528 | tf_op jit(solution)/shard_map/ppermute | solution.py:46
  (6 other events, 20.2 us)

commit v6 on v5

--- a/solution.py
+++ b/solution.py
@@ -83,7 +83,7 @@
     copies = []
     for j, (k, own) in enumerate(wanted):
         core = me if own else 1 - me
-        a = (jnp.where(core == 0, z, y) + k) % 4
+        a = jnp.where(core == 0, z, y) ^ k
         for b in range(4):
             rows = pl.ds(pl.multiple_of(jnp.where(core == 0, a * 8 + b, b * 8 + 4 + a) * 8, 8), 8)
             for i, array in enumerate((p, c, n)):
@@ -260,14 +260,14 @@
 
 
 def _first_axis(arrays):
-    up, down = _shift(1, Z, Y), _shift(3, Z, Y)
+    near, far = _partner(1, Z, Y), _partner(3, Z, Y)
     whole = slice(None)
     sent2, own2 = _blocks(arrays, ((2, False), (2, True)))
     got2 = _send(sent2, _SIBLING)
     sent1, sent3 = _blocks(arrays, ((1, False), (3, False)), (own2,))
     got1, got3 = _send(sent1, _SIBLING), _send(sent3, _SIBLING)
     low2, high2 = _sums((own2, got2), [[(0, LOW), (1, LOW)], [(0, HIGH), (1, HIGH)]], "opposite_pair", (sent1,))
-    low, high = _send(low2, up), _send(high2, down)
+    low, high = _send(low2, near), _send(high2, far)
     own1, own3, sent0, own0 = _blocks(arrays, ((1, True), (3, True), (0, False), (0, True)), (low2,))
     low1, high1, low3, high3 = _sums(
         (own1, got1, own3, got3),
@@ -275,14 +275,14 @@
         "neighbour_pairs",
     )
     got0 = _send(sent0, _SIBLING)
-    high1, low3 = _send(high1, up), _send(low3, down)
-    low1, high3 = _sums((low1, low, high3, high), [[(0, whole), (1, whole)], [(2, whole), (3, whole)]], "passed_on")
+    low1, high3 = _send(low1, near), _send(high3, far)
+    low3, high1 = _sums((low3, low, high1, high), [[(0, whole), (1, whole)], [(2, whole), (3, whole)]], "passed_on")
     low, high = _sums(
-        (own0, low3, high1),
+        (own0, low1, high3),
         [[(0, LOW), (1, whole)], [(0, HIGH), (2, whole)]],
         "early_sum",
     )
-    return _second(low, high, got0, _send(low1, up), _send(high3, down))
+    return _second(low, high, got0, _send(low3, far), _send(high1, near))
 
 
 def _local(p, c, n):

time: 80.1 us -> 78.3 us (0.978)
  starting transfers between devices: 41.9 us -> 40.5 us
    ppermute x30, starting transfers between devices: 41.9 us -> 40.5 us  [_send(): return lax.ppermute(array, AXES, pairs)]
  transfers between devices with their start and end apart: 30 -> 30, of which waited for: 11 -> 9; matrix products, arithmetic and copies ran while one was open for 0% -> 0% of each run, Pallas kernels for 7% -> 8%
where the time goes in v6:
time: 78.3 us; the launch traced here: 78.1 us
  starting transfers between devices  40.5 us (52%)
  waiting for transfers between devices  26.7 us (34%)
  Pallas kernels  10.1 us (13%)
    ppermute x30, starting transfers between devices, _send(): return lax.ppermute(array, AXES, pairs)  40.5 us
    ppermute x30, waiting for transfers between devices, _send(): return lax.ppermute(array, AXES, pairs)  26.7 us
    pallas_call x3, Pallas kernels, _blocks(): pl.pallas_call(functools.partial(_blocks_kernel, wanted), in_specs=[pl.Bl...  7.61 us
  transfers between devices with their start and end apart: 30, of which 9 were waited for; matrix products, arithmetic and copies ran while one was open for 0% of the time, Pallas kernels for 8%

profile of v6, /device:TPU:1, one launch (start us, length us, event | category | flops | bytes accessed | tf_op | source)
XLA Modules:
  0.0 78.1 jit_solution(18108733531310715292)
XLA Ops:
  0.6 2.2 %local_blocks.3 = (f32[2,4,8,4096]{3,2,1,0:T(8,128)S(1)}, f32[2,4,8,4096]{3,2,1,0:T(8,128)S(1)}) custom-call(f32[1,256,4096]{2,1,0:T(8,128)} %refs_0_.5, f32[1,256,4096]{2,1,0:T(8,128)} %refs_1_.5, f32[1,256,4096]{2,1,0:T(8,128)} %refs_2_.5), custom_call_target="tpu_custom_call" | custom-call | flops 1 | bytes 1 | tf_op jit(solution)/shard_map/local_blocks/pallas_call | solution.py:101
  2.8 1.5 %collective-permute-start = (f32[2,4,8,4096]{3,2,1,0:T(8,128)S(1)}, f32[2,4,8,4096]{3,2,1,0:T(8,128)S(1)}, u32[]{:S(2)}, u32[]{:S(2)}) collective-permute-start(f32[2,4,8,4096]{3,2,1,0:T(8,128)S(1)} %get-tuple-element.25), channel_id=1, source_target_pairs={{0,32},{1,33},{2,34},{3,35},{4,36},{5,37},{6,38},{7,39},{8,40},{9,... | collective-permute-start | bytes 3145736 | tf_op jit(solution)/shard_map/ppermute | solution.py:46
  4.3 2.1 %local_blocks.4 = (f32[2,4,8,4096]{3,2,1,0:T(8,128)S(1)}, f32[2,4,8,4096]{3,2,1,0:T(8,128)S(1)}) custom-call(f32[1,256,4096]{2,1,0:T(8,128)} %refs_0_.5, f32[1,256,4096]{2,1,0:T(8,128)} %refs_1_.5, f32[1,256,4096]{2,1,0:T(8,128)} %refs_2_.5, f32[2,4,8,4096]{3,2,1,0:T(8,128)S(1)} %get-tuple-element.24.refs_3_.refs_0_), custom_call_target="tpu_custom_call" | custom-call | flops 1 | bytes 1 | tf_op jit(solution)/shard_map/local_blocks/pallas_call | solution.py:101
  7.2 2.9 %collective-permute-start.7 = (f32[2,2,8,4096]{3,2,1,0:T(8,128)S(1)}, f32[2,2,8,4096]{3,2,1,0:T(8,128)S(1)}, u32[]{:S(2)}, u32[]{:S(2)}) collective-permute-start(f32[2,2,8,4096]{3,2,1,0:T(8,128)S(1)} %get-tuple-element.39), channel_id=1, source_target_pairs={{0,3},{1,2},{2,1},{3,0},{4,7},{5,6},{6,5},{7,4},{8,11},{9,10},{10,... | collective-permute-start | bytes 1572872 | tf_op jit(solution)/shard_map/ppermute | solution.py:46
  10.1 3.3 %local_blocks.5 = (f32[2,4,8,4096]{3,2,1,0:T(8,128)S(1)}, f32[2,4,8,4096]{3,2,1,0:T(8,128)S(1)}, f32[2,4,8,4096]{3,2,1,0:T(8,128)S(1)}, f32[2,4,8,4096]{3,2,1,0:T(8,128)S(1)}) custom-call(f32[1,256,4096]{2,1,0:T(8,128)} %refs_0_.5, f32[1,256,4096]{2,1,0:T(8,128)} %refs_1_.5, f32[1,256,4096]{2,1,0:T(8,128)} %refs_2_.5, ...), custom_call_target="tpu_custom_call" | custom-call | flops 1 | bytes 1 | tf_op jit(solution)/shard_map/local_blocks/pallas_call | solution.py:101
  13.4 1.5 %collective-permute-start.5 = (f32[2,4,8,4096]{3,2,1,0:T(8,128)S(1)}, f32[2,4,8,4096]{3,2,1,0:T(8,128)S(1)}, u32[]{:S(2)}, u32[]{:S(2)}) collective-permute-start(f32[2,4,8,4096]{3,2,1,0:T(8,128)S(1)} %get-tuple-element.36), channel_id=1, source_target_pairs={{0,32},{1,33},{2,34},{3,35},{4,36},{5,37},{6,38},{7,39},{8,40},{9,... | collective-permute-start | bytes 3145736 | tf_op jit(solution)/shard_map/ppermute | solution.py:46
  15.1 1.4 %collective-permute-start.3 = (f32[2,2,8,4096]{3,2,1,0:T(8,128)S(1)}, f32[2,2,8,4096]{3,2,1,0:T(8,128)S(1)}, u32[]{:S(2)}, u32[]{:S(2)}) collective-permute-start(f32[2,2,8,4096]{3,2,1,0:T(8,128)S(1)} %get-tuple-element.32), channel_id=1, source_target_pairs={{0,1},{1,0},{2,3},{3,2},{4,5},{5,4},{6,7},{7,6},{8,9},{9,8},{10,11... | collective-permute-start | bytes 1572872 | tf_op jit(solution)/shard_map/ppermute | solution.py:46
  16.4 1.9 %collective-permute-start.4 = (f32[2,2,8,4096]{3,2,1,0:T(8,128)S(1)}, f32[2,2,8,4096]{3,2,1,0:T(8,128)S(1)}, u32[]{:S(2)}, u32[]{:S(2)}) collective-permute-start(f32[2,2,8,4096]{3,2,1,0:T(8,128)S(1)} %get-tuple-element.33), channel_id=1, source_target_pairs={{0,3},{1,2},{2,1},{3,0},{4,7},{5,6},{6,5},{7,4},{8,11},{9,10},{10,... | collective-permute-start | bytes 1572872 | tf_op jit(solution)/shard_map/ppermute | solution.py:46
  18.5 1.3 %collective-permute-start.8 = (f32[2,2,8,4096]{3,2,1,0:T(8,128)S(1)}, f32[2,2,8,4096]{3,2,1,0:T(8,128)S(1)}, u32[]{:S(2)}, u32[]{:S(2)}) collective-permute-start(f32[2,2,8,4096]{3,2,1,0:T(8,128)S(1)} %get-tuple-element.40), channel_id=1, source_target_pairs={{0,3},{1,2},{2,1},{3,0},{4,7},{5,6},{6,5},{7,4},{8,11},{9,10},{10,... | collective-permute-start | bytes 1572872 | tf_op jit(solution)/shard_map/ppermute | solution.py:46
  19.8 4.2 %collective-permute-done.3.refs_1_ = f32[2,2,8,4096]{3,2,1,0:T(8,128)S(1)} collective-permute-done((f32[2,2,8,4096]{3,2,1,0:T(8,128)S(1)}, f32[2,2,8,4096]{3,2,1,0:T(8,128)S(1)}, u32[]{:S(2)}, u32[]{:S(2)}) %collective-permute-start.3) | collective-permute-done | bytes 524320 | tf_op jit(solution)/shard_map/ppermute | solution.py:46
  24.0 2.0 %collective-permute-done.4.refs_2_ = f32[2,2,8,4096]{3,2,1,0:T(8,128)S(1)} collective-permute-done((f32[2,2,8,4096]{3,2,1,0:T(8,128)S(1)}, f32[2,2,8,4096]{3,2,1,0:T(8,128)S(1)}, u32[]{:S(2)}, u32[]{:S(2)}) %collective-permute-start.4) | collective-permute-done | bytes 524320 | tf_op jit(solution)/shard_map/ppermute | solution.py:46
  26.1 5.5 %collective-permute-done.8.low1 = f32[2,2,8,4096]{3,2,1,0:T(8,128)S(1)} collective-permute-done((f32[2,2,8,4096]{3,2,1,0:T(8,128)S(1)}, f32[2,2,8,4096]{3,2,1,0:T(8,128)S(1)}, u32[]{:S(2)}, u32[]{:S(2)}) %collective-permute-start.8) | collective-permute-done | bytes 524320 | tf_op jit(solution)/shard_map/ppermute | solution.py:46
  33.1 2.5 %collective-permute-start.11 = (f32[2,4,8,1024]{3,2,1,0:T(8,128)S(1)}, f32[2,4,8,1024]{3,2,1,0:T(8,128)S(1)}, u32[]{:S(2)}, u32[]{:S(2)}) collective-permute-start(f32[2,4,8,1024]{3,2,1,0:T(8,128)S(1)} %get-tuple-element.44), channel_id=1, source_target_pairs={{0,16},{1,17},{2,18},{3,19},{4,20},{5,21},{6,22},{7,23},{8,24},{9,... | collective-permute-start | bytes 786440 | tf_op jit(solution)/shard_map/ppermute | solution.py:46
  36.7 1.9 %collective-permute-done.10.b = f32[2,4,8,1024]{3,2,1,0:T(8,128)S(1)} collective-permute-done((f32[2,4,8,1024]{3,2,1,0:T(8,128)S(1)}, f32[2,4,8,1024]{3,2,1,0:T(8,128)S(1)}, u32[]{:S(2)}, u32[]{:S(2)}) %collective-permute-start.10) | collective-permute-done | bytes 262176 | tf_op jit(solution)/shard_map/ppermute | solution.py:46
  38.6 3.8 %collective-permute-done.11.c = f32[2,4,8,1024]{3,2,1,0:T(8,128)S(1)} collective-permute-done((f32[2,4,8,1024]{3,2,1,0:T(8,128)S(1)}, f32[2,4,8,1024]{3,2,1,0:T(8,128)S(1)}, u32[]{:S(2)}, u32[]{:S(2)}) %collective-permute-start.11) | collective-permute-done | bytes 262176 | tf_op jit(solution)/shard_map/ppermute | solution.py:46
  42.5 2.3 %collective-permute-start.15 = (f32[2,4,8,1024]{3,2,1,0:T(8,128)S(1)}, f32[2,4,8,1024]{3,2,1,0:T(8,128)S(1)}, u32[]{:S(2)}, u32[]{:S(2)}) collective-permute-start(f32[2,4,8,1024]{3,2,1,0:T(8,128)S(1)} %second_axis_sum.1.a), channel_id=1, source_target_pairs={{0,68},{1,69},{2,70},{3,71},{4,64},{5,65},{6,66},{7,67},{8,76},{9,... | collective-permute-start | bytes 786440 | tf_op jit(solution)/shard_map/ppermute | solution.py:46
  45.8 6.3 %collective-permute-done.15.d = f32[2,4,8,1024]{3,2,1,0:T(8,128)S(1)} collective-permute-done((f32[2,4,8,1024]{3,2,1,0:T(8,128)S(1)}, f32[2,4,8,1024]{3,2,1,0:T(8,128)S(1)}, u32[]{:S(2)}, u32[]{:S(2)}) %collective-permute-start.15) | collective-permute-done | bytes 262176 | tf_op jit(solution)/shard_map/ppermute | solution.py:46
  53.2 2.1 %collective-permute-start.18 = (f32[8,4352]{1,0:T(8,128)S(1)}, f32[8,4352]{1,0:T(8,128)S(1)}, u32[]{:S(2)}, u32[]{:S(2)}) collective-permute-start(f32[8,4352]{1,0:T(8,128)S(1)} %mean_and_preview.1.a.refs_0_), channel_id=1, source_target_pairs={{0,24},{1,25},{2,26},{3,27},{4,28},{5,29},{6,30},{7,31},{8,16},{9,... | collective-permute-start | bytes 417800 | tf_op jit(solution)/shard_map/ppermute | solution.py:46
  56.5 4.7 %collective-permute-start.19 = (f32[8,4352]{1,0:T(8,128)S(1)}, f32[8,4352]{1,0:T(8,128)S(1)}, u32[]{:S(2)}, u32[]{:S(2)}) collective-permute-start(f32[8,4352]{1,0:T(8,128)S(1)} %mean_and_preview.1.a.refs_0_), channel_id=1, source_target_pairs={{0,32},{1,33},{2,34},{3,35},{4,36},{5,37},{6,38},{7,39},{8,40},{9,... | collective-permute-start | bytes 417800 | tf_op jit(solution)/shard_map/ppermute | solution.py:46
  61.2 2.1 %collective-permute-start.25 = (f32[4,8,1280]{2,1,0:T(8,128)S(1)}, f32[4,8,1280]{2,1,0:T(8,128)S(1)}, u32[]{:S(2)}, u32[]{:S(2)}) collective-permute-start(f32[4,8,1280]{2,1,0:T(8,128)S(1)} %gathered_row.1.refs_8_), channel_id=1, source_target_pairs={{0,3},{1,2},{2,1},{3,0},{4,7},{5,6},{6,5},{7,4},{8,11},{9,10},{10,... | collective-permute-start | bytes 491528 | tf_op jit(solution)/shard_map/ppermute | solution.py:46
  63.3 1.5 %collective-permute-start.24 = (f32[4,8,1280]{2,1,0:T(8,128)S(1)}, f32[4,8,1280]{2,1,0:T(8,128)S(1)}, u32[]{:S(2)}, u32[]{:S(2)}) collective-permute-start(f32[4,8,1280]{2,1,0:T(8,128)S(1)} %gathered_row.1.refs_8_), channel_id=1, source_target_pairs={{0,2},{1,3},{2,0},{3,1},{4,6},{5,7},{6,4},{7,5},{8,10},{9,11},{10,... | collective-permute-start | bytes 491528 | tf_op jit(solution)/shard_map/ppermute | solution.py:46
  64.9 5.6 %collective-permute-start.22 = (f32[8,4352]{1,0:T(8,128)S(1)}, f32[8,4352]{1,0:T(8,128)S(1)}, u32[]{:S(2)}, u32[]{:S(2)}) collective-permute-start(f32[8,4352]{1,0:T(8,128)S(1)} %collective-permute-done.18.d.refs_3_), channel_id=1, source_target_pairs={{0,32},{1,33},{2,34},{3,35},{4,36},{5,37},{6,38},{7,39},{8,40},{9,... | collective-permute-start | bytes 417800 | tf_op jit(solution)/shard_map/ppermute | solution.py:46
  71.8 2.8 %collective-permute-start.29 = (f32[4,8,1280]{2,1,0:T(8,128)S(1)}, f32[4,8,1280]{2,1,0:T(8,128)S(1)}, u32[]{:S(2)}, u32[]{:S(2)}) collective-permute-start(f32[4,8,1280]{2,1,0:T(8,128)S(1)} %collective-permute-done.25.refs_11_), channel_id=1, source_target_pairs={{0,32},{1,33},{2,34},{3,35},{4,36},{5,37},{6,38},{7,39},{8,40},{9,... | collective-permute-start | bytes 491528 | tf_op jit(solution)/shard_map/ppermute | solution.py:46
  75.5 1.4 %collective-permute-done.20.refs_5_ = f32[8,4352]{1,0:T(8,128)S(1)} collective-permute-done((f32[8,4352]{1,0:T(8,128)S(1)}, f32[8,4352]{1,0:T(8,128)S(1)}, u32[]{:S(2)}, u32[]{:S(2)}) %collective-permute-start.20) | collective-permute-done | bytes 139296 | tf_op jit(solution)/shard_map/ppermute | solution.py:46
  (48 shorter events, 10.8 us)
Async XLA Ops:
  6.5 8.4 %collective-permute-start.2 = (f32[2,4,8,4096]{3,2,1,0:T(8,128)S(1)}, f32[2,4,8,4096]{3,2,1,0:T(8,128)S(1)}, u32[]{:S(2)}, u32[]{:S(2)}) collective-permute-start(f32[2,4,8,4096]{3,2,1,0:T(8,128)S(1)} %get-tuple-element.31), channel_id=1, source_target_pairs={{0,32},{1,33},{2,34},{3,35},{4,36},{5,37},{6,38},{7,39},{8,40},{9,... | collective-permute-start | bytes 3145736 | tf_op jit(solution)/shard_map/ppermute | solution.py:46
  6.6 8.3 %collective-permute-start.1 = (f32[2,4,8,4096]{3,2,1,0:T(8,128)S(1)}, f32[2,4,8,4096]{3,2,1,0:T(8,128)S(1)}, u32[]{:S(2)}, u32[]{:S(2)}) collective-permute-start(f32[2,4,8,4096]{3,2,1,0:T(8,128)S(1)} %get-tuple-element.26.refs_2_), channel_id=1, source_target_pairs={{0,32},{1,33},{2,34},{3,35},{4,36},{5,37},{6,38},{7,39},{8,40},{9,... | collective-permute-start | bytes 3145736 | tf_op jit(solution)/shard_map/ppermute | solution.py:46
  7.2 11.2 %collective-permute-start.7 = (f32[2,2,8,4096]{3,2,1,0:T(8,128)S(1)}, f32[2,2,8,4096]{3,2,1,0:T(8,128)S(1)}, u32[]{:S(2)}, u32[]{:S(2)}) collective-permute-start(f32[2,2,8,4096]{3,2,1,0:T(8,128)S(1)} %get-tuple-element.39), channel_id=1, source_target_pairs={{0,3},{1,2},{2,1},{3,0},{4,7},{5,6},{6,5},{7,4},{8,11},{9,10},{10,... | collective-permute-start | bytes 1572872 | tf_op jit(solution)/shard_map/ppermute | solution.py:46
  10.1 8.3 %collective-permute-start.6 = (f32[2,2,8,4096]{3,2,1,0:T(8,128)S(1)}, f32[2,2,8,4096]{3,2,1,0:T(8,128)S(1)}, u32[]{:S(2)}, u32[]{:S(2)}) collective-permute-start(f32[2,2,8,4096]{3,2,1,0:T(8,128)S(1)} %get-tuple-element.27.refs_3_), channel_id=1, source_target_pairs={{0,1},{1,0},{2,3},{3,2},{4,5},{5,4},{6,7},{7,6},{8,9},{9,8},{10,11... | collective-permute-start | bytes 1572872 | tf_op jit(solution)/shard_map/ppermute | solution.py:46
  13.4 18.2 %collective-permute-start.5 = (f32[2,4,8,4096]{3,2,1,0:T(8,128)S(1)}, f32[2,4,8,4096]{3,2,1,0:T(8,128)S(1)}, u32[]{:S(2)}, u32[]{:S(2)}) collective-permute-start(f32[2,4,8,4096]{3,2,1,0:T(8,128)S(1)} %get-tuple-element.36), channel_id=1, source_target_pairs={{0,32},{1,33},{2,34},{3,35},{4,36},{5,37},{6,38},{7,39},{8,40},{9,... | collective-permute-start | bytes 3145736 | tf_op jit(solution)/shard_map/ppermute | solution.py:46
  15.1 8.9 %collective-permute-start.3 = (f32[2,2,8,4096]{3,2,1,0:T(8,128)S(1)}, f32[2,2,8,4096]{3,2,1,0:T(8,128)S(1)}, u32[]{:S(2)}, u32[]{:S(2)}) collective-permute-start(f32[2,2,8,4096]{3,2,1,0:T(8,128)S(1)} %get-tuple-element.32), channel_id=1, source_target_pairs={{0,1},{1,0},{2,3},{3,2},{4,5},{5,4},{6,7},{7,6},{8,9},{9,8},{10,11... | collective-permute-start | bytes 1572872 | tf_op jit(solution)/shard_map/ppermute | solution.py:46
  16.4 9.5 %collective-permute-start.4 = (f32[2,2,8,4096]{3,2,1,0:T(8,128)S(1)}, f32[2,2,8,4096]{3,2,1,0:T(8,128)S(1)}, u32[]{:S(2)}, u32[]{:S(2)}) collective-permute-start(f32[2,2,8,4096]{3,2,1,0:T(8,128)S(1)} %get-tuple-element.33), channel_id=1, source_target_pairs={{0,3},{1,2},{2,1},{3,0},{4,7},{5,6},{6,5},{7,4},{8,11},{9,10},{10,... | collective-permute-start | bytes 1572872 | tf_op jit(solution)/shard_map/ppermute | solution.py:46
  18.5 13.1 %collective-permute-start.8 = (f32[2,2,8,4096]{3,2,1,0:T(8,128)S(1)}, f32[2,2,8,4096]{3,2,1,0:T(8,128)S(1)}, u32[]{:S(2)}, u32[]{:S(2)}) collective-permute-start(f32[2,2,8,4096]{3,2,1,0:T(8,128)S(1)} %get-tuple-element.40), channel_id=1, source_target_pairs={{0,3},{1,2},{2,1},{3,0},{4,7},{5,6},{6,5},{7,4},{8,11},{9,10},{10,... | collective-permute-start | bytes 1572872 | tf_op jit(solution)/shard_map/ppermute | solution.py:46
  19.8 11.8 %collective-permute-start.9 = (f32[2,2,8,4096]{3,2,1,0:T(8,128)S(1)}, f32[2,2,8,4096]{3,2,1,0:T(8,128)S(1)}, u32[]{:S(2)}, u32[]{:S(2)}) collective-permute-start(f32[2,2,8,4096]{3,2,1,0:T(8,128)S(1)} %get-tuple-element.41), channel_id=1, source_target_pairs={{0,1},{1,0},{2,3},{3,2},{4,5},{5,4},{6,7},{7,6},{8,9},{9,8},{10,11... | collective-permute-start | bytes 1572872 | tf_op jit(solution)/shard_map/ppermute | solution.py:46
  31.8 6.8 %collective-permute-start.10 = (f32[2,4,8,1024]{3,2,1,0:T(8,128)S(1)}, f32[2,4,8,1024]{3,2,1,0:T(8,128)S(1)}, u32[]{:S(2)}, u32[]{:S(2)}) collective-permute-start(f32[2,4,8,1024]{3,2,1,0:T(8,128)S(1)} %get-tuple-element.43), channel_id=1, source_target_pairs={{0,8},{1,9},{2,10},{3,11},{4,12},{5,13},{6,14},{7,15},{8,16},{9,17... | collective-permute-start | bytes 786440 | tf_op jit(solution)/shard_map/ppermute | solution.py:46
  33.1 9.3 %collective-permute-start.11 = (f32[2,4,8,1024]{3,2,1,0:T(8,128)S(1)}, f32[2,4,8,1024]{3,2,1,0:T(8,128)S(1)}, u32[]{:S(2)}, u32[]{:S(2)}) collective-permute-start(f32[2,4,8,1024]{3,2,1,0:T(8,128)S(1)} %get-tuple-element.44), channel_id=1, source_target_pairs={{0,16},{1,17},{2,18},{3,19},{4,20},{5,21},{6,22},{7,23},{8,24},{9,... | collective-permute-start | bytes 786440 | tf_op jit(solution)/shard_map/ppermute | solution.py:46
  35.6 6.9 %collective-permute-start.12 = (f32[2,4,8,1024]{3,2,1,0:T(8,128)S(1)}, f32[2,4,8,1024]{3,2,1,0:T(8,128)S(1)}, u32[]{:S(2)}, u32[]{:S(2)}) collective-permute-start(f32[2,4,8,1024]{3,2,1,0:T(8,128)S(1)} %get-tuple-element.45), channel_id=1, source_target_pairs={{0,24},{1,25},{2,26},{3,27},{4,28},{5,29},{6,30},{7,31},{8,0},{9,1... | collective-permute-start | bytes 786440 | tf_op jit(solution)/shard_map/ppermute | solution.py:46
  42.5 9.6 %collective-permute-start.15 = (f32[2,4,8,1024]{3,2,1,0:T(8,128)S(1)}, f32[2,4,8,1024]{3,2,1,0:T(8,128)S(1)}, u32[]{:S(2)}, u32[]{:S(2)}) collective-permute-start(f32[2,4,8,1024]{3,2,1,0:T(8,128)S(1)} %second_axis_sum.1.a), channel_id=1, source_target_pairs={{0,68},{1,69},{2,70},{3,71},{4,64},{5,65},{6,66},{7,67},{8,76},{9,... | collective-permute-start | bytes 786440 | tf_op jit(solution)/shard_map/ppermute | solution.py:46
  44.8 7.4 %collective-permute-start.14 = (f32[2,4,8,1024]{3,2,1,0:T(8,128)S(1)}, f32[2,4,8,1024]{3,2,1,0:T(8,128)S(1)}, u32[]{:S(2)}, u32[]{:S(2)}) collective-permute-start(f32[2,4,8,1024]{3,2,1,0:T(8,128)S(1)} %second_axis_sum.1.a), channel_id=1, source_target_pairs={{0,64},{1,65},{2,66},{3,67},{4,68},{5,69},{6,70},{7,71},{8,72},{9,... | collective-permute-start | bytes 786440 | tf_op jit(solution)/shard_map/ppermute | solution.py:46
  45.5 7.2 %collective-permute-start.13 = (f32[2,4,8,1024]{3,2,1,0:T(8,128)S(1)}, f32[2,4,8,1024]{3,2,1,0:T(8,128)S(1)}, u32[]{:S(2)}, u32[]{:S(2)}) collective-permute-start(f32[2,4,8,1024]{3,2,1,0:T(8,128)S(1)} %second_axis_sum.1.a), channel_id=1, source_target_pairs={{0,4},{1,5},{2,6},{3,7},{4,0},{5,1},{6,2},{7,3},{8,12},{9,13},{10,... | collective-permute-start | bytes 786440 | tf_op jit(solution)/shard_map/ppermute | solution.py:46
  53.2 8.0 %collective-permute-start.18 = (f32[8,4352]{1,0:T(8,128)S(1)}, f32[8,4352]{1,0:T(8,128)S(1)}, u32[]{:S(2)}, u32[]{:S(2)}) collective-permute-start(f32[8,4352]{1,0:T(8,128)S(1)} %mean_and_preview.1.a.refs_0_), channel_id=1, source_target_pairs={{0,24},{1,25},{2,26},{3,27},{4,28},{5,29},{6,30},{7,31},{8,16},{9,... | collective-permute-start | bytes 417800 | tf_op jit(solution)/shard_map/ppermute | solution.py:46
  55.2 6.0 %collective-permute-start.17 = (f32[8,4352]{1,0:T(8,128)S(1)}, f32[8,4352]{1,0:T(8,128)S(1)}, u32[]{:S(2)}, u32[]{:S(2)}) collective-permute-start(f32[8,4352]{1,0:T(8,128)S(1)} %mean_and_preview.1.a.refs_0_), channel_id=1, source_target_pairs={{0,16},{1,17},{2,18},{3,19},{4,20},{5,21},{6,22},{7,23},{8,24},{9,... | collective-permute-start | bytes 417800 | tf_op jit(solution)/shard_map/ppermute | solution.py:46
  56.1 5.1 %collective-permute-start.16 = (f32[8,4352]{1,0:T(8,128)S(1)}, f32[8,4352]{1,0:T(8,128)S(1)}, u32[]{:S(2)}, u32[]{:S(2)}) collective-permute-start(f32[8,4352]{1,0:T(8,128)S(1)} %mean_and_preview.1.a.refs_0_), channel_id=1, source_target_pairs={{0,8},{1,9},{2,10},{3,11},{4,12},{5,13},{6,14},{7,15},{8,0},{9,1},... | collective-permute-start | bytes 417800 | tf_op jit(solution)/shard_map/ppermute | solution.py:46
  56.5 13.9 %collective-permute-start.19 = (f32[8,4352]{1,0:T(8,128)S(1)}, f32[8,4352]{1,0:T(8,128)S(1)}, u32[]{:S(2)}, u32[]{:S(2)}) collective-permute-start(f32[8,4352]{1,0:T(8,128)S(1)} %mean_and_preview.1.a.refs_0_), channel_id=1, source_target_pairs={{0,32},{1,33},{2,34},{3,35},{4,36},{5,37},{6,38},{7,39},{8,40},{9,... | collective-permute-start | bytes 417800 | tf_op jit(solution)/shard_map/ppermute | solution.py:46
  61.2 10.6 %collective-permute-start.25 = (f32[4,8,1280]{2,1,0:T(8,128)S(1)}, f32[4,8,1280]{2,1,0:T(8,128)S(1)}, u32[]{:S(2)}, u32[]{:S(2)}) collective-permute-start(f32[4,8,1280]{2,1,0:T(8,128)S(1)} %gathered_row.1.refs_8_), channel_id=1, source_target_pairs={{0,3},{1,2},{2,1},{3,0},{4,7},{5,6},{6,5},{7,4},{8,11},{9,10},{10,... | collective-permute-start | bytes 491528 | tf_op jit(solution)/shard_map/ppermute | solution.py:46
  63.3 11.3 %collective-permute-start.24 = (f32[4,8,1280]{2,1,0:T(8,128)S(1)}, f32[4,8,1280]{2,1,0:T(8,128)S(1)}, u32[]{:S(2)}, u32[]{:S(2)}) collective-permute-start(f32[4,8,1280]{2,1,0:T(8,128)S(1)} %gathered_row.1.refs_8_), channel_id=1, source_target_pairs={{0,2},{1,3},{2,0},{3,1},{4,6},{5,7},{6,4},{7,5},{8,10},{9,11},{10,... | collective-permute-start | bytes 491528 | tf_op jit(solution)/shard_map/ppermute | solution.py:46
  64.9 9.8 %collective-permute-start.23 = (f32[4,8,1280]{2,1,0:T(8,128)S(1)}, f32[4,8,1280]{2,1,0:T(8,128)S(1)}, u32[]{:S(2)}, u32[]{:S(2)}) collective-permute-start(f32[4,8,1280]{2,1,0:T(8,128)S(1)} %gathered_row.1.refs_8_), channel_id=1, source_target_pairs={{0,1},{1,0},{2,3},{3,2},{4,5},{5,4},{6,7},{7,6},{8,9},{9,8},{10,11... | collective-permute-start | bytes 491528 | tf_op jit(solution)/shard_map/ppermute | solution.py:46
  64.9 6.6 %collective-permute-start.22 = (f32[8,4352]{1,0:T(8,128)S(1)}, f32[8,4352]{1,0:T(8,128)S(1)}, u32[]{:S(2)}, u32[]{:S(2)}) collective-permute-start(f32[8,4352]{1,0:T(8,128)S(1)} %collective-permute-done.18.d.refs_3_), channel_id=1, source_target_pairs={{0,32},{1,33},{2,34},{3,35},{4,36},{5,37},{6,38},{7,39},{8,40},{9,... | collective-permute-start | bytes 417800 | tf_op jit(solution)/shard_map/ppermute | solution.py:46
  71.5 5.4 %collective-permute-start.26 = (f32[4,8,1280]{2,1,0:T(8,128)S(1)}, f32[4,8,1280]{2,1,0:T(8,128)S(1)}, u32[]{:S(2)}, u32[]{:S(2)}) collective-permute-start(f32[4,8,1280]{2,1,0:T(8,128)S(1)} %gathered_row.1.refs_8_), channel_id=1, source_target_pairs={{0,32},{1,33},{2,34},{3,35},{4,36},{5,37},{6,38},{7,39},{8,40},{9,... | collective-permute-start | bytes 491528 | tf_op jit(solution)/shard_map/ppermute | solution.py:46
  (6 other events, 20.2 us)

commit v7 on v6

--- a/solution.py
+++ b/solution.py
@@ -29,16 +29,6 @@
 X, Y, Z = 0, 1, 2
 
 
-def _shift(k, axis0, axis1):
-    pairs = []
-    for d in range(128):
-        at = list(_coords(d))
-        axis = (axis0, axis1)[at[3]]
-        at[axis] = (at[axis] + k) % 4
-        pairs.append((d, _device(*at)))
-    return pairs
-
-
 _SIBLING = [(d, d ^ 32) for d in range(128)]
 
 
@@ -55,9 +45,11 @@
     return pairs
 
 
-def _exchange(arrays, axis0, axis1, pairs=_partner):
-    got = {k: _send(arrays[k], pairs(k, axis0, axis1)) for k in (1, 3, 2)}
-    return [arrays[0], got[1], got[2], got[3]]
+SECOND, THIRD, ROWS, LAST = (0, 2, 3, 1), (0, 1, 2, 3), (0, 1, 2, 3), (0, 1, 3, 2)
+
+
+def _exchange(arrays, axis0, axis1, places):
+    return [arrays[0]] + [_send(arrays[k], _partner(places[k], axis0, axis1)) for k in (1, 2, 3)]
 
 
 def _position():
@@ -135,7 +127,7 @@
 def _second_kernel(low, high, got, low1, high3, *outs):
     core, x, y, _, _, _ = _position()
     for k in range(4):
-        i = (y + k) % 4
+        i = y ^ SECOND[k]
 
         @pl.when((core == 0) & (i < 2))
         def _():
@@ -151,7 +143,7 @@
 
         @pl.when(core == 1)
         def _():
-            at = pl.ds(pl.multiple_of(((x + k) % 4) * 1024, 1024), 1024)
+            at = pl.ds(pl.multiple_of((x ^ SECOND[k]) * 1024, 1024), 1024)
             for j in range(2):
                 outs[k][:, j] = (low[:, j, :, at] + got[:, j, :, at]) + low1[:, j, :, at]
                 outs[k][:, j + 2] = (high[:, j, :, at] + got[:, j + 2, :, at]) + high3[:, j, :, at]
@@ -204,45 +196,54 @@
     )(*parts)
 
 
-def _row_kernel(a, b, c, d, out):
+def _row_kernel(a, b, c, d, out, whole):
     for k, part in enumerate((a, b, c, d)):
         out[k, :, :1024] = part[:, :1024]
         out[k, :, 1024:] = part[:, 4096:]
+        whole[k] = part[...]
 
 
 def _row(parts):
     return pl.pallas_call(
-        _row_kernel, out_shape=_shape(4, 8, 1280), compiler_params=_params(), cost_estimate=COST, name="gathered_row"
+        _row_kernel,
+        out_shape=[_shape(4, 8, 1280), _shape(4, 8, 4352)],
+        compiler_params=_params(),
+        cost_estimate=COST,
+        name="gathered_row",
     )(*parts)
 
 
-def _final_kernel(*refs):
-    own_rows, other_rows, own, other = (refs[4 * i : 4 * i + 4] for i in range(4))
-    grid, preview, lines = refs[16:]
+def _final_kernel(own_rows, other_rows, *refs):
+    own, other, (grid, preview, lines) = refs[:3], refs[3:6], refs[6:]
     me, x, y, z, _, _ = _position()
 
-    def place(rows0, last0, last1):
+    def place(rows0, last0, rows1, last1):
         for k in range(4):
-            fy, fz = y ^ k, z ^ k
-            grid[pl.ds(pl.multiple_of(fy * 8, 8), 8), :] = rows0[k][:, :4096]
+            grid[pl.ds(pl.multiple_of((y ^ ROWS[k]) * 8, 8), 8), :] = rows0[k, :, :4096]
+            fz, fy = z ^ LAST[k], y ^ LAST[k]
             for i in range(4):
                 for j in range(4):
-                    lines[fz * 8 + (y ^ i), :, j * 256 : (j + 1) * 256] = last0[k][i, 2 * j : 2 * j + 2, 1024:]
+                    two = slice(2 * j, 2 * j + 2)
+                    line = rows0[i, two, 4096:] if k == 0 else last0[k - 1][i, two, 1024:]
+                    lines[fz * 8 + (y ^ ROWS[i]), :, j * 256 : (j + 1) * 256] = line
             for i in range(4):
-                fx = x ^ i
+                fx = x ^ ROWS[i]
                 columns = pl.ds(pl.multiple_of(fx * 1024, 1024), 1024)
-                grid[pl.ds(pl.multiple_of(32 + fy * 8, 8), 8), columns] = last1[k][i, :, :1024]
+                block = rows1[i, :, :1024] if k == 0 else last1[k - 1][i, :, :1024]
+                grid[pl.ds(pl.multiple_of(32 + fy * 8, 8), 8), columns] = block
                 at = pl.ds(pl.multiple_of(fx * 256, 256), 256)
                 for j in range(4):
-                    lines[j * 8 + 4 + fy, :, at] = last1[k][i, 2 * j : 2 * j + 2, 1024:]
+                    two = slice(2 * j, 2 * j + 2)
+                    line = rows1[i, two, 4096:] if k == 0 else last1[k - 1][i, two, 1024:]
+                    lines[j * 8 + 4 + fy, :, at] = line
 
     @pl.when(me == 0)
     def _():
-        place(own_rows, own, other)
+        place(own_rows, own, other_rows, other)
 
     @pl.when(me == 1)
     def _():
-        place(other_rows, other, own)
+        place(other_rows, other, own_rows, own)
 
     for i in range(8):
         preview[8 * i : 8 * i + 8, :] = jnp.concatenate([lines[4 * i + j] for j in range(4)], axis=0)
@@ -256,7 +257,7 @@
         compiler_params=_params(),
         cost_estimate=COST,
         name="assemble",
-    )(*own_rows, *other_rows, *own, *other)
+    )(own_rows, other_rows, *own, *other)
 
 
 def _first_axis(arrays):
@@ -287,11 +288,11 @@
 
 def _local(p, c, n):
     arrays = [pltpu.with_memory_space_constraint(array, pltpu.HBM) for array in (p, c, n)]
-    both = _third(_exchange(_first_axis(arrays), Y, X, _shift))
-    packed = _mean(_exchange([both] * 4, X, Z))
-    rows = _exchange([packed] * 4, Y, X)
-    last = _exchange([_row(rows)] * 4, Z, Y)
-    return _final(rows, [_send(part, _SIBLING) for part in rows], last, [_send(part, _SIBLING) for part in last])
+    both = _third(_exchange(_first_axis(arrays), Y, X, SECOND))
+    packed = _mean(_exchange([both] * 4, X, Z, THIRD))
+    row, rows = _row(_exchange([packed] * 4, Y, X, ROWS))
+    last = _exchange([row] * 4, Z, Y, LAST)[1:]
+    return _final(rows, _send(rows, _SIBLING), last, [_send(part, _SIBLING) for part in last])
 
 
 def solution(mesh):

time: 78.3 us -> 77.3 us (0.987)
  starting transfers between devices: 40.5 us -> 31.6 us
  waiting for transfers between devices: 26.7 us -> 34.7 us
    ppermute x30 -> x26, starting transfers between devices: 40.5 us -> 31.6 us  [_send(): return lax.ppermute(array, AXES, pairs)]
    ppermute x30 -> x26, waiting for transfers between devices: 26.7 us -> 34.7 us  [_send(): return lax.ppermute(array, AXES, pairs)]
  transfers between devices with their start and end apart: 30 -> 26, of which waited for: 9 -> 15; matrix products, arithmetic and copies ran while one was open for 0% -> 0% of each run, Pallas kernels for 8% -> 8%
where the time goes in v7:
time: 77.3 us; the launch traced here: 77.1 us
  waiting for transfers between devices  34.7 us (45%)
  starting transfers between devices  31.6 us (41%)
  Pallas kernels  10.1 us (13%)
    ppermute x26, waiting for transfers between devices, _send(): return lax.ppermute(array, AXES, pairs)  34.7 us
    ppermute x26, starting transfers between devices, _send(): return lax.ppermute(array, AXES, pairs)  31.6 us
    pallas_call x3, Pallas kernels, _blocks(): pl.pallas_call(functools.partial(_blocks_kernel, wanted), in_specs=[pl.Bl...  7.61 us
  transfers between devices with their start and end apart: 26, of which 15 were waited for; matrix products, arithmetic and copies ran while one was open for 0% of the time, Pallas kernels for 8%

profile of v7, /device:TPU:1, one launch (start us, length us, event | category | flops | bytes accessed | tf_op | source)
XLA Modules:
  0.0 77.1 jit_solution(966275015054987208)
XLA Ops:
  0.6 2.2 %local_blocks.3 = (f32[2,4,8,4096]{3,2,1,0:T(8,128)S(1)}, f32[2,4,8,4096]{3,2,1,0:T(8,128)S(1)}) custom-call(f32[1,256,4096]{2,1,0:T(8,128)} %refs_0_.5, f32[1,256,4096]{2,1,0:T(8,128)} %refs_1_.5, f32[1,256,4096]{2,1,0:T(8,128)} %refs_2_.5), custom_call_target="tpu_custom_call" | custom-call | flops 1 | bytes 1 | tf_op jit(solution)/shard_map/local_blocks/pallas_call | solution.py:93
  2.8 1.5 %collective-permute-start = (f32[2,4,8,4096]{3,2,1,0:T(8,128)S(1)}, f32[2,4,8,4096]{3,2,1,0:T(8,128)S(1)}, u32[]{:S(2)}, u32[]{:S(2)}) collective-permute-start(f32[2,4,8,4096]{3,2,1,0:T(8,128)S(1)} %get-tuple-element.27), channel_id=1, source_target_pairs={{0,32},{1,33},{2,34},{3,35},{4,36},{5,37},{6,38},{7,39},{8,40},{9,... | collective-permute-start | bytes 3145736 | tf_op jit(solution)/shard_map/ppermute | solution.py:36
  4.3 2.1 %local_blocks.4 = (f32[2,4,8,4096]{3,2,1,0:T(8,128)S(1)}, f32[2,4,8,4096]{3,2,1,0:T(8,128)S(1)}) custom-call(f32[1,256,4096]{2,1,0:T(8,128)} %refs_0_.5, f32[1,256,4096]{2,1,0:T(8,128)} %refs_1_.5, f32[1,256,4096]{2,1,0:T(8,128)} %refs_2_.5, f32[2,4,8,4096]{3,2,1,0:T(8,128)S(1)} %get-tuple-element.26.refs_3_.refs_0_), custom_call_target="tpu_custom_call" | custom-call | flops 1 | bytes 1 | tf_op jit(solution)/shard_map/local_blocks/pallas_call | solution.py:93
  7.2 2.9 %collective-permute-start.7 = (f32[2,2,8,4096]{3,2,1,0:T(8,128)S(1)}, f32[2,2,8,4096]{3,2,1,0:T(8,128)S(1)}, u32[]{:S(2)}, u32[]{:S(2)}) collective-permute-start(f32[2,2,8,4096]{3,2,1,0:T(8,128)S(1)} %get-tuple-element.41), channel_id=1, source_target_pairs={{0,3},{1,2},{2,1},{3,0},{4,7},{5,6},{6,5},{7,4},{8,11},{9,10},{10,... | collective-permute-start | bytes 1572872 | tf_op jit(solution)/shard_map/ppermute | solution.py:36
  10.1 3.3 %local_blocks.5 = (f32[2,4,8,4096]{3,2,1,0:T(8,128)S(1)}, f32[2,4,8,4096]{3,2,1,0:T(8,128)S(1)}, f32[2,4,8,4096]{3,2,1,0:T(8,128)S(1)}, f32[2,4,8,4096]{3,2,1,0:T(8,128)S(1)}) custom-call(f32[1,256,4096]{2,1,0:T(8,128)} %refs_0_.5, f32[1,256,4096]{2,1,0:T(8,128)} %refs_1_.5, f32[1,256,4096]{2,1,0:T(8,128)} %refs_2_.5, ...), custom_call_target="tpu_custom_call" | custom-call | flops 1 | bytes 1 | tf_op jit(solution)/shard_map/local_blocks/pallas_call | solution.py:93
  13.4 1.5 %collective-permute-start.5 = (f32[2,4,8,4096]{3,2,1,0:T(8,128)S(1)}, f32[2,4,8,4096]{3,2,1,0:T(8,128)S(1)}, u32[]{:S(2)}, u32[]{:S(2)}) collective-permute-start(f32[2,4,8,4096]{3,2,1,0:T(8,128)S(1)} %get-tuple-element.38), channel_id=1, source_target_pairs={{0,32},{1,33},{2,34},{3,35},{4,36},{5,37},{6,38},{7,39},{8,40},{9,... | collective-permute-start | bytes 3145736 | tf_op jit(solution)/shard_map/ppermute | solution.py:36
  15.1 1.4 %collective-permute-start.3 = (f32[2,2,8,4096]{3,2,1,0:T(8,128)S(1)}, f32[2,2,8,4096]{3,2,1,0:T(8,128)S(1)}, u32[]{:S(2)}, u32[]{:S(2)}) collective-permute-start(f32[2,2,8,4096]{3,2,1,0:T(8,128)S(1)} %get-tuple-element.34), channel_id=1, source_target_pairs={{0,1},{1,0},{2,3},{3,2},{4,5},{5,4},{6,7},{7,6},{8,9},{9,8},{10,11... | collective-permute-start | bytes 1572872 | tf_op jit(solution)/shard_map/ppermute | solution.py:36
  16.4 1.9 %collective-permute-start.4 = (f32[2,2,8,4096]{3,2,1,0:T(8,128)S(1)}, f32[2,2,8,4096]{3,2,1,0:T(8,128)S(1)}, u32[]{:S(2)}, u32[]{:S(2)}) collective-permute-start(f32[2,2,8,4096]{3,2,1,0:T(8,128)S(1)} %get-tuple-element.35), channel_id=1, source_target_pairs={{0,3},{1,2},{2,1},{3,0},{4,7},{5,6},{6,5},{7,4},{8,11},{9,10},{10,... | collective-permute-start | bytes 1572872 | tf_op jit(solution)/shard_map/ppermute | solution.py:36
  18.5 1.3 %collective-permute-start.8 = (f32[2,2,8,4096]{3,2,1,0:T(8,128)S(1)}, f32[2,2,8,4096]{3,2,1,0:T(8,128)S(1)}, u32[]{:S(2)}, u32[]{:S(2)}) collective-permute-start(f32[2,2,8,4096]{3,2,1,0:T(8,128)S(1)} %get-tuple-element.42), channel_id=1, source_target_pairs={{0,3},{1,2},{2,1},{3,0},{4,7},{5,6},{6,5},{7,4},{8,11},{9,10},{10,... | collective-permute-start | bytes 1572872 | tf_op jit(solution)/shard_map/ppermute | solution.py:36
  19.8 4.2 %collective-permute-done.3.refs_1_ = f32[2,2,8,4096]{3,2,1,0:T(8,128)S(1)} collective-permute-done((f32[2,2,8,4096]{3,2,1,0:T(8,128)S(1)}, f32[2,2,8,4096]{3,2,1,0:T(8,128)S(1)}, u32[]{:S(2)}, u32[]{:S(2)}) %collective-permute-start.3) | collective-permute-done | bytes 524320 | tf_op jit(solution)/shard_map/ppermute | solution.py:36
  24.0 2.0 %collective-permute-done.4.refs_2_ = f32[2,2,8,4096]{3,2,1,0:T(8,128)S(1)} collective-permute-done((f32[2,2,8,4096]{3,2,1,0:T(8,128)S(1)}, f32[2,2,8,4096]{3,2,1,0:T(8,128)S(1)}, u32[]{:S(2)}, u32[]{:S(2)}) %collective-permute-start.4) | collective-permute-done | bytes 524320 | tf_op jit(solution)/shard_map/ppermute | solution.py:36
  26.1 5.5 %collective-permute-done.8.low1 = f32[2,2,8,4096]{3,2,1,0:T(8,128)S(1)} collective-permute-done((f32[2,2,8,4096]{3,2,1,0:T(8,128)S(1)}, f32[2,2,8,4096]{3,2,1,0:T(8,128)S(1)}, u32[]{:S(2)}, u32[]{:S(2)}) %collective-permute-start.8) | collective-permute-done | bytes 524320 | tf_op jit(solution)/shard_map/ppermute | solution.py:36
  31.8 2.8 %collective-permute-start.10 = (f32[2,4,8,1024]{3,2,1,0:T(8,128)S(1)}, f32[2,4,8,1024]{3,2,1,0:T(8,128)S(1)}, u32[]{:S(2)}, u32[]{:S(2)}) collective-permute-start(f32[2,4,8,1024]{3,2,1,0:T(8,128)S(1)} %get-tuple-element.45), channel_id=1, source_target_pairs={{0,16},{1,17},{2,18},{3,19},{4,20},{5,21},{6,22},{7,23},{8,24},{9,... | collective-permute-start | bytes 786440 | tf_op jit(solution)/shard_map/ppermute | solution.py:36
  35.5 3.4 %collective-permute-done.10.b = f32[2,4,8,1024]{3,2,1,0:T(8,128)S(1)} collective-permute-done((f32[2,4,8,1024]{3,2,1,0:T(8,128)S(1)}, f32[2,4,8,1024]{3,2,1,0:T(8,128)S(1)}, u32[]{:S(2)}, u32[]{:S(2)}) %collective-permute-start.10) | collective-permute-done | bytes 262176 | tf_op jit(solution)/shard_map/ppermute | solution.py:36
  38.9 2.8 %collective-permute-done.11.c = f32[2,4,8,1024]{3,2,1,0:T(8,128)S(1)} collective-permute-done((f32[2,4,8,1024]{3,2,1,0:T(8,128)S(1)}, f32[2,4,8,1024]{3,2,1,0:T(8,128)S(1)}, u32[]{:S(2)}, u32[]{:S(2)}) %collective-permute-start.11) | collective-permute-done | bytes 262176 | tf_op jit(solution)/shard_map/ppermute | solution.py:36
  41.9 2.5 %collective-permute-start.15 = (f32[2,4,8,1024]{3,2,1,0:T(8,128)S(1)}, f32[2,4,8,1024]{3,2,1,0:T(8,128)S(1)}, u32[]{:S(2)}, u32[]{:S(2)}) collective-permute-start(f32[2,4,8,1024]{3,2,1,0:T(8,128)S(1)} %second_axis_sum.1.a), channel_id=1, source_target_pairs={{0,68},{1,69},{2,70},{3,71},{4,64},{5,65},{6,66},{7,67},{8,76},{9,... | collective-permute-start | bytes 786440 | tf_op jit(solution)/shard_map/ppermute | solution.py:36
  45.2 5.3 %collective-permute-done.15.d = f32[2,4,8,1024]{3,2,1,0:T(8,128)S(1)} collective-permute-done((f32[2,4,8,1024]{3,2,1,0:T(8,128)S(1)}, f32[2,4,8,1024]{3,2,1,0:T(8,128)S(1)}, u32[]{:S(2)}, u32[]{:S(2)}) %collective-permute-start.15) | collective-permute-done | bytes 262176 | tf_op jit(solution)/shard_map/ppermute | solution.py:36
  52.6 2.4 %collective-permute-start.18 = (f32[8,4352]{1,0:T(8,128)S(1)}, f32[8,4352]{1,0:T(8,128)S(1)}, u32[]{:S(2)}, u32[]{:S(2)}) collective-permute-start(f32[8,4352]{1,0:T(8,128)S(1)} %mean_and_preview.1.a), channel_id=1, source_target_pairs={{0,24},{1,25},{2,26},{3,27},{4,28},{5,29},{6,30},{7,31},{8,16},{9,... | collective-permute-start | bytes 417800 | tf_op jit(solution)/shard_map/ppermute | solution.py:36
  55.9 2.6 %collective-permute-done.18.d = f32[8,4352]{1,0:T(8,128)S(1)} collective-permute-done((f32[8,4352]{1,0:T(8,128)S(1)}, f32[8,4352]{1,0:T(8,128)S(1)}, u32[]{:S(2)}, u32[]{:S(2)}) %collective-permute-start.18) | collective-permute-done | bytes 139296 | tf_op jit(solution)/shard_map/ppermute | solution.py:36
  58.5 1.9 %collective-permute-done.17.c = f32[8,4352]{1,0:T(8,128)S(1)} collective-permute-done((f32[8,4352]{1,0:T(8,128)S(1)}, f32[8,4352]{1,0:T(8,128)S(1)}, u32[]{:S(2)}, u32[]{:S(2)}) %collective-permute-start.17) | collective-permute-done | bytes 139296 | tf_op jit(solution)/shard_map/ppermute | solution.py:36
  60.5 5.4 %collective-permute-start.19 = (f32[4,8,4352]{2,1,0:T(8,128)S(1)}, f32[4,8,4352]{2,1,0:T(8,128)S(1)}, u32[]{:S(2)}, u32[]{:S(2)}) collective-permute-start(f32[4,8,4352]{2,1,0:T(8,128)S(1)} %get-tuple-element.48.own_rows), channel_id=1, source_target_pairs={{0,32},{1,33},{2,34},{3,35},{4,36},{5,37},{6,38},{7,39},{8,40},{9,... | collective-permute-start | bytes 1671176 | tf_op jit(solution)/shard_map/ppermute | solution.py:36
  65.9 1.7 %collective-permute-start.22 = (f32[4,8,1280]{2,1,0:T(8,128)S(1)}, f32[4,8,1280]{2,1,0:T(8,128)S(1)}, u32[]{:S(2)}, u32[]{:S(2)}) collective-permute-start(f32[4,8,1280]{2,1,0:T(8,128)S(1)} %get-tuple-element.49), channel_id=1, source_target_pairs={{0,2},{1,3},{2,0},{3,1},{4,6},{5,7},{6,4},{7,5},{8,10},{9,11},{10,... | collective-permute-start | bytes 491528 | tf_op jit(solution)/shard_map/ppermute | solution.py:36
  68.7 3.1 %collective-permute-done.22.refs_2_ = f32[4,8,1280]{2,1,0:T(8,128)S(1)} collective-permute-done((f32[4,8,1280]{2,1,0:T(8,128)S(1)}, f32[4,8,1280]{2,1,0:T(8,128)S(1)}, u32[]{:S(2)}, u32[]{:S(2)}) %collective-permute-start.22) | collective-permute-done | bytes 163872 | tf_op jit(solution)/shard_map/ppermute | solution.py:36
  75.9 1.2 %assemble.1 = (f32[64,4096]{1,0:T(8,128)}, f32[64,1024]{1,0:T(8,128)}) custom-call(f32[4,8,4352]{2,1,0:T(8,128)S(1)} %get-tuple-element.48.own_rows, f32[4,8,4352]{2,1,0:T(8,128)S(1)} %collective-permute-done.19.other_rows, f32[4,8,1280]{2,1,0:T(8,128)S(1)} %collective-permute-done.20.refs_0_, f32[4,8,1280]{2,1,0:T(8,128)S(1)} %collective-permute-done.21.refs_1_, ...), custom_call_target="tpu_custom_call" | custom-call | flops 1 | bytes 1 | tf_op jit(solution)/shard_map/assemble/pallas_call | solution.py:253
  (40 shorter events, 11.5 us)
Async XLA Ops:
  2.8 4.2 %collective-permute-start = (f32[2,4,8,4096]{3,2,1,0:T(8,128)S(1)}, f32[2,4,8,4096]{3,2,1,0:T(8,128)S(1)}, u32[]{:S(2)}, u32[]{:S(2)}) collective-permute-start(f32[2,4,8,4096]{3,2,1,0:T(8,128)S(1)} %get-tuple-element.27), channel_id=1, source_target_pairs={{0,32},{1,33},{2,34},{3,35},{4,36},{5,37},{6,38},{7,39},{8,40},{9,... | collective-permute-start | bytes 3145736 | tf_op jit(solution)/shard_map/ppermute | solution.py:36
  6.5 8.4 %collective-permute-start.2 = (f32[2,4,8,4096]{3,2,1,0:T(8,128)S(1)}, f32[2,4,8,4096]{3,2,1,0:T(8,128)S(1)}, u32[]{:S(2)}, u32[]{:S(2)}) collective-permute-start(f32[2,4,8,4096]{3,2,1,0:T(8,128)S(1)} %get-tuple-element.33), channel_id=1, source_target_pairs={{0,32},{1,33},{2,34},{3,35},{4,36},{5,37},{6,38},{7,39},{8,40},{9,... | collective-permute-start | bytes 3145736 | tf_op jit(solution)/shard_map/ppermute | solution.py:36
  6.6 8.3 %collective-permute-start.1 = (f32[2,4,8,4096]{3,2,1,0:T(8,128)S(1)}, f32[2,4,8,4096]{3,2,1,0:T(8,128)S(1)}, u32[]{:S(2)}, u32[]{:S(2)}) collective-permute-start(f32[2,4,8,4096]{3,2,1,0:T(8,128)S(1)} %get-tuple-element.28.refs_2_), channel_id=1, source_target_pairs={{0,32},{1,33},{2,34},{3,35},{4,36},{5,37},{6,38},{7,39},{8,40},{9,... | collective-permute-start | bytes 3145736 | tf_op jit(solution)/shard_map/ppermute | solution.py:36
  7.2 11.2 %collective-permute-start.7 = (f32[2,2,8,4096]{3,2,1,0:T(8,128)S(1)}, f32[2,2,8,4096]{3,2,1,0:T(8,128)S(1)}, u32[]{:S(2)}, u32[]{:S(2)}) collective-permute-start(f32[2,2,8,4096]{3,2,1,0:T(8,128)S(1)} %get-tuple-element.41), channel_id=1, source_target_pairs={{0,3},{1,2},{2,1},{3,0},{4,7},{5,6},{6,5},{7,4},{8,11},{9,10},{10,... | collective-permute-start | bytes 1572872 | tf_op jit(solution)/shard_map/ppermute | solution.py:36
  10.1 8.3 %collective-permute-start.6 = (f32[2,2,8,4096]{3,2,1,0:T(8,128)S(1)}, f32[2,2,8,4096]{3,2,1,0:T(8,128)S(1)}, u32[]{:S(2)}, u32[]{:S(2)}) collective-permute-start(f32[2,2,8,4096]{3,2,1,0:T(8,128)S(1)} %get-tuple-element.29.refs_3_), channel_id=1, source_target_pairs={{0,1},{1,0},{2,3},{3,2},{4,5},{5,4},{6,7},{7,6},{8,9},{9,8},{10,11... | collective-permute-start | bytes 1572872 | tf_op jit(solution)/shard_map/ppermute | solution.py:36
  13.4 18.2 %collective-permute-start.5 = (f32[2,4,8,4096]{3,2,1,0:T(8,128)S(1)}, f32[2,4,8,4096]{3,2,1,0:T(8,128)S(1)}, u32[]{:S(2)}, u32[]{:S(2)}) collective-permute-start(f32[2,4,8,4096]{3,2,1,0:T(8,128)S(1)} %get-tuple-element.38), channel_id=1, source_target_pairs={{0,32},{1,33},{2,34},{3,35},{4,36},{5,37},{6,38},{7,39},{8,40},{9,... | collective-permute-start | bytes 3145736 | tf_op jit(solution)/shard_map/ppermute | solution.py:36
  15.1 8.9 %collective-permute-start.3 = (f32[2,2,8,4096]{3,2,1,0:T(8,128)S(1)}, f32[2,2,8,4096]{3,2,1,0:T(8,128)S(1)}, u32[]{:S(2)}, u32[]{:S(2)}) collective-permute-start(f32[2,2,8,4096]{3,2,1,0:T(8,128)S(1)} %get-tuple-element.34), channel_id=1, source_target_pairs={{0,1},{1,0},{2,3},{3,2},{4,5},{5,4},{6,7},{7,6},{8,9},{9,8},{10,11... | collective-permute-start | bytes 1572872 | tf_op jit(solution)/shard_map/ppermute | solution.py:36
  16.4 9.5 %collective-permute-start.4 = (f32[2,2,8,4096]{3,2,1,0:T(8,128)S(1)}, f32[2,2,8,4096]{3,2,1,0:T(8,128)S(1)}, u32[]{:S(2)}, u32[]{:S(2)}) collective-permute-start(f32[2,2,8,4096]{3,2,1,0:T(8,128)S(1)} %get-tuple-element.35), channel_id=1, source_target_pairs={{0,3},{1,2},{2,1},{3,0},{4,7},{5,6},{6,5},{7,4},{8,11},{9,10},{10,... | collective-permute-start | bytes 1572872 | tf_op jit(solution)/shard_map/ppermute | solution.py:36
  18.5 13.1 %collective-permute-start.8 = (f32[2,2,8,4096]{3,2,1,0:T(8,128)S(1)}, f32[2,2,8,4096]{3,2,1,0:T(8,128)S(1)}, u32[]{:S(2)}, u32[]{:S(2)}) collective-permute-start(f32[2,2,8,4096]{3,2,1,0:T(8,128)S(1)} %get-tuple-element.42), channel_id=1, source_target_pairs={{0,3},{1,2},{2,1},{3,0},{4,7},{5,6},{6,5},{7,4},{8,11},{9,10},{10,... | collective-permute-start | bytes 1572872 | tf_op jit(solution)/shard_map/ppermute | solution.py:36
  19.8 11.8 %collective-permute-start.9 = (f32[2,2,8,4096]{3,2,1,0:T(8,128)S(1)}, f32[2,2,8,4096]{3,2,1,0:T(8,128)S(1)}, u32[]{:S(2)}, u32[]{:S(2)}) collective-permute-start(f32[2,2,8,4096]{3,2,1,0:T(8,128)S(1)} %get-tuple-element.43), channel_id=1, source_target_pairs={{0,1},{1,0},{2,3},{3,2},{4,5},{5,4},{6,7},{7,6},{8,9},{9,8},{10,11... | collective-permute-start | bytes 1572872 | tf_op jit(solution)/shard_map/ppermute | solution.py:36
  31.8 7.1 %collective-permute-start.10 = (f32[2,4,8,1024]{3,2,1,0:T(8,128)S(1)}, f32[2,4,8,1024]{3,2,1,0:T(8,128)S(1)}, u32[]{:S(2)}, u32[]{:S(2)}) collective-permute-start(f32[2,4,8,1024]{3,2,1,0:T(8,128)S(1)} %get-tuple-element.45), channel_id=1, source_target_pairs={{0,16},{1,17},{2,18},{3,19},{4,20},{5,21},{6,22},{7,23},{8,24},{9,... | collective-permute-start | bytes 786440 | tf_op jit(solution)/shard_map/ppermute | solution.py:36
  34.6 7.1 %collective-permute-start.11 = (f32[2,4,8,1024]{3,2,1,0:T(8,128)S(1)}, f32[2,4,8,1024]{3,2,1,0:T(8,128)S(1)}, u32[]{:S(2)}, u32[]{:S(2)}) collective-permute-start(f32[2,4,8,1024]{3,2,1,0:T(8,128)S(1)} %get-tuple-element.46), channel_id=1, source_target_pairs={{0,24},{1,25},{2,26},{3,27},{4,28},{5,29},{6,30},{7,31},{8,16},{9,... | collective-permute-start | bytes 786440 | tf_op jit(solution)/shard_map/ppermute | solution.py:36
  35.5 6.4 %collective-permute-start.12 = (f32[2,4,8,1024]{3,2,1,0:T(8,128)S(1)}, f32[2,4,8,1024]{3,2,1,0:T(8,128)S(1)}, u32[]{:S(2)}, u32[]{:S(2)}) collective-permute-start(f32[2,4,8,1024]{3,2,1,0:T(8,128)S(1)} %get-tuple-element.47), channel_id=1, source_target_pairs={{0,8},{1,9},{2,10},{3,11},{4,12},{5,13},{6,14},{7,15},{8,0},{9,1},... | collective-permute-start | bytes 786440 | tf_op jit(solution)/shard_map/ppermute | solution.py:36
  41.9 8.6 %collective-permute-start.15 = (f32[2,4,8,1024]{3,2,1,0:T(8,128)S(1)}, f32[2,4,8,1024]{3,2,1,0:T(8,128)S(1)}, u32[]{:S(2)}, u32[]{:S(2)}) collective-permute-start(f32[2,4,8,1024]{3,2,1,0:T(8,128)S(1)} %second_axis_sum.1.a), channel_id=1, source_target_pairs={{0,68},{1,69},{2,70},{3,71},{4,64},{5,65},{6,66},{7,67},{8,76},{9,... | collective-permute-start | bytes 786440 | tf_op jit(solution)/shard_map/ppermute | solution.py:36
  44.4 6.8 %collective-permute-start.14 = (f32[2,4,8,1024]{3,2,1,0:T(8,128)S(1)}, f32[2,4,8,1024]{3,2,1,0:T(8,128)S(1)}, u32[]{:S(2)}, u32[]{:S(2)}) collective-permute-start(f32[2,4,8,1024]{3,2,1,0:T(8,128)S(1)} %second_axis_sum.1.a), channel_id=1, source_target_pairs={{0,64},{1,65},{2,66},{3,67},{4,68},{5,69},{6,70},{7,71},{8,72},{9,... | collective-permute-start | bytes 786440 | tf_op jit(solution)/shard_map/ppermute | solution.py:36
  44.9 7.2 %collective-permute-start.13 = (f32[2,4,8,1024]{3,2,1,0:T(8,128)S(1)}, f32[2,4,8,1024]{3,2,1,0:T(8,128)S(1)}, u32[]{:S(2)}, u32[]{:S(2)}) collective-permute-start(f32[2,4,8,1024]{3,2,1,0:T(8,128)S(1)} %second_axis_sum.1.a), channel_id=1, source_target_pairs={{0,4},{1,5},{2,6},{3,7},{4,0},{5,1},{6,2},{7,3},{8,12},{9,13},{10,... | collective-permute-start | bytes 786440 | tf_op jit(solution)/shard_map/ppermute | solution.py:36
  52.6 5.9 %collective-permute-start.18 = (f32[8,4352]{1,0:T(8,128)S(1)}, f32[8,4352]{1,0:T(8,128)S(1)}, u32[]{:S(2)}, u32[]{:S(2)}) collective-permute-start(f32[8,4352]{1,0:T(8,128)S(1)} %mean_and_preview.1.a), channel_id=1, source_target_pairs={{0,24},{1,25},{2,26},{3,27},{4,28},{5,29},{6,30},{7,31},{8,16},{9,... | collective-permute-start | bytes 417800 | tf_op jit(solution)/shard_map/ppermute | solution.py:36
  55.0 5.4 %collective-permute-start.17 = (f32[8,4352]{1,0:T(8,128)S(1)}, f32[8,4352]{1,0:T(8,128)S(1)}, u32[]{:S(2)}, u32[]{:S(2)}) collective-permute-start(f32[8,4352]{1,0:T(8,128)S(1)} %mean_and_preview.1.a), channel_id=1, source_target_pairs={{0,16},{1,17},{2,18},{3,19},{4,20},{5,21},{6,22},{7,23},{8,24},{9,... | collective-permute-start | bytes 417800 | tf_op jit(solution)/shard_map/ppermute | solution.py:36
  55.6 4.8 %collective-permute-start.16 = (f32[8,4352]{1,0:T(8,128)S(1)}, f32[8,4352]{1,0:T(8,128)S(1)}, u32[]{:S(2)}, u32[]{:S(2)}) collective-permute-start(f32[8,4352]{1,0:T(8,128)S(1)} %mean_and_preview.1.a), channel_id=1, source_target_pairs={{0,8},{1,9},{2,10},{3,11},{4,12},{5,13},{6,14},{7,15},{8,0},{9,1},... | collective-permute-start | bytes 417800 | tf_op jit(solution)/shard_map/ppermute | solution.py:36
  60.5 15.4 %collective-permute-start.19 = (f32[4,8,4352]{2,1,0:T(8,128)S(1)}, f32[4,8,4352]{2,1,0:T(8,128)S(1)}, u32[]{:S(2)}, u32[]{:S(2)}) collective-permute-start(f32[4,8,4352]{2,1,0:T(8,128)S(1)} %get-tuple-element.48.own_rows), channel_id=1, source_target_pairs={{0,32},{1,33},{2,34},{3,35},{4,36},{5,37},{6,38},{7,39},{8,40},{9,... | collective-permute-start | bytes 1671176 | tf_op jit(solution)/shard_map/ppermute | solution.py:36
  65.9 6.0 %collective-permute-start.22 = (f32[4,8,1280]{2,1,0:T(8,128)S(1)}, f32[4,8,1280]{2,1,0:T(8,128)S(1)}, u32[]{:S(2)}, u32[]{:S(2)}) collective-permute-start(f32[4,8,1280]{2,1,0:T(8,128)S(1)} %get-tuple-element.49), channel_id=1, source_target_pairs={{0,2},{1,3},{2,0},{3,1},{4,6},{5,7},{6,4},{7,5},{8,10},{9,11},{10,... | collective-permute-start | bytes 491528 | tf_op jit(solution)/shard_map/ppermute | solution.py:36
  67.6 6.0 %collective-permute-start.21 = (f32[4,8,1280]{2,1,0:T(8,128)S(1)}, f32[4,8,1280]{2,1,0:T(8,128)S(1)}, u32[]{:S(2)}, u32[]{:S(2)}) collective-permute-start(f32[4,8,1280]{2,1,0:T(8,128)S(1)} %get-tuple-element.49), channel_id=1, source_target_pairs={{0,3},{1,2},{2,1},{3,0},{4,7},{5,6},{6,5},{7,4},{8,11},{9,10},{10,... | collective-permute-start | bytes 491528 | tf_op jit(solution)/shard_map/ppermute | solution.py:36
  68.7 5.8 %collective-permute-start.20 = (f32[4,8,1280]{2,1,0:T(8,128)S(1)}, f32[4,8,1280]{2,1,0:T(8,128)S(1)}, u32[]{:S(2)}, u32[]{:S(2)}) collective-permute-start(f32[4,8,1280]{2,1,0:T(8,128)S(1)} %get-tuple-element.49), channel_id=1, source_target_pairs={{0,1},{1,0},{2,3},{3,2},{4,5},{5,4},{6,7},{7,6},{8,9},{9,8},{10,11... | collective-permute-start | bytes 491528 | tf_op jit(solution)/shard_map/ppermute | solution.py:36
  71.8 2.7 %collective-permute-start.25 = (f32[4,8,1280]{2,1,0:T(8,128)S(1)}, f32[4,8,1280]{2,1,0:T(8,128)S(1)}, u32[]{:S(2)}, u32[]{:S(2)}) collective-permute-start(f32[4,8,1280]{2,1,0:T(8,128)S(1)} %collective-permute-done.22.refs_2_), channel_id=1, source_target_pairs={{0,32},{1,33},{2,34},{3,35},{4,36},{5,37},{6,38},{7,39},{8,40},{9,... | collective-permute-start | bytes 491528 | tf_op jit(solution)/shard_map/ppermute | solution.py:36
  (2 other events, 3.4 us)

commit v8 on v7

--- a/solution.py
+++ b/solution.py
@@ -261,29 +261,29 @@
 
 
 def _first_axis(arrays):
-    near, far = _partner(1, Z, Y), _partner(3, Z, Y)
+    near, far = _partner(3, Z, Y), _partner(1, Z, Y)
     whole = slice(None)
     sent2, own2 = _blocks(arrays, ((2, False), (2, True)))
     got2 = _send(sent2, _SIBLING)
-    sent1, sent3 = _blocks(arrays, ((1, False), (3, False)), (own2,))
-    got1, got3 = _send(sent1, _SIBLING), _send(sent3, _SIBLING)
-    low2, high2 = _sums((own2, got2), [[(0, LOW), (1, LOW)], [(0, HIGH), (1, HIGH)]], "opposite_pair", (sent1,))
+    sent_near, sent_far = _blocks(arrays, ((3, False), (1, False)), (own2,))
+    got_near, got_far = _send(sent_near, _SIBLING), _send(sent_far, _SIBLING)
+    low2, high2 = _sums((own2, got2), [[(0, LOW), (1, LOW)], [(0, HIGH), (1, HIGH)]], "opposite_pair", (sent_near,))
     low, high = _send(low2, near), _send(high2, far)
-    own1, own3, sent0, own0 = _blocks(arrays, ((1, True), (3, True), (0, False), (0, True)), (low2,))
-    low1, high1, low3, high3 = _sums(
-        (own1, got1, own3, got3),
+    own_near, own_far, sent0, own0 = _blocks(arrays, ((3, True), (1, True), (0, False), (0, True)), (low2,))
+    low_near, high_near, low_far, high_far = _sums(
+        (own_near, got_near, own_far, got_far),
         [[(0, LOW), (1, LOW)], [(0, HIGH), (1, HIGH)], [(2, LOW), (3, LOW)], [(2, HIGH), (3, HIGH)]],
         "neighbour_pairs",
     )
     got0 = _send(sent0, _SIBLING)
-    low1, high3 = _send(low1, near), _send(high3, far)
-    low3, high1 = _sums((low3, low, high1, high), [[(0, whole), (1, whole)], [(2, whole), (3, whole)]], "passed_on")
+    low_near, high_far = _send(low_near, near), _send(high_far, far)
+    low_far, high_near = _sums((low_far, low, high_near, high), [[(0, whole), (1, whole)], [(2, whole), (3, whole)]], "passed_on")
     low, high = _sums(
-        (own0, low1, high3),
+        (own0, low_near, high_far),
         [[(0, LOW), (1, whole)], [(0, HIGH), (2, whole)]],
         "early_sum",
     )
-    return _second(low, high, got0, _send(low3, far), _send(high1, near))
+    return _second(low, high, got0, _send(low_far, far), _send(high_near, near))
 
 
 def _local(p, c, n):

time: 77.3 us -> 76.7 us (level)
  starting transfers between devices: 31.6 us -> 30.8 us
    ppermute x26, starting transfers between devices: 31.6 us -> 30.8 us  [_send(): return lax.ppermute(array, AXES, pairs)]
  transfers between devices with their start and end apart: 26 -> 26, of which waited for: 15 -> 14; matrix products, arithmetic and copies ran while one was open for 0% -> 0% of each run, Pallas kernels for 8% -> 8%
where the time goes in v8:
time: 76.7 us; the launch traced here: 76.5 us
  waiting for transfers between devices  35 us (46%)
  starting transfers between devices  30.8 us (40%)
  Pallas kernels  10.1 us (13%)
    ppermute x26, waiting for transfers between devices, _send(): return lax.ppermute(array, AXES, pairs)  35 us
    ppermute x26, starting transfers between devices, _send(): return lax.ppermute(array, AXES, pairs)  30.8 us
    pallas_call x3, Pallas kernels, _blocks(): pl.pallas_call(functools.partial(_blocks_kernel, wanted), in_specs=[pl.Bl...  7.61 us
  transfers between devices with their start and end apart: 26, of which 14 were waited for; matrix products, arithmetic and copies ran while one was open for 0% of the time, Pallas kernels for 8%

profile of v8, /device:TPU:1, one launch (start us, length us, event | category | flops | bytes accessed | tf_op | source)
XLA Modules:
  0.0 76.5 jit_solution(15346687738793693261)
XLA Ops:
  0.6 2.2 %local_blocks.3 = (f32[2,4,8,4096]{3,2,1,0:T(8,128)S(1)}, f32[2,4,8,4096]{3,2,1,0:T(8,128)S(1)}) custom-call(f32[1,256,4096]{2,1,0:T(8,128)} %refs_0_.5, f32[1,256,4096]{2,1,0:T(8,128)} %refs_1_.5, f32[1,256,4096]{2,1,0:T(8,128)} %refs_2_.5), custom_call_target="tpu_custom_call" | custom-call | flops 1 | bytes 1 | tf_op jit(solution)/shard_map/local_blocks/pallas_call | solution.py:93
  2.8 1.5 %collective-permute-start = (f32[2,4,8,4096]{3,2,1,0:T(8,128)S(1)}, f32[2,4,8,4096]{3,2,1,0:T(8,128)S(1)}, u32[]{:S(2)}, u32[]{:S(2)}) collective-permute-start(f32[2,4,8,4096]{3,2,1,0:T(8,128)S(1)} %get-tuple-element.27), channel_id=1, source_target_pairs={{0,32},{1,33},{2,34},{3,35},{4,36},{5,37},{6,38},{7,39},{8,40},{9,... | collective-permute-start | bytes 3145736 | tf_op jit(solution)/shard_map/ppermute | solution.py:36
  4.3 2.1 %local_blocks.4 = (f32[2,4,8,4096]{3,2,1,0:T(8,128)S(1)}, f32[2,4,8,4096]{3,2,1,0:T(8,128)S(1)}) custom-call(f32[1,256,4096]{2,1,0:T(8,128)} %refs_0_.5, f32[1,256,4096]{2,1,0:T(8,128)} %refs_1_.5, f32[1,256,4096]{2,1,0:T(8,128)} %refs_2_.5, f32[2,4,8,4096]{3,2,1,0:T(8,128)S(1)} %get-tuple-element.26.refs_3_.refs_0_), custom_call_target="tpu_custom_call" | custom-call | flops 1 | bytes 1 | tf_op jit(solution)/shard_map/local_blocks/pallas_call | solution.py:93
  7.2 1.5 %collective-permute-start.7 = (f32[2,2,8,4096]{3,2,1,0:T(8,128)S(1)}, f32[2,2,8,4096]{3,2,1,0:T(8,128)S(1)}, u32[]{:S(2)}, u32[]{:S(2)}) collective-permute-start(f32[2,2,8,4096]{3,2,1,0:T(8,128)S(1)} %get-tuple-element.41), channel_id=1, source_target_pairs={{0,1},{1,0},{2,3},{3,2},{4,5},{5,4},{6,7},{7,6},{8,9},{9,8},{10,11... | collective-permute-start | bytes 1572872 | tf_op jit(solution)/shard_map/ppermute | solution.py:36
  8.6 1.9 %collective-permute-start.6 = (f32[2,2,8,4096]{3,2,1,0:T(8,128)S(1)}, f32[2,2,8,4096]{3,2,1,0:T(8,128)S(1)}, u32[]{:S(2)}, u32[]{:S(2)}) collective-permute-start(f32[2,2,8,4096]{3,2,1,0:T(8,128)S(1)} %get-tuple-element.29.refs_3_), channel_id=1, source_target_pairs={{0,3},{1,2},{2,1},{3,0},{4,7},{5,6},{6,5},{7,4},{8,11},{9,10},{10,... | collective-permute-start | bytes 1572872 | tf_op jit(solution)/shard_map/ppermute | solution.py:36
  10.5 3.3 %local_blocks.5 = (f32[2,4,8,4096]{3,2,1,0:T(8,128)S(1)}, f32[2,4,8,4096]{3,2,1,0:T(8,128)S(1)}, f32[2,4,8,4096]{3,2,1,0:T(8,128)S(1)}, f32[2,4,8,4096]{3,2,1,0:T(8,128)S(1)}) custom-call(f32[1,256,4096]{2,1,0:T(8,128)} %refs_0_.5, f32[1,256,4096]{2,1,0:T(8,128)} %refs_1_.5, f32[1,256,4096]{2,1,0:T(8,128)} %refs_2_.5, ...), custom_call_target="tpu_custom_call" | custom-call | flops 1 | bytes 1 | tf_op jit(solution)/shard_map/local_blocks/pallas_call | solution.py:93
  13.8 1.4 %collective-permute-start.5 = (f32[2,4,8,4096]{3,2,1,0:T(8,128)S(1)}, f32[2,4,8,4096]{3,2,1,0:T(8,128)S(1)}, u32[]{:S(2)}, u32[]{:S(2)}) collective-permute-start(f32[2,4,8,4096]{3,2,1,0:T(8,128)S(1)} %get-tuple-element.38), channel_id=1, source_target_pairs={{0,32},{1,33},{2,34},{3,35},{4,36},{5,37},{6,38},{7,39},{8,40},{9,... | collective-permute-start | bytes 3145736 | tf_op jit(solution)/shard_map/ppermute | solution.py:36
  15.5 2.8 %collective-permute-start.3 = (f32[2,2,8,4096]{3,2,1,0:T(8,128)S(1)}, f32[2,2,8,4096]{3,2,1,0:T(8,128)S(1)}, u32[]{:S(2)}, u32[]{:S(2)}) collective-permute-start(f32[2,2,8,4096]{3,2,1,0:T(8,128)S(1)} %get-tuple-element.34), channel_id=1, source_target_pairs={{0,3},{1,2},{2,1},{3,0},{4,7},{5,6},{6,5},{7,4},{8,11},{9,10},{10,... | collective-permute-start | bytes 1572872 | tf_op jit(solution)/shard_map/ppermute | solution.py:36
  18.4 1.5 %collective-permute-start.8 = (f32[2,2,8,4096]{3,2,1,0:T(8,128)S(1)}, f32[2,2,8,4096]{3,2,1,0:T(8,128)S(1)}, u32[]{:S(2)}, u32[]{:S(2)}) collective-permute-start(f32[2,2,8,4096]{3,2,1,0:T(8,128)S(1)} %get-tuple-element.42), channel_id=1, source_target_pairs={{0,1},{1,0},{2,3},{3,2},{4,5},{5,4},{6,7},{7,6},{8,9},{9,8},{10,11... | collective-permute-start | bytes 1572872 | tf_op jit(solution)/shard_map/ppermute | solution.py:36
  20.3 4.8 %collective-permute-done.3.refs_1_ = f32[2,2,8,4096]{3,2,1,0:T(8,128)S(1)} collective-permute-done((f32[2,2,8,4096]{3,2,1,0:T(8,128)S(1)}, f32[2,2,8,4096]{3,2,1,0:T(8,128)S(1)}, u32[]{:S(2)}, u32[]{:S(2)}) %collective-permute-start.3) | collective-permute-done | bytes 524320 | tf_op jit(solution)/shard_map/ppermute | solution.py:36
  25.2 1.5 %collective-permute-done.4.refs_2_ = f32[2,2,8,4096]{3,2,1,0:T(8,128)S(1)} collective-permute-done((f32[2,2,8,4096]{3,2,1,0:T(8,128)S(1)}, f32[2,2,8,4096]{3,2,1,0:T(8,128)S(1)}, u32[]{:S(2)}, u32[]{:S(2)}) %collective-permute-start.4) | collective-permute-done | bytes 524320 | tf_op jit(solution)/shard_map/ppermute | solution.py:36
  26.7 5.5 %collective-permute-done.8.low1 = f32[2,2,8,4096]{3,2,1,0:T(8,128)S(1)} collective-permute-done((f32[2,2,8,4096]{3,2,1,0:T(8,128)S(1)}, f32[2,2,8,4096]{3,2,1,0:T(8,128)S(1)}, u32[]{:S(2)}, u32[]{:S(2)}) %collective-permute-start.8) | collective-permute-done | bytes 524320 | tf_op jit(solution)/shard_map/ppermute | solution.py:36
  32.4 2.8 %collective-permute-start.10 = (f32[2,4,8,1024]{3,2,1,0:T(8,128)S(1)}, f32[2,4,8,1024]{3,2,1,0:T(8,128)S(1)}, u32[]{:S(2)}, u32[]{:S(2)}) collective-permute-start(f32[2,4,8,1024]{3,2,1,0:T(8,128)S(1)} %get-tuple-element.45), channel_id=1, source_target_pairs={{0,16},{1,17},{2,18},{3,19},{4,20},{5,21},{6,22},{7,23},{8,24},{9,... | collective-permute-start | bytes 786440 | tf_op jit(solution)/shard_map/ppermute | solution.py:36
  36.1 3.4 %collective-permute-done.10.b = f32[2,4,8,1024]{3,2,1,0:T(8,128)S(1)} collective-permute-done((f32[2,4,8,1024]{3,2,1,0:T(8,128)S(1)}, f32[2,4,8,1024]{3,2,1,0:T(8,128)S(1)}, u32[]{:S(2)}, u32[]{:S(2)}) %collective-permute-start.10) | collective-permute-done | bytes 262176 | tf_op jit(solution)/shard_map/ppermute | solution.py:36
  39.5 2.8 %collective-permute-done.11.c = f32[2,4,8,1024]{3,2,1,0:T(8,128)S(1)} collective-permute-done((f32[2,4,8,1024]{3,2,1,0:T(8,128)S(1)}, f32[2,4,8,1024]{3,2,1,0:T(8,128)S(1)}, u32[]{:S(2)}, u32[]{:S(2)}) %collective-permute-start.11) | collective-permute-done | bytes 262176 | tf_op jit(solution)/shard_map/ppermute | solution.py:36
  43.5 1.5 %collective-permute-start.14 = (f32[2,4,8,1024]{3,2,1,0:T(8,128)S(1)}, f32[2,4,8,1024]{3,2,1,0:T(8,128)S(1)}, u32[]{:S(2)}, u32[]{:S(2)}) collective-permute-start(f32[2,4,8,1024]{3,2,1,0:T(8,128)S(1)} %second_axis_sum.1.a), channel_id=1, source_target_pairs={{0,64},{1,65},{2,66},{3,67},{4,68},{5,69},{6,70},{7,71},{8,72},{9,... | collective-permute-start | bytes 786440 | tf_op jit(solution)/shard_map/ppermute | solution.py:36
  45.9 6.3 %collective-permute-done.15.d = f32[2,4,8,1024]{3,2,1,0:T(8,128)S(1)} collective-permute-done((f32[2,4,8,1024]{3,2,1,0:T(8,128)S(1)}, f32[2,4,8,1024]{3,2,1,0:T(8,128)S(1)}, u32[]{:S(2)}, u32[]{:S(2)}) %collective-permute-start.15) | collective-permute-done | bytes 262176 | tf_op jit(solution)/shard_map/ppermute | solution.py:36
  53.2 2.4 %collective-permute-start.18 = (f32[8,4352]{1,0:T(8,128)S(1)}, f32[8,4352]{1,0:T(8,128)S(1)}, u32[]{:S(2)}, u32[]{:S(2)}) collective-permute-start(f32[8,4352]{1,0:T(8,128)S(1)} %mean_and_preview.1.a), channel_id=1, source_target_pairs={{0,24},{1,25},{2,26},{3,27},{4,28},{5,29},{6,30},{7,31},{8,16},{9,... | collective-permute-start | bytes 417800 | tf_op jit(solution)/shard_map/ppermute | solution.py:36
  56.6 2.6 %collective-permute-done.18.d = f32[8,4352]{1,0:T(8,128)S(1)} collective-permute-done((f32[8,4352]{1,0:T(8,128)S(1)}, f32[8,4352]{1,0:T(8,128)S(1)}, u32[]{:S(2)}, u32[]{:S(2)}) %collective-permute-start.18) | collective-permute-done | bytes 139296 | tf_op jit(solution)/shard_map/ppermute | solution.py:36
  59.1 1.9 %collective-permute-done.17.c = f32[8,4352]{1,0:T(8,128)S(1)} collective-permute-done((f32[8,4352]{1,0:T(8,128)S(1)}, f32[8,4352]{1,0:T(8,128)S(1)}, u32[]{:S(2)}, u32[]{:S(2)}) %collective-permute-start.17) | collective-permute-done | bytes 139296 | tf_op jit(solution)/shard_map/ppermute | solution.py:36
  61.1 4.1 %collective-permute-start.19 = (f32[4,8,4352]{2,1,0:T(8,128)S(1)}, f32[4,8,4352]{2,1,0:T(8,128)S(1)}, u32[]{:S(2)}, u32[]{:S(2)}) collective-permute-start(f32[4,8,4352]{2,1,0:T(8,128)S(1)} %get-tuple-element.48.own_rows), channel_id=1, source_target_pairs={{0,32},{1,33},{2,34},{3,35},{4,36},{5,37},{6,38},{7,39},{8,40},{9,... | collective-permute-start | bytes 1671176 | tf_op jit(solution)/shard_map/ppermute | solution.py:36
  66.3 1.6 %collective-permute-start.21 = (f32[4,8,1280]{2,1,0:T(8,128)S(1)}, f32[4,8,1280]{2,1,0:T(8,128)S(1)}, u32[]{:S(2)}, u32[]{:S(2)}) collective-permute-start(f32[4,8,1280]{2,1,0:T(8,128)S(1)} %get-tuple-element.49), channel_id=1, source_target_pairs={{0,3},{1,2},{2,1},{3,0},{4,7},{5,6},{6,5},{7,4},{8,11},{9,10},{10,... | collective-permute-start | bytes 491528 | tf_op jit(solution)/shard_map/ppermute | solution.py:36
  67.9 3.3 %collective-permute-done.22.refs_2_ = f32[4,8,1280]{2,1,0:T(8,128)S(1)} collective-permute-done((f32[4,8,1280]{2,1,0:T(8,128)S(1)}, f32[4,8,1280]{2,1,0:T(8,128)S(1)}, u32[]{:S(2)}, u32[]{:S(2)}) %collective-permute-start.22) | collective-permute-done | bytes 163872 | tf_op jit(solution)/shard_map/ppermute | solution.py:36
  75.3 1.2 %assemble.1 = (f32[64,4096]{1,0:T(8,128)}, f32[64,1024]{1,0:T(8,128)}) custom-call(f32[4,8,4352]{2,1,0:T(8,128)S(1)} %get-tuple-element.48.own_rows, f32[4,8,4352]{2,1,0:T(8,128)S(1)} %collective-permute-done.19.other_rows, f32[4,8,1280]{2,1,0:T(8,128)S(1)} %collective-permute-done.20.refs_0_, f32[4,8,1280]{2,1,0:T(8,128)S(1)} %collective-permute-done.21.refs_1_, ...), custom_call_target="tpu_custom_call" | custom-call | flops 1 | bytes 1 | tf_op jit(solution)/shard_map/assemble/pallas_call | solution.py:253
  (40 shorter events, 11.8 us)
Async XLA Ops:
  2.8 4.2 %collective-permute-start = (f32[2,4,8,4096]{3,2,1,0:T(8,128)S(1)}, f32[2,4,8,4096]{3,2,1,0:T(8,128)S(1)}, u32[]{:S(2)}, u32[]{:S(2)}) collective-permute-start(f32[2,4,8,4096]{3,2,1,0:T(8,128)S(1)} %get-tuple-element.27), channel_id=1, source_target_pairs={{0,32},{1,33},{2,34},{3,35},{4,36},{5,37},{6,38},{7,39},{8,40},{9,... | collective-permute-start | bytes 3145736 | tf_op jit(solution)/shard_map/ppermute | solution.py:36
  6.5 8.8 %collective-permute-start.2 = (f32[2,4,8,4096]{3,2,1,0:T(8,128)S(1)}, f32[2,4,8,4096]{3,2,1,0:T(8,128)S(1)}, u32[]{:S(2)}, u32[]{:S(2)}) collective-permute-start(f32[2,4,8,4096]{3,2,1,0:T(8,128)S(1)} %get-tuple-element.33), channel_id=1, source_target_pairs={{0,32},{1,33},{2,34},{3,35},{4,36},{5,37},{6,38},{7,39},{8,40},{9,... | collective-permute-start | bytes 3145736 | tf_op jit(solution)/shard_map/ppermute | solution.py:36
  6.6 8.7 %collective-permute-start.1 = (f32[2,4,8,4096]{3,2,1,0:T(8,128)S(1)}, f32[2,4,8,4096]{3,2,1,0:T(8,128)S(1)}, u32[]{:S(2)}, u32[]{:S(2)}) collective-permute-start(f32[2,4,8,4096]{3,2,1,0:T(8,128)S(1)} %get-tuple-element.28.refs_2_), channel_id=1, source_target_pairs={{0,32},{1,33},{2,34},{3,35},{4,36},{5,37},{6,38},{7,39},{8,40},{9,... | collective-permute-start | bytes 3145736 | tf_op jit(solution)/shard_map/ppermute | solution.py:36
  7.2 11.1 %collective-permute-start.7 = (f32[2,2,8,4096]{3,2,1,0:T(8,128)S(1)}, f32[2,2,8,4096]{3,2,1,0:T(8,128)S(1)}, u32[]{:S(2)}, u32[]{:S(2)}) collective-permute-start(f32[2,2,8,4096]{3,2,1,0:T(8,128)S(1)} %get-tuple-element.41), channel_id=1, source_target_pairs={{0,1},{1,0},{2,3},{3,2},{4,5},{5,4},{6,7},{7,6},{8,9},{9,8},{10,11... | collective-permute-start | bytes 1572872 | tf_op jit(solution)/shard_map/ppermute | solution.py:36
  8.6 9.7 %collective-permute-start.6 = (f32[2,2,8,4096]{3,2,1,0:T(8,128)S(1)}, f32[2,2,8,4096]{3,2,1,0:T(8,128)S(1)}, u32[]{:S(2)}, u32[]{:S(2)}) collective-permute-start(f32[2,2,8,4096]{3,2,1,0:T(8,128)S(1)} %get-tuple-element.29.refs_3_), channel_id=1, source_target_pairs={{0,3},{1,2},{2,1},{3,0},{4,7},{5,6},{6,5},{7,4},{8,11},{9,10},{10,... | collective-permute-start | bytes 1572872 | tf_op jit(solution)/shard_map/ppermute | solution.py:36
  13.8 18.4 %collective-permute-start.5 = (f32[2,4,8,4096]{3,2,1,0:T(8,128)S(1)}, f32[2,4,8,4096]{3,2,1,0:T(8,128)S(1)}, u32[]{:S(2)}, u32[]{:S(2)}) collective-permute-start(f32[2,4,8,4096]{3,2,1,0:T(8,128)S(1)} %get-tuple-element.38), channel_id=1, source_target_pairs={{0,32},{1,33},{2,34},{3,35},{4,36},{5,37},{6,38},{7,39},{8,40},{9,... | collective-permute-start | bytes 3145736 | tf_op jit(solution)/shard_map/ppermute | solution.py:36
  15.5 9.7 %collective-permute-start.3 = (f32[2,2,8,4096]{3,2,1,0:T(8,128)S(1)}, f32[2,2,8,4096]{3,2,1,0:T(8,128)S(1)}, u32[]{:S(2)}, u32[]{:S(2)}) collective-permute-start(f32[2,2,8,4096]{3,2,1,0:T(8,128)S(1)} %get-tuple-element.34), channel_id=1, source_target_pairs={{0,3},{1,2},{2,1},{3,0},{4,7},{5,6},{6,5},{7,4},{8,11},{9,10},{10,... | collective-permute-start | bytes 1572872 | tf_op jit(solution)/shard_map/ppermute | solution.py:36
  18.3 8.3 %collective-permute-start.4 = (f32[2,2,8,4096]{3,2,1,0:T(8,128)S(1)}, f32[2,2,8,4096]{3,2,1,0:T(8,128)S(1)}, u32[]{:S(2)}, u32[]{:S(2)}) collective-permute-start(f32[2,2,8,4096]{3,2,1,0:T(8,128)S(1)} %get-tuple-element.35), channel_id=1, source_target_pairs={{0,1},{1,0},{2,3},{3,2},{4,5},{5,4},{6,7},{7,6},{8,9},{9,8},{10,11... | collective-permute-start | bytes 1572872 | tf_op jit(solution)/shard_map/ppermute | solution.py:36
  18.4 13.8 %collective-permute-start.8 = (f32[2,2,8,4096]{3,2,1,0:T(8,128)S(1)}, f32[2,2,8,4096]{3,2,1,0:T(8,128)S(1)}, u32[]{:S(2)}, u32[]{:S(2)}) collective-permute-start(f32[2,2,8,4096]{3,2,1,0:T(8,128)S(1)} %get-tuple-element.42), channel_id=1, source_target_pairs={{0,1},{1,0},{2,3},{3,2},{4,5},{5,4},{6,7},{7,6},{8,9},{9,8},{10,11... | collective-permute-start | bytes 1572872 | tf_op jit(solution)/shard_map/ppermute | solution.py:36
  20.0 12.3 %collective-permute-start.9 = (f32[2,2,8,4096]{3,2,1,0:T(8,128)S(1)}, f32[2,2,8,4096]{3,2,1,0:T(8,128)S(1)}, u32[]{:S(2)}, u32[]{:S(2)}) collective-permute-start(f32[2,2,8,4096]{3,2,1,0:T(8,128)S(1)} %get-tuple-element.43), channel_id=1, source_target_pairs={{0,3},{1,2},{2,1},{3,0},{4,7},{5,6},{6,5},{7,4},{8,11},{9,10},{10,... | collective-permute-start | bytes 1572872 | tf_op jit(solution)/shard_map/ppermute | solution.py:36
  32.4 7.1 %collective-permute-start.10 = (f32[2,4,8,1024]{3,2,1,0:T(8,128)S(1)}, f32[2,4,8,1024]{3,2,1,0:T(8,128)S(1)}, u32[]{:S(2)}, u32[]{:S(2)}) collective-permute-start(f32[2,4,8,1024]{3,2,1,0:T(8,128)S(1)} %get-tuple-element.45), channel_id=1, source_target_pairs={{0,16},{1,17},{2,18},{3,19},{4,20},{5,21},{6,22},{7,23},{8,24},{9,... | collective-permute-start | bytes 786440 | tf_op jit(solution)/shard_map/ppermute | solution.py:36
  35.3 7.1 %collective-permute-start.11 = (f32[2,4,8,1024]{3,2,1,0:T(8,128)S(1)}, f32[2,4,8,1024]{3,2,1,0:T(8,128)S(1)}, u32[]{:S(2)}, u32[]{:S(2)}) collective-permute-start(f32[2,4,8,1024]{3,2,1,0:T(8,128)S(1)} %get-tuple-element.46), channel_id=1, source_target_pairs={{0,24},{1,25},{2,26},{3,27},{4,28},{5,29},{6,30},{7,31},{8,16},{9,... | collective-permute-start | bytes 786440 | tf_op jit(solution)/shard_map/ppermute | solution.py:36
  36.1 6.4 %collective-permute-start.12 = (f32[2,4,8,1024]{3,2,1,0:T(8,128)S(1)}, f32[2,4,8,1024]{3,2,1,0:T(8,128)S(1)}, u32[]{:S(2)}, u32[]{:S(2)}) collective-permute-start(f32[2,4,8,1024]{3,2,1,0:T(8,128)S(1)} %get-tuple-element.47), channel_id=1, source_target_pairs={{0,8},{1,9},{2,10},{3,11},{4,12},{5,13},{6,14},{7,15},{8,0},{9,1},... | collective-permute-start | bytes 786440 | tf_op jit(solution)/shard_map/ppermute | solution.py:36
  42.5 9.6 %collective-permute-start.15 = (f32[2,4,8,1024]{3,2,1,0:T(8,128)S(1)}, f32[2,4,8,1024]{3,2,1,0:T(8,128)S(1)}, u32[]{:S(2)}, u32[]{:S(2)}) collective-permute-start(f32[2,4,8,1024]{3,2,1,0:T(8,128)S(1)} %second_axis_sum.1.a), channel_id=1, source_target_pairs={{0,68},{1,69},{2,70},{3,71},{4,64},{5,65},{6,66},{7,67},{8,76},{9,... | collective-permute-start | bytes 786440 | tf_op jit(solution)/shard_map/ppermute | solution.py:36
  43.5 8.6 %collective-permute-start.14 = (f32[2,4,8,1024]{3,2,1,0:T(8,128)S(1)}, f32[2,4,8,1024]{3,2,1,0:T(8,128)S(1)}, u32[]{:S(2)}, u32[]{:S(2)}) collective-permute-start(f32[2,4,8,1024]{3,2,1,0:T(8,128)S(1)} %second_axis_sum.1.a), channel_id=1, source_target_pairs={{0,64},{1,65},{2,66},{3,67},{4,68},{5,69},{6,70},{7,71},{8,72},{9,... | collective-permute-start | bytes 786440 | tf_op jit(solution)/shard_map/ppermute | solution.py:36
  45.1 7.7 %collective-permute-start.13 = (f32[2,4,8,1024]{3,2,1,0:T(8,128)S(1)}, f32[2,4,8,1024]{3,2,1,0:T(8,128)S(1)}, u32[]{:S(2)}, u32[]{:S(2)}) collective-permute-start(f32[2,4,8,1024]{3,2,1,0:T(8,128)S(1)} %second_axis_sum.1.a), channel_id=1, source_target_pairs={{0,4},{1,5},{2,6},{3,7},{4,0},{5,1},{6,2},{7,3},{8,12},{9,13},{10,... | collective-permute-start | bytes 786440 | tf_op jit(solution)/shard_map/ppermute | solution.py:36
  53.2 5.9 %collective-permute-start.18 = (f32[8,4352]{1,0:T(8,128)S(1)}, f32[8,4352]{1,0:T(8,128)S(1)}, u32[]{:S(2)}, u32[]{:S(2)}) collective-permute-start(f32[8,4352]{1,0:T(8,128)S(1)} %mean_and_preview.1.a), channel_id=1, source_target_pairs={{0,24},{1,25},{2,26},{3,27},{4,28},{5,29},{6,30},{7,31},{8,16},{9,... | collective-permute-start | bytes 417800 | tf_op jit(solution)/shard_map/ppermute | solution.py:36
  55.7 5.4 %collective-permute-start.17 = (f32[8,4352]{1,0:T(8,128)S(1)}, f32[8,4352]{1,0:T(8,128)S(1)}, u32[]{:S(2)}, u32[]{:S(2)}) collective-permute-start(f32[8,4352]{1,0:T(8,128)S(1)} %mean_and_preview.1.a), channel_id=1, source_target_pairs={{0,16},{1,17},{2,18},{3,19},{4,20},{5,21},{6,22},{7,23},{8,24},{9,... | collective-permute-start | bytes 417800 | tf_op jit(solution)/shard_map/ppermute | solution.py:36
  56.2 4.8 %collective-permute-start.16 = (f32[8,4352]{1,0:T(8,128)S(1)}, f32[8,4352]{1,0:T(8,128)S(1)}, u32[]{:S(2)}, u32[]{:S(2)}) collective-permute-start(f32[8,4352]{1,0:T(8,128)S(1)} %mean_and_preview.1.a), channel_id=1, source_target_pairs={{0,8},{1,9},{2,10},{3,11},{4,12},{5,13},{6,14},{7,15},{8,0},{9,1},... | collective-permute-start | bytes 417800 | tf_op jit(solution)/shard_map/ppermute | solution.py:36
  61.1 14.2 %collective-permute-start.19 = (f32[4,8,4352]{2,1,0:T(8,128)S(1)}, f32[4,8,4352]{2,1,0:T(8,128)S(1)}, u32[]{:S(2)}, u32[]{:S(2)}) collective-permute-start(f32[4,8,4352]{2,1,0:T(8,128)S(1)} %get-tuple-element.48.own_rows), channel_id=1, source_target_pairs={{0,32},{1,33},{2,34},{3,35},{4,36},{5,37},{6,38},{7,39},{8,40},{9,... | collective-permute-start | bytes 1671176 | tf_op jit(solution)/shard_map/ppermute | solution.py:36
  65.3 6.0 %collective-permute-start.22 = (f32[4,8,1280]{2,1,0:T(8,128)S(1)}, f32[4,8,1280]{2,1,0:T(8,128)S(1)}, u32[]{:S(2)}, u32[]{:S(2)}) collective-permute-start(f32[4,8,1280]{2,1,0:T(8,128)S(1)} %get-tuple-element.49), channel_id=1, source_target_pairs={{0,2},{1,3},{2,0},{3,1},{4,6},{5,7},{6,4},{7,5},{8,10},{9,11},{10,... | collective-permute-start | bytes 491528 | tf_op jit(solution)/shard_map/ppermute | solution.py:36
  66.3 6.7 %collective-permute-start.21 = (f32[4,8,1280]{2,1,0:T(8,128)S(1)}, f32[4,8,1280]{2,1,0:T(8,128)S(1)}, u32[]{:S(2)}, u32[]{:S(2)}) collective-permute-start(f32[4,8,1280]{2,1,0:T(8,128)S(1)} %get-tuple-element.49), channel_id=1, source_target_pairs={{0,3},{1,2},{2,1},{3,0},{4,7},{5,6},{6,5},{7,4},{8,11},{9,10},{10,... | collective-permute-start | bytes 491528 | tf_op jit(solution)/shard_map/ppermute | solution.py:36
  67.9 6.0 %collective-permute-start.20 = (f32[4,8,1280]{2,1,0:T(8,128)S(1)}, f32[4,8,1280]{2,1,0:T(8,128)S(1)}, u32[]{:S(2)}, u32[]{:S(2)}) collective-permute-start(f32[4,8,1280]{2,1,0:T(8,128)S(1)} %get-tuple-element.49), channel_id=1, source_target_pairs={{0,1},{1,0},{2,3},{3,2},{4,5},{5,4},{6,7},{7,6},{8,9},{9,8},{10,11... | collective-permute-start | bytes 491528 | tf_op jit(solution)/shard_map/ppermute | solution.py:36
  71.2 2.7 %collective-permute-start.25 = (f32[4,8,1280]{2,1,0:T(8,128)S(1)}, f32[4,8,1280]{2,1,0:T(8,128)S(1)}, u32[]{:S(2)}, u32[]{:S(2)}) collective-permute-start(f32[4,8,1280]{2,1,0:T(8,128)S(1)} %collective-permute-done.22.refs_2_), channel_id=1, source_target_pairs={{0,32},{1,33},{2,34},{3,35},{4,36},{5,37},{6,38},{7,39},{8,40},{9,... | collective-permute-start | bytes 491528 | tf_op jit(solution)/shard_map/ppermute | solution.py:36
  (2 other events, 3.4 us)
